TPU v7x, 256 devices: a whole 4x4x8 slice. The times are simulated.
256 devices in a mesh: ctx: 32 (over y_lo, z, core), head: 8 (over x, y_hi).
Axes of the slice: x: 4, y: 4 (y_hi: 2, y_lo: 2; y = y_hi * 2 + y_lo), z: 8, core: 2. Of those that a mesh axis runs over, the one named last changes fastest.
Arguments:
- main_q_nope: bfloat16 [512, 16384], P(None, 'head'), may hold values from -130 to 130
- main_q_rope: bfloat16 [512, 8192], P(None, 'head'), may hold values from -6 to 6
- main_k_nope: bfloat16 [32768, 16384], P('ctx', 'head'), may hold values from -9 to 9
- main_k_rope: bfloat16 [32768, 64], P('ctx'), may hold values from -6 to 6
- index_q: bfloat16 [512, 8192], P('head'), may hold values from -90 to 90
- index_k: bfloat16 [32768, 128], P('ctx'), may hold values from -8 to 8
- index_w: float32 [512, 64], P('head'), may hold values from -3 to 3
- query_pos: int32 [512], replicated, may hold values from 0 to 32767
- key_blocks: int32 [32], P('ctx'), may hold values from 0 to 31, each once
Outputs:
- grad_index_q: float32 [512, 8192], P('head', 'ctx')
- grad_index_k: float32 [32768, 128], P(('ctx', 'head'))
- grad_index_w: float32 [512, 64], P('head')
All inputs are finite; a program needn't handle non-finite values.
Results may differ from a plain program's by a relative error of at most 0.015.
Values sent between devices are 32-bit elements; how exact they have to be, the bound alone decides.
No kernel may reach another device: no remote copies, remote signals or barrier semaphores. Data moves between devices by JAX's collectives and lax.ppermute only.
A program may use at most 128 MiB of HBM per device.

v0:
```python
import math

import jax
import jax.numpy as jnp
from jax import lax
from jax.sharding import PartitionSpec as P

HEADS = 128
NOPE = 128
ROPE = 64
IDX_HEADS = 64
IDX_DIM = 128


negative_fill = -1e30


def combined_all(value, axis, join):
    pieces = jax.tree.map(lambda part: lax.all_gather(part, axis), value)
    head = jax.tree.map(lambda part: part[0], pieces)
    tail = jax.tree.map(lambda part: part[1:], pieces)
    subtotal, _ = lax.scan(lambda subtotal, piece: (join(subtotal, piece), None), head, tail)
    return subtotal


def merged_pair(top_first, total_first, top_second, total_second):
    joint_top = jnp.maximum(top_first, top_second)
    joint_total = total_first * jnp.exp(top_first - joint_top) + total_second * jnp.exp(
        top_second - joint_top
    )
    return (joint_top, joint_total)


def pair_merge(earlier, later):
    return merged_pair(earlier[0], earlier[1], later[0], later[1])


def local_stats(values, visible):
    row_top = jnp.max(values, axis=-1)
    row_total = jnp.sum(jnp.where(visible, jnp.exp(values - row_top[..., None]), 0.0), axis=-1)
    return (row_top, row_total)


def per_device(
    main_q_nope,
    main_q_rope,
    main_k_nope,
    main_k_rope,
    index_q,
    index_k,
    index_w,
    query_pos,
    key_blocks,
):
    key_count = index_k.shape[0]
    row_count = index_q.shape[0]
    query_count = main_q_nope.shape[0]
    head_count = main_q_nope.shape[1] // NOPE
    key_pos = key_blocks[0] * key_count + jnp.arange(key_count, dtype=jnp.int32)
    visible = key_pos[None, :] <= query_pos[:, None]
    row_start = lax.axis_index("head") * row_count
    visible_rows = lax.dynamic_slice_in_dim(visible, row_start, row_count, 0)
    score_scale = 1.0 / math.sqrt(NOPE + ROPE)
    query_nope = main_q_nope.reshape(query_count, head_count, NOPE)
    query_rope = main_q_rope.reshape(query_count, head_count, ROPE)
    key_nope = main_k_nope.reshape(key_count, head_count, NOPE)
    scores = jnp.einsum("qhd,khd->hqk", query_nope, key_nope, preferred_element_type=jnp.float32)
    scores = scores + jnp.einsum(
        "qhr,kr->hqk", query_rope, main_k_rope, preferred_element_type=jnp.float32
    )
    scores = jnp.where(visible[None], scores * score_scale, negative_fill)
    main_top, main_total = local_stats(scores, visible[None])
    inv_root = 1.0 / math.sqrt(IDX_DIM)
    q_heads = index_q.reshape(row_count, IDX_HEADS, IDX_DIM)
    main_top, main_total = combined_all((main_top, main_total), "ctx", pair_merge)
    main_lse = main_top + jnp.log(main_total)
    head_probs = jnp.sum(
        jnp.where(visible[None], jnp.exp(scores - main_lse[..., None]), 0.0), axis=0
    )
    summed_all = lax.psum(head_probs, "head")
    summed_rows = lax.dynamic_slice_in_dim(summed_all, row_start, row_count, 0)
    target = summed_rows / HEADS
    inner = (
        jnp.einsum("rjd,kd->rjk", q_heads, index_k, preferred_element_type=jnp.float32) * inv_root
    )
    active = jnp.maximum(inner, 0.0)
    logits = jnp.sum(index_w[:, :, None] * active, axis=1)
    logits = jnp.where(visible_rows, logits, negative_fill)
    index_top, index_total = local_stats(logits, visible_rows)
    inner, active, logits, index_top, index_total = (inner, active, logits, index_top, index_total)
    index_top, index_total = combined_all((index_top, index_total), "ctx", pair_merge)
    index_lse = index_top + jnp.log(index_total)
    logit_grad = jnp.where(visible_rows, jnp.exp(logits - index_lse[:, None]) - target, 0.0)
    weighted = jnp.where(inner > 0, logit_grad[:, None, :] * index_w[:, :, None], 0.0).astype(
        jnp.bfloat16
    )
    query_part = jnp.einsum("rjk,kd->rjd", weighted, index_k, preferred_element_type=jnp.float32)
    query_part = query_part.reshape(row_count, IDX_HEADS * IDX_DIM) * inv_root
    grad_index_q = lax.psum_scatter(query_part, "ctx", scatter_dimension=1, tiled=True)
    key_part = (
        jnp.einsum("rjk,rjd->kd", weighted, q_heads, preferred_element_type=jnp.float32) * inv_root
    )
    grad_index_k = lax.psum_scatter(key_part, "head", scatter_dimension=0, tiled=True)
    weight_part = jnp.sum(logit_grad[:, None, :] * active, axis=2)
    grad_index_w = lax.psum(weight_part, "ctx")
    return (grad_index_q, grad_index_k, grad_index_w)


def solution(mesh):
    return jax.shard_map(
        per_device,
        mesh=mesh,
        in_specs=(
            P(None, "head"),
            P(None, "head"),
            P("ctx", "head"),
            P("ctx", None),
            P("head", None),
            P("ctx", None),
            P("head", None),
            P(),
            P("ctx"),
        ),
        out_specs=(P("head", "ctx"), P(("ctx", "head"), None), P("head", None)),
        check_vma=False,
    )
```

profile of v0, /device:TPU:2, one launch (start us, length us, event | category | flops | bytes accessed | tf_op | source)
XLA Modules:
  0.0 570.9 jit_solution(10825419716385870085)
XLA Ops:
  8.0 2.3 copy.20
  10.3 1.0 broadcast_compare_fusion
  11.4 17.0 %fusion.18 = f32[1024,512,16]{0,1,2:T(8,128)} fusion(bf16[512,16,64]{0,2,1:T(8,128)(2,1)} %bitcast.82, bf16[1024,64]{0,1:T(8,128)(2,1)} %param.16), kind=kOutput, calls=%fused_computation.36 | convolution fusion | flops 1073741824 | bytes 34734080 | tf_op jit(solution)/shard_map/qhr,kr->hqk/dot_general | solution.py:68
  28.4 22.4 %fusion.25 = (f32[16,512]{1,0:T(8,128)S(1)}, f32[16,512,1024]{2,1,0:T(8,128)}) fusion(f32[1024,512,16]{0,1,2:T(8,128)} %fusion.18, pred[512,1024]{1,0:T(8,128)(4,1)S(1)} %broadcast_compare_fusion, bf16[1024,2048]{1,0:T(8,128)(2,1)S(1)} %copy-done.2, bf16[512,2048]{1,0:T(8,128)(2,1)S(1)} %copy-done), kind=kOutput, calls=%fused_computation.45 | convolution fusion | flops 2181029888 | bytes 73957376 | tf_op jit(solution)/shard_map/qhd,khd->hqk/dot_general | solution.py:67
  50.8 15.5 %select_reduce_fusion.1 = f32[16,512]{1,0:T(8,128)} fusion(f32[16,512,1024]{2,1,0:T(8,128)} %get-tuple-element.90, f32[16,512]{1,0:T(8,128)S(1)} %get-tuple-element.89, pred[512,1024]{1,0:T(8,128)(4,1)S(1)} %broadcast_compare_fusion), kind=kLoop, calls=%fused_computation.16 | loop fusion | flops 25157632 | bytes 34144256 | tf_op jit(solution)/shard_map/reduce_sum | solution.py:40
  67.1 1.5 copy.29
  70.0 7.2 %multiply_reduce_fusion.1 = (f32[64,1024]{1,0:T(8,128)S(1)}, f32[64,64,1024]{2,1,0:T(8,128)}) fusion(f32[64,64]{1,0:T(8,128)S(1)} %copy-done.5, bf16[64,64,128]{2,1,0:T(8,128)(2,1)S(1)} %bitcast.83, bf16[1024,128]{1,0:T(8,128)(2,1)S(1)} %copy-done.4), kind=kOutput, calls=%fused_computation.19 | convolution fusion | flops 1090453504 | bytes 18366464 | tf_op jit(solution)/shard_map/rjd,kd->rjk/dot_general | solution.py:84
  78.1 110.9 %all-reduce.2 = (f32[2048]{0:T(1024)S(1)}, f32[2048]{0:T(1024)S(1)}) all-reduce(f32[2048]{0:T(1024)S(1)} %dynamic-update-slice, f32[2048]{0:T(1024)S(1)} %dynamic-update-slice.1), channel_id=2, replica_groups=mesh['ctx'=32,'head'=8] {'ctx'}, use_global_device_ids=true, to_apply=%add | all-reduce | flops 4096 | bytes 32768
  189.3 2.3 slice.47
  192.3 6.4 %all-gather.7.cloned.1.call-done = f32[512,512]{1,0:T(8,128)} async-done(((f32[16,512]{1,0:T(8,128)}), f32[512,512]{1,0:T(8,128)}) %all-gather.7.cloned.1.call-update) | async-done | bytes 1048592 | tf_op jit(solution)/shard_map/all_gather | solution.py:19
  198.8 2.3 slice.46
  201.8 25.8 %while.25 = (s32[]{:T(128)}, f32[16,512]{1,0:T(8,128)S(1)}, f32[16,512]{1,0:T(8,128)S(1)}, f32[31,16,512]{2,1,0:T(8,128)}, f32[31,16,512]{2,1,0:T(8,128)}, /*index=5*/s32[]{:T(128)}) while((s32[]{:T(128)}, f32[16,512]{1,0:T(8,128)S(1)}, f32[16,512]{1,0:T(8,128)S(1)}, f32[31,16,512]{2,1,0:T(8,128)}, f32[31,16,512]{2,1,0:T(8,128)}, ...), condition=%wide.region_8.9_spmd, body=%wide.region_7.8_spmd.sunk | while | flops 49154 | bytes 196681 | solution.py:22
  202.6 0.8 fusion.34
  203.5 0.8 fusion.34
  204.3 0.8 fusion.34
  205.1 0.8 fusion.34
  206.0 0.8 fusion.34
  206.8 0.8 fusion.34
  207.6 0.8 fusion.34
  208.5 0.8 fusion.34
  209.3 0.8 fusion.34
  210.1 0.8 fusion.34
  211.0 0.8 fusion.34
  211.8 0.8 fusion.34
  212.6 0.8 fusion.34
  213.5 0.8 fusion.34
  214.3 0.8 fusion.34
  215.1 0.8 fusion.34
  216.0 0.8 fusion.34
  216.8 0.8 fusion.34
  217.6 0.8 fusion.34
  218.5 0.8 fusion.34
  219.3 0.8 fusion.34
  220.1 0.8 fusion.34
  221.0 0.8 fusion.34
  223.5 0.8 fusion.34
  225.1 0.8 fusion.34
  226.8 0.8 fusion.34
  227.6 15.5 %select_reduce_fusion = f32[512,1024]{1,0:T(8,128)} fusion(f32[16,512,1024]{2,1,0:T(8,128)} %get-tuple-element.90, f32[16,512]{1,0:T(8,128)S(1)} %log_add_fusion, pred[512,1024]{1,0:T(8,128)(4,1)S(1)} %broadcast_compare_fusion), kind=kLoop, calls=%fused_computation.15 | loop fusion | flops 24641536 | bytes 36208640 | tf_op jit(solution)/shard_map/reduce_sum | solution.py:77
  243.2 1.2 while.24
  244.4 113.6 %all-reduce.5.cloned.1.call-done = f32[512,1024]{1,0:T(8,128)} async-done(((f32[512,1024]{1,0:T(8,128)}), f32[512,1024]{1,0:T(8,128)}) %all-reduce.5.cloned.1.call-update) | async-done | bytes 2097168 | tf_op jit(solution)/shard_map/psum | solution.py:80
  358.0 1.1 subtract_select_fusion
  359.1 8.5 %fusion.13 = f32[1024,128]{1,0:T(8,128)} fusion(bf16[64,64,128]{2,1,0:T(8,128)(2,1)S(1)} %bitcast.84, f32[64,64,1024]{2,1,0:T(8,128)} %get-tuple-element.92, f32[64,1024]{1,0:T(8,128)S(1)} %subtract_select_fusion, f32[64,64]{1,0:T(8,128)S(1)} %copy-done.5), kind=kOutput, calls=%fused_computation.27 | convolution fusion | flops 1094844416 | bytes 18628608 | tf_op jit(solution)/shard_map/rjk,rjd->kd/dot_general | solution.py:101
  367.7 7.3 %convolution_multiply_fusion = f32[64,64,128]{2,1,0:T(8,128)S(1)} fusion(bf16[1024,128]{1,0:T(8,128)(2,1)S(1)} %copy-done.4, f32[64,64,1024]{2,1,0:T(8,128)} %get-tuple-element.92, f32[64,1024]{1,0:T(8,128)S(1)} %subtract_select_fusion, f32[64,64]{1,0:T(8,128)S(1)} %copy-done.5), kind=kOutput, calls=%fused_computation.25 | convolution fusion | flops 1095237632 | bytes 19415040 | tf_op jit(solution)/shard_map/rjk,kd->rjd/dot_general | solution.py:97
  375.0 2.5 copy.44
  377.6 8.1 %multiply_reduce_fusion = f32[64,64]{1,0:T(8,128)S(1)} fusion(f32[64,64,1024]{2,1,0:T(8,128)} %get-tuple-element.92, f32[64,1024]{1,0:T(8,128)S(1)} %subtract_select_fusion), kind=kLoop, calls=%fused_computation.17 | loop fusion | flops 16773120 | bytes 17055744 | tf_op jit(solution)/shard_map/reduce_sum | solution.py:104
  385.6 105.3 %psum.15 = f32[64,64]{1,0:T(8,128)} all-reduce(f32[64,64]{1,0:T(8,128)S(1)} %multiply_reduce_fusion), channel_id=1, replica_groups=mesh['ctx'=32,'head'=8] {'ctx'}, use_global_device_ids=true, to_apply=%region_14.15 | all-reduce | flops 4096 | bytes 32768 | tf_op jit(solution)/shard_map/psum | solution.py:105
  490.9 73.5 %reduce-scatter.3.cloned.1.call-done = f32[64,256]{1,0:T(8,128)} async-done(((f32[64,8192]{1,0:T(8,128)}), f32[64,256]{1,0:T(8,128)}) %reduce-scatter.3.cloned.1.call-update) | async-done | bytes 65552 | tf_op jit(solution)/shard_map/reduce_scatter | solution.py:99
  (80 shorter events, 9.3 us)
Async XLA Ops:
  7.2 21.3 %copy-start = (bf16[512,2048]{1,0:T(8,128)(2,1)S(1)}, bf16[512,2048]{1,0:T(8,128)(2,1)}, u32[]{:S(2)}) copy-start(bf16[512,2048]{1,0:T(8,128)(2,1)} %param.13) | copy-start | bytes 6291460
  7.2 182.2 %all-gather.9.cloned.1.call-start = ((), (), s32[]{:S(2)}) async-start(), calls=%async_computation.6 | async-start | bytes 1081344 | tf_op jit(solution)/shard_map/all_gather | solution.py:19
  11.4 17.1 %copy-start.2 = (bf16[1024,2048]{1,0:T(8,128)(2,1)S(1)}, bf16[1024,2048]{1,0:T(8,128)(2,1)}, u32[]{:S(2)}) copy-start(bf16[1024,2048]{1,0:T(8,128)(2,1)} %param.15) | copy-start | bytes 12582916
  50.8 15.5 %copy-start.3 = (f32[16,512]{1,0:T(8,128)}, f32[16,512]{1,0:T(8,128)S(1)}, u32[]{:S(2)}) copy-start(f32[16,512]{1,0:T(8,128)S(1)} %get-tuple-element.89) | copy-start | bytes 98308
  50.8 17.8 %copy-start.6 = (u32[256]{0:T(256)S(1)}, u32[256]{0:T(256)}, u32[]{:S(2)}) copy-start(u32[256]{0:T(256)} %constant.48) | copy-start | bytes 3076
  50.8 19.2 %copy-start.4 = (bf16[1024,128]{1,0:T(8,128)(2,1)S(1)}, bf16[1024,128]{1,0:T(8,128)(2,1)}, u32[]{:S(2)}) copy-start(bf16[1024,128]{1,0:T(8,128)(2,1)} %param.18) | copy-start | bytes 786436
  50.8 19.2 %copy-start.5 = (f32[64,64]{1,0:T(8,128)S(1)}, f32[64,64]{1,0:T(8,128)}, u32[]{:S(2)}) copy-start(f32[64,64]{1,0:T(8,128)} %param.19) | copy-start | bytes 49156
  66.3 132.5 %all-gather.7.cloned.1.call-start = ((), (), s32[]{:S(2)}) async-start(), calls=%async_computation.5 | async-start | bytes 1081344 | tf_op jit(solution)/shard_map/all_gather | solution.py:19
  67.0 291.0 %all-reduce.5.cloned.1.call-start = ((), (), s32[]{:S(2)}) async-start(), calls=%async_computation.2 | async-start | bytes 4194304 | tf_op jit(solution)/shard_map/psum | solution.py:80
  243.1 247.8 %reduce-scatter.5.cloned.1.call-start = ((), (), s32[]{:S(2)}) async-start(), calls=%async_computation.4 | async-start | bytes 589824 | tf_op jit(solution)/shard_map/reduce_scatter | solution.py:103
  367.6 196.8 %reduce-scatter.3.cloned.1.call-start = ((), (), s32[]{:S(2)}) async-start(), calls=%async_computation.3 | async-start | bytes 2162688 | tf_op jit(solution)/shard_map/reduce_scatter | solution.py:99
  367.7 196.8 %copy-start.1 = (bf16[512,2048]{1,0:T(8,128)(2,1)S(1)}, bf16[512,2048]{1,0:T(8,128)(2,1)}, u32[]{:S(2)}) copy-start(bf16[512,2048]{1,0:T(8,128)(2,1)} %param.13) | copy-start | bytes 6291460
Sparse Core Ops, SparseCore 0:
  66.4 66.5 all-gather.8
  135.4 63.3 all-gather.6
  243.3 114.7 all-reduce.4
  367.7 75.5 reduce-scatter.4
  446.4 117.9 reduce-scatter.2
where the time goes:
time: 574 us; the launch traced here: 571 us
  blocking collectives  216 us (38%)
  waiting for transfers between devices  194 us (34%)
  other arithmetic  67.7 us (12%)
  matrix products  62.4 us (11%)
  between operations  15.4 us (3%)
  local copies, waits for them, and re-layouts  13.9 us (2%)
    psum x1, waiting for transfers between devices, per_device(): summed_all = lax.psum(head_probs, 'head')  114 us
    unnamed x1, blocking collectives  111 us
    psum x1, blocking collectives, per_device(): grad_index_w = lax.psum(weight_part, 'ctx')  105 us
    reduce_scatter x1, waiting for transfers between devices, per_device(): lax.psum_scatter(query_part, 'ctx', scatter_dimension=1, tiled=True)  73.5 us
    add x62, other arithmetic, merged_pair(): total_first * jnp.exp(top_first - joint_top)  26.2 us
    dot_general x1, matrix products, per_device(): jnp.einsum('qhd,khd->hqk', query_nope, key_nope, preferred_element_type=j...  22.4 us
    dot_general x1, matrix products, per_device(): jnp.einsum('qhr,kr->hqk', query_rope, main_k_rope, preferred_element_type...  17 us
    reduce_sum x2, other arithmetic, local_stats(): jnp.sum(jnp.where(visible, jnp.exp(values - row_top[..., None]), 0.0), ax...  15.7 us
  transfers between devices with their start and end apart: 5, of which 3 were waited for; matrix products, arithmetic and copies ran while one was open for 6% of the time, Pallas kernels for 0%

commit v1 on v0

v1 whole, which is shorter than its diff:
```python
import math

import jax
import jax.numpy as jnp
from jax import lax
from jax.experimental import pallas as pl
from jax.experimental.pallas import tpu as pltpu
from jax.sharding import PartitionSpec as P

HEADS = 128
NOPE = 128
ROPE = 64
IDX_HEADS = 64
IDX_DIM = 128
N_CTX = 32
N_HEAD = 8
N_Z = 8
LOG2E = math.log2(math.e)
SCORE_SCALE = LOG2E / math.sqrt(NOPE + ROPE)
INV_ROOT = 1.0 / math.sqrt(IDX_DIM)
NEG = -1e30
F32 = jnp.float32
BF16 = jnp.bfloat16
NT = (((1,), (1,)), ((), ()))
NN = (((1,), (0,)), ((), ()))
GROUP = 8


def dot(a, b, dims):
    return lax.dot_general(a, b, dims, preferred_element_type=F32)


def column(row, lanes=128):
    return jnp.broadcast_to(row, (lanes, row.shape[1])).T


def ctx_place():
    ctx = lax.axis_index("ctx")
    return ctx // (2 * N_Z), ctx // 2 % N_Z, ctx % 2


def fill_rope(krt_ref, krp):
    kr = krt_ref[...].T
    zero = jnp.zeros_like(kr)
    krp[0] = jnp.concatenate([kr, zero], axis=1)
    krp[1] = jnp.concatenate([zero, kr], axis=1)


def fill_weights(w_ref, wb):
    for j in range(IDX_HEADS):
        wb[j] = jnp.broadcast_to(w_ref[:, j : j + 1], wb.shape[1:])


def lanes_of(block, width):
    return jnp.concatenate([block] * (width // 128), axis=-1)


def stacked(block):
    count = block.shape[1] // 128
    return jnp.concatenate([block[:, i * 128 : (i + 1) * 128] for i in range(count)], axis=0)


def index_kernel(
    base_ref, qpos_ref, iq_first, iq_odd, iq_next, ik_ref, w_ref, logits_ref, row_ref, r_ref,
    wb, qcol, even, odd,
):
    step = pl.program_id(0)
    rows, keys = logits_ref.shape

    @pl.when(step == 0)
    def _():
        even[...] = dot(stacked(iq_first[...]), ik_ref[...], NT)
        fill_weights(w_ref, wb)
        logits_ref[...] = jnp.zeros_like(logits_ref)
        qcol[...] = column(qpos_ref[...])

    for n, (source, done, made) in enumerate(((iq_odd, even, odd), (iq_next, odd, even))):
        q = stacked(source[...])
        for half in range(2):
            wide = slice(half * 512, (half + 1) * 512)
            made[:, wide] = dot(q, ik_ref[wide, :], NT)
            for kc in range(4 * half, 4 * half + 4):
                cols = slice(kc * 128, (kc + 1) * 128)
                total = logits_ref[:, cols]
                for i in range(GROUP):
                    mine = slice(i * rows, (i + 1) * rows)
                    inner = done[mine, cols]
                    r_ref[n, mine, cols] = inner.astype(BF16)
                    total = total + jnp.maximum(inner, 0.0) * wb[(2 * step + n) * GROUP + i]
                logits_ref[:, cols] = total

    @pl.when(step == pl.num_programs(0) - 1)
    def _():
        key = lax.broadcasted_iota(jnp.int32, (rows, keys), 1) + base_ref[0] * keys
        start = pl.multiple_of(lax.axis_index("head") * rows, rows)
        limit = lanes_of(qcol[pl.ds(start, rows), :], keys)
        logits = jnp.where(key <= limit, logits_ref[...] * (INV_ROOT * LOG2E), NEG)
        logits_ref[...] = logits
        top = jnp.max(logits, axis=1, keepdims=True)
        total = jnp.sum(jnp.exp2(logits - top), axis=1, keepdims=True)
        lse = jnp.broadcast_to(top + jnp.log2(total), (rows, 128)).T
        row_ref[...] = jnp.concatenate([lse[:16, :rows], jnp.zeros((16, 128 - rows), F32)], axis=1)


def pair_operands(refs, krp, p):
    qn_ref, qr_ref, kn_ref = refs
    part = slice(p * 128, (p + 1) * 128)
    q = jnp.concatenate([qn_ref[:, part], qr_ref[...]], axis=1)
    return q, jnp.concatenate([kn_ref[:, part], krp[p]], axis=1)


def online_lse(s_ref, bias, cols, chunk=64):
    keys = bias.shape[0]
    top = jnp.full((8, 256), 2.0 * NEG, F32)
    total = jnp.zeros((8, 256), F32)
    for kc in range(keys // chunk):
        rows = slice(kc * chunk, (kc + 1) * chunk)
        s = (s_ref[rows, cols] + bias[rows, cols]).reshape(chunk // 8, 8, 256)
        new = jnp.maximum(top, jnp.max(s, axis=0))
        e = jnp.exp2((s - new[None]) * SCORE_SCALE)
        total = total * jnp.exp2((top - new) * SCORE_SCALE) + jnp.sum(e, axis=0)
        top = new
    best = jnp.max(top, axis=0, keepdims=True)
    total = jnp.sum(total * jnp.exp2((top - best) * SCORE_SCALE), axis=0, keepdims=True)
    return best * SCORE_SCALE + jnp.log2(total)


def stats_kernel(base_ref, qpos_ref, row_ref, krt_ref, *refs):
    first, odd_in, next_in = refs[:3], refs[3:6], refs[6:9]
    out_ref, bias, krp, even, odd = refs[9:]
    step = pl.program_id(0)
    keys, queries = bias.shape

    @pl.when(step == 0)
    def _():
        fill_rope(krt_ref, krp)
        for p in range(2):
            q, k = pair_operands(first, krp, p)
            even[p] = dot(k, q, NT)
        key = lax.broadcasted_iota(jnp.int32, bias.shape, 0) + base_ref[0] * keys
        bias[...] = jnp.where(key <= qpos_ref[...], 0.0, NEG)
        out_ref[:, queries:] = row_ref[...]

    for n, (source, done, made) in enumerate(((odd_in, even, odd), (next_in, odd, even))):
        for p in range(2):
            q, k = pair_operands(source, krp, p)
            made[p] = dot(k, q, NT)
            for qc in range(queries // 256):
                cols = slice(qc * 256, (qc + 1) * 256)
                out_ref[pl.ds(4 * step + 2 * n + p, 1), cols] = online_lse(done.at[p], bias, cols)


def probs_kernel(lse_ref, krt_ref, *refs):
    first, odd_in, next_in = refs[:3], refs[3:6], refs[6:9]
    out_ref, krp, even, odd = refs[9:]
    step = pl.program_id(0)
    queries, keys = out_ref.shape

    @pl.when(step == 0)
    def _():
        fill_rope(krt_ref, krp)
        for p in range(2):
            even[p] = dot(*pair_operands(first, krp, p), NT)
        out_ref[...] = jnp.zeros_like(out_ref)

    for n, (source, done, made) in enumerate(((odd_in, even, odd), (next_in, odd, even))):
        at = 4 * step + 2 * n
        lse = [column(lse_ref[pl.ds(at + p, 1), :queries]) for p in range(2)]
        for half in range(2):
            made[half] = dot(*pair_operands(source, krp, half), NT)
            for r in range(8 * half, 8 * half + 8):
                rows = slice(r * 32, (r + 1) * 32)
                total = out_ref[rows, :]
                for p in range(2):
                    s = done[p, rows, :] * SCORE_SCALE - lanes_of(lse[p][rows], keys)
                    total = total + jnp.exp2(s)
                out_ref[rows, :] = total


def lg_kernel(lse_ref, logits_ref, target_ref, lg_ref):
    rows, width = lg_ref.shape
    lse = column(lse_ref[:1, :])[:rows]
    for c in range(width // 128):
        cols = slice(c * 128, (c + 1) * 128)
        target = target_ref[0, :, cols]
        for h in range(1, N_HEAD):
            target = target + target_ref[h, :, cols]
        logits = logits_ref[:, cols]
        lg = jnp.exp2(logits - lse) - target * (1.0 / HEADS)
        lg_ref[:, cols] = jnp.where(logits > 0.5 * NEG, lg, 0.0)


def masked_lg(r, lg):
    lg = jnp.concatenate([lg] * (r.shape[0] // lg.shape[0]), axis=0)
    return jnp.where(r > 0, lg, jnp.zeros_like(lg))


def gk_kernel(lg_ref, iq_ref, w_ref, r_ref, gk_ref, gw_out, wb, lgb_ref, gkt_ref, gw_ref):
    step = pl.program_id(0)
    rows, keys = lg_ref.shape

    @pl.when(step == 0)
    def _():
        fill_weights(w_ref, wb)
        lgb_ref[...] = lg_ref[...].astype(BF16)
        gkt_ref[...] = jnp.zeros_like(gkt_ref)
        gw_ref[...] = jnp.zeros_like(gw_ref)

    q = stacked(iq_ref[...])
    w = jnp.concatenate([wb[step * GROUP + i] for i in range(GROUP)], axis=0)
    wqt = (q.astype(F32) * w).astype(BF16).T
    totals = [jnp.zeros((rows, 128), F32) for _ in range(GROUP)]
    for kc in range(keys // 256):
        cols = slice(kc * 256, (kc + 1) * 256)
        r = r_ref[0, :, cols]
        gkt_ref[:, cols] += dot(wqt, masked_lg(r, lgb_ref[:, cols]), NN)
        lg = lg_ref[:, cols]
        for i in range(GROUP):
            active = jnp.maximum(r[i * rows : (i + 1) * rows].astype(F32), 0.0) * lg
            totals[i] = totals[i] + active[:, :128] + active[:, 128:]
    lane = lax.broadcasted_iota(jnp.int32, (rows, IDX_HEADS), 1)
    new = gw_ref[...]
    for i in range(GROUP):
        value = jnp.sum(totals[i], axis=1, keepdims=True) * INV_ROOT
        new = jnp.where(lane == step * GROUP + i, value, new)
    gw_ref[...] = new

    @pl.when(step == pl.num_programs(0) - 1)
    def _():
        for c in range(keys // 128):
            gk_ref[c] = gkt_ref[:, c * 128 : (c + 1) * 128].T * INV_ROOT
        gw_out[...] = jnp.concatenate([gw_ref[i * 16 : (i + 1) * 16, :] for i in range(4)], axis=1)


def group_dests(part):
    y_lo, _, core = ctx_place()
    return [(y_lo * N_Z + part * 4 + i) * 2 + core for i in range(4)]


def inner_kernel(iq_ref, *refs):
    iks, (r_ref, ikb_ref) = refs[:4], refs[4:]
    part, source = pl.program_id(0), pl.program_id(1)

    @pl.when((part == 0) & (source == 0))
    def _():
        for i in range(4):
            ikb_ref[i] = iks[i][...].astype(BF16)

    dests = group_dests(part)
    blocks = [iq_ref[:, pl.ds(pl.multiple_of(c * 256, 256), 256)] for c in dests]
    q = jnp.concatenate([stacked(block) for block in blocks], axis=0)
    r_ref[0, 0] = dot(q, ikb_ref[source], NT).astype(BF16)


def gq_kernel(lg0, lg1, lg2, lg3, r_ref, ikb_ref, w_ref, gwy_ref, gwc_ref, gq_ref, wb, lgb_ref, g_ref):
    part, source = pl.program_id(0), pl.program_id(1)
    rows = lg0.shape[0]

    @pl.when((part == 0) & (source == 0))
    def _():
        fill_weights(w_ref, wb)
        for i, lg in enumerate((lg0, lg1, lg2, lg3)):
            lgb_ref[i] = lg[...].astype(BF16)

    grown = dot(masked_lg(r_ref[0, 0], lgb_ref[source]), ikb_ref[source], NN)

    @pl.when(source == 0)
    def _():
        g_ref[...] = grown

    @pl.when(source > 0)
    def _():
        g_ref[...] += grown

    @pl.when(source == 3)
    def _():
        gw = gwy_ref[...] + gwc_ref[...]
        dests = group_dests(part)
        for i in range(4):
            pair = []
            for n in range(2):
                at = (2 * i + n) * rows
                pair.append(g_ref[at : at + rows, :] * wb[dests[i] * 2 + n] * INV_ROOT)
            gq_ref[i, :rows, :] = jnp.concatenate(pair, axis=1)
            gq_ref[i, rows:, :] = gw


def finish_kernel(parts_ref, gks_ref, gq_ref, gk_ref, gw_ref):
    total, keys = parts_ref[0], gks_ref[0]
    for i in range(1, 8):
        total = total + parts_ref[i]
        keys = keys + gks_ref[i]
    gq_ref[...] = total[:64]
    gk_ref[...] = keys
    gw_ref[...] = jnp.concatenate([total[64:, i * 64 : (i + 1) * 64] for i in range(4)], axis=0)


def smem():
    return pl.BlockSpec(memory_space=pltpu.SMEM)


def whole(shape):
    return pl.BlockSpec(shape, lambda *_: (0,) * len(shape))


def wholes(arrays):
    return [whole(x.shape) for x in arrays]


def floats(*shapes):
    return [jax.ShapeDtypeStruct(s, F32) for s in shapes]


def in_vmem():
    return pl.BlockSpec(memory_space=pltpu.VMEM)


def call(kernel, name, grid, ins, in_specs, out_shapes, out_specs, scratch, vmem=56):
    return pl.pallas_call(
        kernel,
        grid=grid,
        in_specs=in_specs,
        out_specs=out_specs,
        out_shape=out_shapes,
        scratch_shapes=scratch,
        compiler_params=pltpu.CompilerParams(vmem_limit_bytes=vmem * 1024 * 1024),
        name=name,
    )(*ins)


def turns(count):
    return [lambda i: 0, lambda i: 2 * i + 1, lambda i: jnp.minimum(2 * i + 2, count - 1)]


def column_block(rows, width, turn):
    return pl.BlockSpec((rows, width), lambda i: (0, turn(i)))


def run_index(key_blocks, qpos, iq, ik, w):
    rows, keys = iq.shape[0], ik.shape[0]
    groups = IDX_HEADS // GROUP
    shapes = [(rows, keys), (16, 128)]
    stored = (groups, GROUP * rows, keys)
    return call(
        index_kernel,
        "index_forward",
        (groups // 2,),
        (key_blocks, qpos, iq, iq, iq, ik, w),
        [
            smem(),
            whole(qpos.shape),
            *[column_block(rows, GROUP * 128, turn) for turn in turns(groups)],
            *wholes([ik, w]),
        ],
        [*floats(*shapes), jax.ShapeDtypeStruct(stored, BF16)],
        [*[whole(s) for s in shapes], pl.BlockSpec((2, *stored[1:]), lambda i: (i, 0, 0))],
        [
            pltpu.VMEM((IDX_HEADS, rows, 128), F32),
            pltpu.VMEM((qpos.shape[1], 128), jnp.int32),
            pltpu.VMEM((GROUP * rows, keys), F32),
            pltpu.VMEM((GROUP * rows, keys), F32),
        ],
    )


def main_specs(queries, keys, pairs):
    specs = []
    for turn in turns(pairs):
        specs += [
            column_block(queries, 256, turn),
            column_block(queries, 128, turn),
            column_block(keys, 256, turn),
        ]
    return specs


def run_stats(key_blocks, qpos, index_row, qn, qr, kn, krt):
    queries, keys, pairs = qn.shape[0], kn.shape[0], qn.shape[1] // 256
    shape = (2 * pairs, queries + 128)
    return call(
        stats_kernel,
        "main_stats",
        (pairs // 2,),
        (key_blocks, qpos, index_row, krt, *[qn, qr, kn] * 3),
        [smem(), *wholes([qpos, index_row, krt]), *main_specs(queries, keys, pairs)],
        floats(shape),
        [whole(shape)],
        [
            pltpu.VMEM((keys, queries), F32),
            pltpu.VMEM((2, keys, 128), BF16),
            pltpu.VMEM((2, keys, queries), F32),
            pltpu.VMEM((2, keys, queries), F32),
        ],
    )[0]


def run_probs(lse, qn, qr, kn, krt):
    queries, keys, pairs = qn.shape[0], kn.shape[0], qn.shape[1] // 256
    return call(
        probs_kernel,
        "main_probs",
        (pairs // 2,),
        (lse, krt, *[qn, qr, kn] * 3),
        [*wholes([lse, krt]), *main_specs(queries, keys, pairs)],
        floats((queries, keys)),
        [whole((queries, keys))],
        [
            pltpu.VMEM((2, keys, 128), BF16),
            pltpu.VMEM((2, queries, keys), F32),
            pltpu.VMEM((2, queries, keys), F32),
        ],
    )[0]


def run_lg(lse, logits, target):
    return pl.pallas_call(
        lg_kernel,
        in_specs=[in_vmem()] * 3,
        out_specs=in_vmem(),
        out_shape=floats(logits.shape)[0],
        compiler_params=pltpu.CompilerParams(vmem_limit_bytes=8 * 1024 * 1024),
        name="logit_grad",
    )(lse, logits, target)


def run_gk(lg, iq, w, r):
    rows, keys = lg.shape
    shapes = [(keys // 128, 128, IDX_DIM), (16, 256)]
    return call(
        gk_kernel,
        "grad_k",
        (IDX_HEADS // GROUP,),
        (lg, iq, w, r),
        [
            whole(lg.shape),
            pl.BlockSpec((rows, GROUP * 128), lambda i: (0, i)),
            whole(w.shape),
            pl.BlockSpec((1, *r.shape[1:]), lambda i: (i, 0, 0)),
        ],
        floats(*shapes),
        [whole(s) for s in shapes],
        [
            pltpu.VMEM((IDX_HEADS, rows, 128), F32),
            pltpu.VMEM((rows, keys), BF16),
            pltpu.VMEM((IDX_DIM, keys), F32),
            pltpu.VMEM((rows, IDX_HEADS), F32),
        ],
    )


def run_inner(iq, iks):
    rows, keys = iq.shape[0], iks[0].shape[0]
    stored, kept = (2, 4, 8 * rows, keys), (4, keys, IDX_DIM)
    return call(
        inner_kernel,
        "inner_group",
        (2, 4),
        [iq, *iks],
        wholes([iq, *iks]),
        [jax.ShapeDtypeStruct(stored, BF16), jax.ShapeDtypeStruct(kept, BF16)],
        [pl.BlockSpec((1, 1, *stored[2:]), lambda i, j: (i, j, 0, 0)), whole(kept)],
        [],
    )


def run_gq(lgs, r, ikb, w, gwy, gwc):
    rows, keys = lgs[0].shape
    shape = (N_Z, rows + 16, 256)
    return call(
        gq_kernel,
        "grad_q",
        (2, 4),
        [*lgs, r, ikb, w, gwy, gwc],
        [
            *wholes(lgs),
            pl.BlockSpec((1, 1, *r.shape[2:]), lambda i, j: (i, j, 0, 0)),
            *wholes([ikb, w, gwy, gwc]),
        ],
        floats(shape),
        [pl.BlockSpec((4, *shape[1:]), lambda i, j: (i, 0, 0))],
        [
            pltpu.VMEM((IDX_HEADS, rows, 128), F32),
            pltpu.VMEM((4, rows, keys), BF16),
            pltpu.VMEM((8 * rows, IDX_DIM), F32),
        ],
    )[0]


def run_finish(parts, gks):
    shapes = [(64, 256), (128, 128), (64, 64)]
    return pl.pallas_call(
        finish_kernel,
        in_specs=[in_vmem()] * 2,
        out_specs=[in_vmem()] * 3,
        out_shape=floats(*shapes),
        name="finish",
    )(parts, gks)


def ctx_xor(value, bits):
    return lax.ppermute(value, "ctx", [(i, i ^ bits) for i in range(N_CTX)])


def z_shift(value, by):
    to = [i // 16 * 16 + (i // 2 + by) % N_Z * 2 + i % 2 for i in range(N_CTX)]
    return lax.ppermute(value, "ctx", list(enumerate(to)))


def merged(*values):
    top = values[0]
    for value in values[1:]:
        top = jnp.maximum(top, value)
    total = sum(jnp.exp2(value - top) for value in values)
    return top + jnp.log2(total)


def per_device(qn, qr, kn, kr, iq, ik, w, query_pos, key_blocks):
    qpos = query_pos[None, :]
    krt = kr.T
    ikf = ik.astype(F32)
    ikf_y = ctx_xor(ikf, 16)
    logits, index_row, r = run_index(key_blocks, qpos, iq, ik, w)
    lse = run_stats(key_blocks, qpos, index_row, qn, qr, kn, krt)
    lse, ikf_y = lax.optimization_barrier((lse, ikf_y))
    lse = merged(lse, ctx_xor(lse, 1))
    lse = merged(lse, ctx_xor(lse, 16))
    below, above = z_shift(lse, 1), z_shift(lse, -1)
    two, three = merged(lse, below), merged(lse, below, above)
    lse = merged(three, z_shift(three, 3), z_shift(two, -3))
    probs = run_probs(lse, qn, qr, kn, krt)
    probs, ikf, ikf_y = lax.optimization_barrier((probs, ikf, ikf_y))
    target = lax.all_to_all(probs.reshape(N_HEAD, -1, probs.shape[1]), "head", 0, 0)
    r_group, ikb = run_inner(iq, [ik, ctx_xor(ikf, 1), ikf_y, ctx_xor(ikf_y, 1)])

    target, r_group, ikb = lax.optimization_barrier((target, r_group, ikb))
    lg = run_lg(lse[:8, qn.shape[0] :], logits, target)
    lg_y, lg_c = ctx_xor(lg, 16), ctx_xor(lg, 1)
    gks, gw = run_gk(lg, iq, w, r)
    lg_y, gw = lax.optimization_barrier((lg_y, gw))
    lg_yc = ctx_xor(lg_y, 1)
    gw = gw + ctx_xor(gw, 16)
    parts = run_gq([lg, lg_c, lg_y, lg_yc], r_group, ikb, w, gw, ctx_xor(gw, 1))
    gks, parts = lax.optimization_barrier((gks, parts))
    groups = [[(y * N_Z + z) * 2 + c for z in range(N_Z)] for y in range(2) for c in range(2)]
    parts = lax.all_to_all(parts, "ctx", 0, 0, axis_index_groups=groups)
    gks = lax.all_to_all(gks, "head", 0, 0)
    return run_finish(parts, gks)


def solution(mesh):
    return jax.shard_map(
        per_device,
        mesh=mesh,
        in_specs=(
            P(None, "head"),
            P(None, "head"),
            P("ctx", "head"),
            P("ctx", None),
            P("head", None),
            P("ctx", None),
            P("head", None),
            P(),
            P("ctx"),
        ),
        out_specs=(P("head", "ctx"), P(("ctx", "head"), None), P("head", None)),
        check_vma=False,
    )
```

time: 574 us -> 167 us (0.29)
  blocking collectives: 216 us -> 39.1 us
  waiting for transfers between devices: 194 us -> 30.4 us
  Pallas kernels: 0 us -> 65 us
  other arithmetic: 67.7 us -> 3.28 us
  matrix products: 62.4 us -> 0 us
  starting transfers between devices: 0.2 us -> 22.2 us
  between operations: 15.4 us -> 1.4 us
  local copies, waits for them, and re-layouts: 13.9 us -> 3.33 us
    psum x1 -> x0, waiting for transfers between devices: 114 us -> none  [per_device(): summed_all = lax.psum(head_probs, 'head')]
    unnamed x1 -> x0, blocking collectives: 111 us -> none
    psum x1 -> x0, blocking collectives: 105 us -> none  [per_device(): grad_index_w = lax.psum(weight_part, 'ctx')]
    reduce_scatter x2 -> x0, waiting for transfers between devices: 73.5 us -> none  [the longest x1 73.5 us: per_device(): lax.psum_scatter(query_part, 'ctx', scatter_dimension=1, tiled=True)]
    pallas_call x0 -> x8, Pallas kernels: none -> 65 us  [the longest x6 63 us: call(): pl.pallas_call(kernel, grid=grid, in_specs=in_specs, out_specs=out_specs,...]
    dot_general x5 -> x0, matrix products: 62.4 us -> none  [the longest x1 22.4 us: per_device(): jnp.einsum('qhd,khd->hqk', query_nope, key_nope, preferred_element_type=j...]
    reduce_sum x4 -> x0, other arithmetic: 39.2 us -> none  [the longest x2 15.7 us: local_stats(): jnp.sum(jnp.where(visible, jnp.exp(values - row_top[..., None]), 0.0), ax...]
    all_to_all x0 -> x2, blocking collectives: none -> 39.1 us  [the longest x1 23.2 us: per_device(): parts = lax.all_to_all(parts, 'ctx', 0, 0, axis_index_groups=groups)]
  transfers between devices with their start and end apart: 5 -> 15, of which waited for: 3 -> 11; matrix products, arithmetic and copies ran while one was open for 6% -> 1% of each run, Pallas kernels for 0% -> 25%
where the time goes in v1:
time: 167 us; the launch traced here: 165 us
  Pallas kernels  65 us (39%)
  blocking collectives  39.1 us (23%)
  waiting for transfers between devices  30.4 us (18%)
  starting transfers between devices  22.2 us (13%)
  local copies, waits for them, and re-layouts  3.33 us (2%)
  other arithmetic  3.28 us (2%)
    pallas_call x6, Pallas kernels, call(): pl.pallas_call(kernel, grid=grid, in_specs=in_specs, out_specs=out_specs,...  63 us
    all_to_all x1, blocking collectives, per_device(): parts = lax.all_to_all(parts, 'ctx', 0, 0, axis_index_groups=groups)  23.2 us
    all_to_all x1, blocking collectives, per_device(): gks = lax.all_to_all(gks, 'head', 0, 0)  15.9 us
    all_to_all x1, waiting for transfers between devices, per_device(): lax.all_to_all(probs.reshape(N_HEAD, -1, probs.shape[1]), 'head', 0, 0)  11 us
    ppermute x4, starting transfers between devices, z_shift(): return lax.ppermute(value, 'ctx', list(enumerate(to)))  9.84 us
    ppermute x10, waiting for transfers between devices, ctx_xor(): return lax.ppermute(value, 'ctx', [(i, i ^ bits) for i in range(N_CTX)])  9.69 us
    ppermute x4, waiting for transfers between devices, z_shift(): return lax.ppermute(value, 'ctx', list(enumerate(to)))  9.69 us
    all_to_all x1, starting transfers between devices, per_device(): lax.all_to_all(probs.reshape(N_HEAD, -1, probs.shape[1]), 'head', 0, 0)  7.31 us
  transfers between devices with their start and end apart: 15, of which 11 were waited for; matrix products, arithmetic and copies ran while one was open for 1% of the time, Pallas kernels for 25%

profile of v1, /device:TPU:2, one launch (start us, length us, event | category | flops | bytes accessed | tf_op | source)
XLA Modules:
  0.0 164.8 jit_solution(11283084467722972990)
XLA Ops:
  0.6 1.0 convert_element_type.3
  1.6 1.7 %collective-permute-start = (f32[1024,128]{1,0:T(8,128)S(1)}, f32[1024,128]{1,0:T(8,128)S(1)}, u32[]{:S(2)}, u32[]{:S(2)}) collective-permute-start(f32[1024,128]{1,0:T(8,128)S(1)} %convert_element_type.3), channel_id=1, source_target_pairs={{0,128},{8,136},{16,144},{24,152},{32,160},{40,168},{48,176},{56,1... | collective-permute-start | bytes 1572872 | tf_op jit(solution)/shard_map/ppermute | solution.py:501
  3.9 8.2 %index_forward.1 = (f32[64,1024]{1,0:T(8,128)}, f32[16,128]{1,0:T(8,128)}, bf16[8,512,1024]{2,1,0:T(8,128)(2,1)}) custom-call(s32[1]{0:T(128)S(6)} %copy.12.base_ref, s32[1,512]{1,0:T(1,128)} %bitcast.6, bf16[64,8192]{1,0:T(8,128)(2,1)} %iq_ref.3, bf16[64,8192]{1,0:T(8,128)(2,1)} %iq_ref.3, bf16[64,8192]{1,0:T(8,128)(2,1)} %iq_ref.3, ...), custom_call_target="tpu_custom_call" | custom-call | tf_op jit(solution)/shard_map/index_forward/pallas_call | solution.py:319
  12.2 14.6 %main_stats.1 = f32[16,640]{1,0:T(8,128)} custom-call(s32[1]{0:T(128)S(6)} %copy.12.base_ref, s32[1,512]{1,0:T(1,128)} %bitcast.7, f32[16,128]{1,0:T(8,128)} %get-tuple-element.22.row_ref, bf16[64,1024]{1,0:T(8,128)(2,1)} %bitcast.4, bf16[512,2048]{1,0:T(8,128)(2,1)} %refs_6_.3, bf16[512,1024]{1,0:T(8,128)(2,1)} %refs_7_.3, bf16[1024,2048]{1,0:T(8,128)(2,1)} %refs_8_.3, ...), custom_call_target="tpu_custom_call" | custom-call | tf_op jit(solution)/shard_map/main_stats/pallas_call | solution.py:319
  26.7 0.0 collective-permute-done.refs_2_
  26.8 0.1 collective-permute-start.1
  26.9 1.4 collective-permute-done.1
  28.3 0.8 multiply_add_fusion.4
  29.1 0.5 collective-permute-start.2
  29.6 3.6 %collective-permute-done.2 = f32[16,640]{1,0:T(8,128)S(1)} collective-permute-done((f32[16,640]{1,0:T(8,128)S(1)}, f32[16,640]{1,0:T(8,128)S(1)}, u32[]{:S(2)}, u32[]{:S(2)}) %collective-permute-start.2) | collective-permute-done | bytes 40992 | tf_op jit(solution)/shard_map/ppermute | solution.py:501
  33.2 5.9 %collective-permute-start.4 = (f32[16,640]{1,0:T(8,128)S(1)}, f32[16,640]{1,0:T(8,128)S(1)}, u32[]{:S(2)}, u32[]{:S(2)}) collective-permute-start(f32[16,640]{1,0:T(8,128)S(1)} %multiply_add_fusion.3), channel_id=1, source_target_pairs={{0,112},{8,120},{16,0},{24,8},{32,16},{40,24},{48,32},{56,40},{64,... | collective-permute-start | bytes 122888 | tf_op jit(solution)/shard_map/ppermute | solution.py:506
  39.1 1.7 %collective-permute-done.4 = f32[16,640]{1,0:T(8,128)S(1)} collective-permute-done((f32[16,640]{1,0:T(8,128)S(1)}, f32[16,640]{1,0:T(8,128)S(1)}, u32[]{:S(2)}, u32[]{:S(2)}) %collective-permute-start.4) | collective-permute-done | bytes 40992 | tf_op jit(solution)/shard_map/ppermute | solution.py:506
  40.8 3.5 %collective-permute-done.3 = f32[16,640]{1,0:T(8,128)S(1)} collective-permute-done((f32[16,640]{1,0:T(8,128)S(1)}, f32[16,640]{1,0:T(8,128)S(1)}, u32[]{:S(2)}, u32[]{:S(2)}) %collective-permute-start.3) | collective-permute-done | bytes 40992 | tf_op jit(solution)/shard_map/ppermute | solution.py:506
  44.4 0.1 multiply_add_fusion.2
  44.4 0.8 collective-permute-start.6
  45.2 3.1 %collective-permute-start.5 = (f32[16,640]{1,0:T(8,128)S(1)}, f32[16,640]{1,0:T(8,128)S(1)}, u32[]{:S(2)}, u32[]{:S(2)}) collective-permute-start(f32[16,640]{1,0:T(8,128)S(1)} %get-tuple-element.41), channel_id=1, source_target_pairs={{0,48},{8,56},{16,64},{24,72},{32,80},{40,88},{48,96},{56,104},{64... | collective-permute-start | bytes 122888 | tf_op jit(solution)/shard_map/ppermute | solution.py:506
  48.3 2.3 %collective-permute-done.6 = f32[16,640]{1,0:T(8,128)S(1)} collective-permute-done((f32[16,640]{1,0:T(8,128)S(1)}, f32[16,640]{1,0:T(8,128)S(1)}, u32[]{:S(2)}, u32[]{:S(2)}) %collective-permute-start.6) | collective-permute-done | bytes 40992 | tf_op jit(solution)/shard_map/ppermute | solution.py:506
  50.6 2.2 %collective-permute-done.5 = f32[16,640]{1,0:T(8,128)S(1)} collective-permute-done((f32[16,640]{1,0:T(8,128)S(1)}, f32[16,640]{1,0:T(8,128)S(1)}, u32[]{:S(2)}, u32[]{:S(2)}) %collective-permute-start.5) | collective-permute-done | bytes 40992 | tf_op jit(solution)/shard_map/ppermute | solution.py:506
  52.8 0.7 multiply_add_fusion.lse_ref
  53.5 11.8 %main_probs.1 = f32[512,1024]{1,0:T(8,128)} custom-call(f32[16,640]{1,0:T(8,128)} %multiply_add_fusion.lse_ref, bf16[64,1024]{1,0:T(8,128)(2,1)} %bitcast.5, bf16[512,2048]{1,0:T(8,128)(2,1)} %refs_6_.3, bf16[512,1024]{1,0:T(8,128)(2,1)} %refs_7_.3, bf16[1024,2048]{1,0:T(8,128)(2,1)} %refs_8_.3, bf16[512,2048]{1,0:T(8,128)(2,1)} %refs_6_.3, ...), custom_call_target="tpu_custom_call" | custom-call | tf_op jit(solution)/shard_map/main_probs/pallas_call | solution.py:319
  65.2 7.3 %all-to-all-start = ((f32[8,64,1024]{2,1,0:T(8,128)}), f32[8,64,1024]{2,1,0:T(8,128)S(1)}, u32[]{:S(2)}, u32[]{:S(2)}) async-start(f32[8,64,1024]{2,1,0:T(8,128)} %bitcast.3), calls=%async_computation | async-start | bytes 4194304 | tf_op jit(solution)/shard_map/all_to_all | solution.py:532
  72.5 0.0 collective-permute-start.7
  72.5 0.5 collective-permute-start.8
  73.1 0.7 slice.4.lse_ref
  73.7 0.7 collective-permute-done.7.refs_1_
  74.5 0.7 collective-permute-done.8.refs_3_
  75.2 0.1 copy-done.4
  75.3 0.8 copy-done.5
  76.1 8.3 %inner_group.1 = (bf16[2,4,512,1024]{3,2,1,0:T(8,128)(2,1)}, bf16[4,1024,128]{2,1,0:T(8,128)(2,1)}) custom-call(bf16[64,8192]{1,0:T(8,128)(2,1)} %iq_ref.3, bf16[1024,128]{1,0:T(8,128)(2,1)} %refs_0_.5, f32[1024,128]{1,0:T(8,128)} %copy-done.4, f32[1024,128]{1,0:T(8,128)} %copy-done.3, f32[1024,128]{1,0:T(8,128)} %copy-done.5), custom_call_target="tpu_custom_call" | custom-call | tf_op jit(solution)/shard_map/inner_group/pallas_call | solution.py:319
  84.3 11.0 %all-to-all-done.target_ref = f32[8,64,1024]{2,1,0:T(8,128)S(1)} async-done(((f32[8,64,1024]{2,1,0:T(8,128)}), f32[8,64,1024]{2,1,0:T(8,128)S(1)}, u32[]{:S(2)}, u32[]{:S(2)}) %all-to-all-start) | async-done | bytes 2097184 | tf_op jit(solution)/shard_map/all_to_all | solution.py:532
  95.4 0.1 logit_grad.1.lg_ref.lg0
  95.5 0.2 collective-permute-start.10
  95.7 0.0 collective-permute-start.9
  95.7 0.5 copy-done
  96.2 10.2 %grad_k.1 = (f32[8,128,128]{2,1,0:T(8,128)}, f32[16,256]{1,0:T(8,128)}) custom-call(f32[64,1024]{1,0:T(8,128)} %copy-done, bf16[64,8192]{1,0:T(8,128)(2,1)} %iq_ref.3, f32[64,64]{1,0:T(8,128)} %w_ref.5, bf16[8,512,1024]{2,1,0:T(8,128)(2,1)} %get-tuple-element.32.r_ref), custom_call_target="tpu_custom_call" | custom-call | tf_op jit(solution)/shard_map/grad_k/pallas_call | solution.py:319
  106.4 0.0 collective-permute-done.10.lg2
  106.4 0.1 collective-permute-start.11
  106.5 1.9 %collective-permute-start.12 = (f32[16,256]{1,0:T(8,128)}, f32[16,256]{1,0:T(8,128)S(1)}, u32[]{:S(2)}, u32[]{:S(2)}) collective-permute-start(f32[16,256]{1,0:T(8,128)} %get-tuple-element.38), channel_id=1, source_target_pairs={{0,128},{8,136},{16,144},{24,152},{32,160},{40,168},{48,176},{56,1... | collective-permute-start | bytes 49160 | tf_op jit(solution)/shard_map/ppermute | solution.py:501
  108.4 2.1 %collective-permute-done.12 = f32[16,256]{1,0:T(8,128)S(1)} collective-permute-done((f32[16,256]{1,0:T(8,128)}, f32[16,256]{1,0:T(8,128)S(1)}, u32[]{:S(2)}, u32[]{:S(2)}) %collective-permute-start.12) | collective-permute-done | bytes 16416 | tf_op jit(solution)/shard_map/ppermute | solution.py:501
  110.5 0.7 add.51.gwy_ref
  111.2 0.0 collective-permute-done.9.lg1
  111.3 1.2 collective-permute-done.13.gwc_ref
  112.4 0.6 copy-done.10
  113.0 0.7 copy-done.8
  113.7 10.0 %grad_q.1 = f32[8,80,256]{2,1,0:T(8,128)} custom-call(f32[64,1024]{1,0:T(8,128)} %copy-done, f32[64,1024]{1,0:T(8,128)} %copy-done.7, f32[64,1024]{1,0:T(8,128)} %copy-done.6, f32[64,1024]{1,0:T(8,128)} %copy-done.8, bf16[2,4,512,1024]{3,2,1,0:T(8,128)(2,1)} %get-tuple-element.36.r_ref, bf16[4,1024,128]{2,1,0:T(8,128)(2,1)} %get-tuple-element.37.ikb_ref, ...), custom_call_target="tpu_custom_call" | custom-call | tf_op jit(solution)/shard_map/grad_q/pallas_call | solution.py:319
  123.7 15.9 %all_to_all.15.gks_ref = f32[8,128,128]{2,1,0:T(8,128)} all-to-all(f32[8,128,128]{2,1,0:T(8,128)S(1)} %copy-done.2), channel_id=1, replica_groups=mesh['ctx'=32,'head'=8] {'head'}, dimensions={0} | all-to-all | bytes 1048576 | tf_op jit(solution)/shard_map/all_to_all | solution.py:546
  139.6 23.2 %all_to_all.16.parts_ref = f32[8,80,256]{2,1,0:T(8,128)} all-to-all(f32[8,80,256]{2,1,0:T(8,128)} %grad_q.1), channel_id=1, replica_groups={{0,16,32,48,64,80,96,112},{8,24,40,56,72,88,104,120},{128,144,160,176,1..., dimensions={0} | all-to-all | bytes 1310720 | tf_op jit(solution)/shard_map/all_to_all | solution.py:545
  162.8 1.9 %finish.1 = (f32[64,256]{1,0:T(8,128)}, f32[128,128]{1,0:T(8,128)}, f32[64,64]{1,0:T(8,128)}) custom-call(f32[8,80,256]{2,1,0:T(8,128)} %all_to_all.16.parts_ref, f32[8,128,128]{2,1,0:T(8,128)} %all_to_all.15.gks_ref), custom_call_target="tpu_custom_call" | custom-call | tf_op jit(solution)/shard_map/finish/pallas_call | solution.py:491
  (21 shorter events, 0.1 us)
Async XLA Ops:
  1.6 25.1 %collective-permute-start = (f32[1024,128]{1,0:T(8,128)S(1)}, f32[1024,128]{1,0:T(8,128)S(1)}, u32[]{:S(2)}, u32[]{:S(2)}) collective-permute-start(f32[1024,128]{1,0:T(8,128)S(1)} %convert_element_type.3), channel_id=1, source_target_pairs={{0,128},{8,136},{16,144},{24,152},{32,160},{40,168},{48,176},{56,1... | collective-permute-start | bytes 1572872 | tf_op jit(solution)/shard_map/ppermute | solution.py:501
  26.7 45.8 %copy-start.3 = (f32[1024,128]{1,0:T(8,128)}, f32[1024,128]{1,0:T(8,128)S(1)}, u32[]{:S(2)}) copy-start(f32[1024,128]{1,0:T(8,128)S(1)} %collective-permute-done.refs_2_) | copy-start | bytes 1572868
  26.8 1.5 collective-permute-start.1
  29.1 4.1 %collective-permute-start.2 = (f32[16,640]{1,0:T(8,128)S(1)}, f32[16,640]{1,0:T(8,128)S(1)}, u32[]{:S(2)}, u32[]{:S(2)}) collective-permute-start(f32[16,640]{1,0:T(8,128)S(1)} %multiply_add_fusion.4), channel_id=1, source_target_pairs={{0,128},{8,136},{16,144},{24,152},{32,160},{40,168},{48,176},{56,1... | collective-permute-start | bytes 122888 | tf_op jit(solution)/shard_map/ppermute | solution.py:501
  33.2 7.6 %collective-permute-start.4 = (f32[16,640]{1,0:T(8,128)S(1)}, f32[16,640]{1,0:T(8,128)S(1)}, u32[]{:S(2)}, u32[]{:S(2)}) collective-permute-start(f32[16,640]{1,0:T(8,128)S(1)} %multiply_add_fusion.3), channel_id=1, source_target_pairs={{0,112},{8,120},{16,0},{24,8},{32,16},{40,24},{48,32},{56,40},{64,... | collective-permute-start | bytes 122888 | tf_op jit(solution)/shard_map/ppermute | solution.py:506
  39.1 5.2 %collective-permute-start.3 = (f32[16,640]{1,0:T(8,128)S(1)}, f32[16,640]{1,0:T(8,128)S(1)}, u32[]{:S(2)}, u32[]{:S(2)}) collective-permute-start(f32[16,640]{1,0:T(8,128)S(1)} %multiply_add_fusion.3), channel_id=1, source_target_pairs={{0,16},{8,24},{16,32},{24,40},{32,48},{40,56},{48,64},{56,72},{64,... | collective-permute-start | bytes 122888 | tf_op jit(solution)/shard_map/ppermute | solution.py:506
  44.4 6.2 %collective-permute-start.6 = (f32[16,640]{1,0:T(8,128)S(1)}, f32[16,640]{1,0:T(8,128)S(1)}, u32[]{:S(2)}, u32[]{:S(2)}) collective-permute-start(f32[16,640]{1,0:T(8,128)S(1)} %get-tuple-element.42), channel_id=1, source_target_pairs={{0,80},{8,88},{16,96},{24,104},{32,112},{40,120},{48,0},{56,8},{64... | collective-permute-start | bytes 122888 | tf_op jit(solution)/shard_map/ppermute | solution.py:506
  45.2 7.6 %collective-permute-start.5 = (f32[16,640]{1,0:T(8,128)S(1)}, f32[16,640]{1,0:T(8,128)S(1)}, u32[]{:S(2)}, u32[]{:S(2)}) collective-permute-start(f32[16,640]{1,0:T(8,128)S(1)} %get-tuple-element.41), channel_id=1, source_target_pairs={{0,48},{8,56},{16,64},{24,72},{32,80},{40,88},{48,96},{56,104},{64... | collective-permute-start | bytes 122888 | tf_op jit(solution)/shard_map/ppermute | solution.py:506
  65.2 30.1 %copy-start.1 = (f32[64,1024]{1,0:T(8,128)S(1)}, f32[64,1024]{1,0:T(8,128)}, u32[]{:S(2)}) copy-start(f32[64,1024]{1,0:T(8,128)} %get-tuple-element.24.logits_ref) | copy-start | bytes 786436
  65.2 30.1 %all-to-all-start = ((f32[8,64,1024]{2,1,0:T(8,128)}), f32[8,64,1024]{2,1,0:T(8,128)S(1)}, u32[]{:S(2)}, u32[]{:S(2)}) async-start(f32[8,64,1024]{2,1,0:T(8,128)} %bitcast.3), calls=%async_computation | async-start | bytes 4194304 | tf_op jit(solution)/shard_map/all_to_all | solution.py:532
  72.5 1.9 %collective-permute-start.7 = (f32[1024,128]{1,0:T(8,128)S(1)}, f32[1024,128]{1,0:T(8,128)S(1)}, u32[]{:S(2)}, u32[]{:S(2)}) collective-permute-start(f32[1024,128]{1,0:T(8,128)S(1)} %convert_element_type.3), channel_id=1, source_target_pairs={{0,8},{8,0},{16,24},{24,16},{32,40},{40,32},{48,56},{56,48},{64,72... | collective-permute-start | bytes 1572872 | tf_op jit(solution)/shard_map/ppermute | solution.py:501
  72.5 2.7 %collective-permute-start.8 = (f32[1024,128]{1,0:T(8,128)S(1)}, f32[1024,128]{1,0:T(8,128)S(1)}, u32[]{:S(2)}, u32[]{:S(2)}) collective-permute-start(f32[1024,128]{1,0:T(8,128)S(1)} %collective-permute-done.refs_2_), channel_id=1, source_target_pairs={{0,8},{8,0},{16,24},{24,16},{32,40},{40,32},{48,56},{56,48},{64,72... | collective-permute-start | bytes 1572872 | tf_op jit(solution)/shard_map/ppermute | solution.py:501
  74.4 0.8 copy-start.4
  75.2 0.8 copy-start.5
  95.5 0.7 copy-start
  95.5 10.8 %collective-permute-start.10 = (f32[64,1024]{1,0:T(8,128)S(1)}, f32[64,1024]{1,0:T(8,128)S(1)}, u32[]{:S(2)}, u32[]{:S(2)}) collective-permute-start(f32[64,1024]{1,0:T(8,128)S(1)} %logit_grad.1.lg_ref.lg0), channel_id=1, source_target_pairs={{0,128},{8,136},{16,144},{24,152},{32,160},{40,168},{48,176},{56,1... | collective-permute-start | bytes 786440 | tf_op jit(solution)/shard_map/ppermute | solution.py:501
  95.7 15.5 %collective-permute-start.9 = (f32[64,1024]{1,0:T(8,128)S(1)}, f32[64,1024]{1,0:T(8,128)S(1)}, u32[]{:S(2)}, u32[]{:S(2)}) collective-permute-start(f32[64,1024]{1,0:T(8,128)S(1)} %logit_grad.1.lg_ref.lg0), channel_id=1, source_target_pairs={{0,8},{8,0},{16,24},{24,16},{32,40},{40,32},{48,56},{56,48},{64,72... | collective-permute-start | bytes 786440 | tf_op jit(solution)/shard_map/ppermute | solution.py:501
  106.4 6.1 %copy-start.6 = (f32[64,1024]{1,0:T(8,128)}, f32[64,1024]{1,0:T(8,128)S(1)}, u32[]{:S(2)}) copy-start(f32[64,1024]{1,0:T(8,128)S(1)} %collective-permute-done.10.lg2) | copy-start | bytes 786436
  106.4 6.1 %collective-permute-start.11 = (f32[64,1024]{1,0:T(8,128)S(1)}, f32[64,1024]{1,0:T(8,128)S(1)}, u32[]{:S(2)}, u32[]{:S(2)}) collective-permute-start(f32[64,1024]{1,0:T(8,128)S(1)} %collective-permute-done.10.lg2), channel_id=1, source_target_pairs={{0,8},{8,0},{16,24},{24,16},{32,40},{40,32},{48,56},{56,48},{64,72... | collective-permute-start | bytes 786440 | tf_op jit(solution)/shard_map/ppermute | solution.py:501
  106.5 4.0 %collective-permute-start.12 = (f32[16,256]{1,0:T(8,128)}, f32[16,256]{1,0:T(8,128)S(1)}, u32[]{:S(2)}, u32[]{:S(2)}) collective-permute-start(f32[16,256]{1,0:T(8,128)} %get-tuple-element.38), channel_id=1, source_target_pairs={{0,128},{8,136},{16,144},{24,152},{32,160},{40,168},{48,176},{56,1... | collective-permute-start | bytes 49160 | tf_op jit(solution)/shard_map/ppermute | solution.py:501
  111.2 1.2 copy-start.9
  111.2 12.5 %copy-start.2 = (f32[8,128,128]{2,1,0:T(8,128)S(1)}, f32[8,128,128]{2,1,0:T(8,128)}, u32[]{:S(2)}) copy-start(f32[8,128,128]{2,1,0:T(8,128)} %get-tuple-element.40) | copy-start | bytes 1572868
  111.2 1.2 collective-permute-start.13
  111.2 1.2 copy-start.7
  112.4 0.6 copy-start.10
  113.0 0.7 copy-start.8

commit v2 on v1

--- a/solution.py
+++ b/solution.py
@@ -61,33 +61,27 @@
 
 
 def index_kernel(
-    base_ref, qpos_ref, iq_first, iq_odd, iq_next, ik_ref, w_ref, logits_ref, row_ref, r_ref,
-    wb, qcol, even, odd,
+    base_ref, qpos_ref, iq_ref, ik_ref, w_ref, logits_ref, row_ref, r_ref, wb, qcol, s_ref
 ):
     step = pl.program_id(0)
     rows, keys = logits_ref.shape
 
     @pl.when(step == 0)
     def _():
-        even[...] = dot(stacked(iq_first[...]), ik_ref[...], NT)
         fill_weights(w_ref, wb)
         logits_ref[...] = jnp.zeros_like(logits_ref)
         qcol[...] = column(qpos_ref[...])
 
-    for n, (source, done, made) in enumerate(((iq_odd, even, odd), (iq_next, odd, even))):
-        q = stacked(source[...])
-        for half in range(2):
-            wide = slice(half * 512, (half + 1) * 512)
-            made[:, wide] = dot(q, ik_ref[wide, :], NT)
-            for kc in range(4 * half, 4 * half + 4):
-                cols = slice(kc * 128, (kc + 1) * 128)
-                total = logits_ref[:, cols]
-                for i in range(GROUP):
-                    mine = slice(i * rows, (i + 1) * rows)
-                    inner = done[mine, cols]
-                    r_ref[n, mine, cols] = inner.astype(BF16)
-                    total = total + jnp.maximum(inner, 0.0) * wb[(2 * step + n) * GROUP + i]
-                logits_ref[:, cols] = total
+    s_ref[...] = dot(stacked(iq_ref[...]), ik_ref[...], NT)
+    for kc in range(keys // 128):
+        cols = slice(kc * 128, (kc + 1) * 128)
+        total = logits_ref[:, cols]
+        for i in range(GROUP):
+            mine = slice(i * rows, (i + 1) * rows)
+            inner = s_ref[mine, cols]
+            r_ref[0, mine, cols] = inner.astype(BF16)
+            total = total + jnp.maximum(inner, 0.0) * wb[step * GROUP + i]
+        logits_ref[:, cols] = total
 
     @pl.when(step == pl.num_programs(0) - 1)
     def _():
@@ -125,56 +119,48 @@
     return best * SCORE_SCALE + jnp.log2(total)
 
 
-def stats_kernel(base_ref, qpos_ref, row_ref, krt_ref, *refs):
-    first, odd_in, next_in = refs[:3], refs[3:6], refs[6:9]
-    out_ref, bias, krp, even, odd = refs[9:]
+def stats_kernel(
+    base_ref, qpos_ref, row_ref, krt_ref, qn_ref, qr_ref, kn_ref, out_ref, bias, krp, s_ref
+):
     step = pl.program_id(0)
     keys, queries = bias.shape
 
     @pl.when(step == 0)
     def _():
-        fill_rope(krt_ref, krp)
-        for p in range(2):
-            q, k = pair_operands(first, krp, p)
-            even[p] = dot(k, q, NT)
         key = lax.broadcasted_iota(jnp.int32, bias.shape, 0) + base_ref[0] * keys
         bias[...] = jnp.where(key <= qpos_ref[...], 0.0, NEG)
+        fill_rope(krt_ref, krp)
         out_ref[:, queries:] = row_ref[...]
 
-    for n, (source, done, made) in enumerate(((odd_in, even, odd), (next_in, odd, even))):
-        for p in range(2):
-            q, k = pair_operands(source, krp, p)
-            made[p] = dot(k, q, NT)
-            for qc in range(queries // 256):
-                cols = slice(qc * 256, (qc + 1) * 256)
-                out_ref[pl.ds(4 * step + 2 * n + p, 1), cols] = online_lse(done.at[p], bias, cols)
-
-
-def probs_kernel(lse_ref, krt_ref, *refs):
-    first, odd_in, next_in = refs[:3], refs[3:6], refs[6:9]
-    out_ref, krp, even, odd = refs[9:]
+    for p in range(2):
+        q, k = pair_operands((qn_ref, qr_ref, kn_ref), krp, p)
+        s_ref[p] = dot(k, q, NT)
+    for p in range(2):
+        for qc in range(queries // 256):
+            cols = slice(qc * 256, (qc + 1) * 256)
+            out_ref[pl.ds(2 * step + p, 1), cols] = online_lse(s_ref.at[p], bias, cols)
+
+
+def probs_kernel(lse_ref, krt_ref, qn_ref, qr_ref, kn_ref, out_ref, krp, s_ref):
     step = pl.program_id(0)
     queries, keys = out_ref.shape
 
     @pl.when(step == 0)
     def _():
         fill_rope(krt_ref, krp)
+        out_ref[...] = jnp.zeros_like(out_ref)
+
+    lse = []
+    for p in range(2):
+        s_ref[p] = dot(*pair_operands((qn_ref, qr_ref, kn_ref), krp, p), NT)
+        lse.append(column(lse_ref[pl.ds(2 * step + p, 1), :queries]))
+    for r in range(queries // 32):
+        rows = slice(r * 32, (r + 1) * 32)
+        total = out_ref[rows, :]
         for p in range(2):
-            even[p] = dot(*pair_operands(first, krp, p), NT)
-        out_ref[...] = jnp.zeros_like(out_ref)
-
-    for n, (source, done, made) in enumerate(((odd_in, even, odd), (next_in, odd, even))):
-        at = 4 * step + 2 * n
-        lse = [column(lse_ref[pl.ds(at + p, 1), :queries]) for p in range(2)]
-        for half in range(2):
-            made[half] = dot(*pair_operands(source, krp, half), NT)
-            for r in range(8 * half, 8 * half + 8):
-                rows = slice(r * 32, (r + 1) * 32)
-                total = out_ref[rows, :]
-                for p in range(2):
-                    s = done[p, rows, :] * SCORE_SCALE - lanes_of(lse[p][rows], keys)
-                    total = total + jnp.exp2(s)
-                out_ref[rows, :] = total
+            s = s_ref[p, rows, :] * SCORE_SCALE - lanes_of(lse[p][rows], keys)
+            total = total + jnp.exp2(s)
+        out_ref[rows, :] = total
 
 
 def lg_kernel(lse_ref, logits_ref, target_ref, lg_ref):
@@ -195,7 +181,8 @@
     return jnp.where(r > 0, lg, jnp.zeros_like(lg))
 
 
-def gk_kernel(lg_ref, iq_ref, w_ref, r_ref, gk_ref, gw_out, wb, lgb_ref, gkt_ref, gw_ref):
+def gk_kernel(lg_ref, iq_ref, w_ref, *refs):
+    rs, (gk_ref, gw_out, wb, lgb_ref, gkt_ref, gw_ref) = refs[:PIECES], refs[PIECES:]
     step = pl.program_id(0)
     rows, keys = lg_ref.shape
 
@@ -212,7 +199,7 @@
     totals = [jnp.zeros((rows, 128), F32) for _ in range(GROUP)]
     for kc in range(keys // 256):
         cols = slice(kc * 256, (kc + 1) * 256)
-        r = r_ref[0, :, cols]
+        r = jnp.concatenate([r_ref[0, :, cols] for r_ref in rs], axis=0)
         gkt_ref[:, cols] += dot(wqt, masked_lg(r, lgb_ref[:, cols]), NN)
         lg = lg_ref[:, cols]
         for i in range(GROUP):
@@ -252,7 +239,9 @@
     r_ref[0, 0] = dot(q, ikb_ref[source], NT).astype(BF16)
 
 
-def gq_kernel(lg0, lg1, lg2, lg3, r_ref, ikb_ref, w_ref, gwy_ref, gwc_ref, gq_ref, wb, lgb_ref, g_ref):
+def gq_kernel(lg0, lg1, lg2, lg3, *refs):
+    rs, (ikb_ref, w_ref, *gws) = refs[:PIECES], refs[PIECES : PIECES + 6]
+    gq_ref, wb, lgb_ref, g_ref = refs[PIECES + 6 :]
     part, source = pl.program_id(0), pl.program_id(1)
     rows = lg0.shape[0]
 
@@ -262,7 +251,8 @@
         for i, lg in enumerate((lg0, lg1, lg2, lg3)):
             lgb_ref[i] = lg[...].astype(BF16)
 
-    grown = dot(masked_lg(r_ref[0, 0], lgb_ref[source]), ikb_ref[source], NN)
+    r = jnp.concatenate([r_ref[0, 0] for r_ref in rs], axis=0)
+    grown = dot(masked_lg(r, lgb_ref[source]), ikb_ref[source], NN)
 
     @pl.when(source == 0)
     def _():
@@ -274,7 +264,7 @@
 
     @pl.when(source == 3)
     def _():
-        gw = gwy_ref[...] + gwc_ref[...]
+        gw = (gws[0][...] + gws[1][...]) + (gws[2][...] + gws[3][...])
         dests = group_dests(part)
         for i in range(4):
             pair = []
@@ -309,6 +299,15 @@
 
 def floats(*shapes):
     return [jax.ShapeDtypeStruct(s, F32) for s in shapes]
+
+
+PIECES = 4
+
+
+def piece_specs(shape, index):
+    *lead, rows, width = shape
+    block = (*[1] * len(lead), rows // PIECES, width)
+    return [pl.BlockSpec(block, lambda *at, n=n: (*index(*at), n, 0)) for n in range(PIECES)]
 
 
 def in_vmem():
@@ -328,14 +327,6 @@
     )(*ins)
 
 
-def turns(count):
-    return [lambda i: 0, lambda i: 2 * i + 1, lambda i: jnp.minimum(2 * i + 2, count - 1)]
-
-
-def column_block(rows, width, turn):
-    return pl.BlockSpec((rows, width), lambda i: (0, turn(i)))
-
-
 def run_index(key_blocks, qpos, iq, ik, w):
     rows, keys = iq.shape[0], ik.shape[0]
     groups = IDX_HEADS // GROUP
@@ -344,34 +335,30 @@
     return call(
         index_kernel,
         "index_forward",
-        (groups // 2,),
-        (key_blocks, qpos, iq, iq, iq, ik, w),
+        (groups,),
+        (key_blocks, qpos, iq, ik, w),
         [
             smem(),
             whole(qpos.shape),
-            *[column_block(rows, GROUP * 128, turn) for turn in turns(groups)],
+            pl.BlockSpec((rows, GROUP * 128), lambda i: (0, i)),
             *wholes([ik, w]),
         ],
         [*floats(*shapes), jax.ShapeDtypeStruct(stored, BF16)],
-        [*[whole(s) for s in shapes], pl.BlockSpec((2, *stored[1:]), lambda i: (i, 0, 0))],
+        [*[whole(s) for s in shapes], pl.BlockSpec((1, *stored[1:]), lambda i: (i, 0, 0))],
         [
             pltpu.VMEM((IDX_HEADS, rows, 128), F32),
             pltpu.VMEM((qpos.shape[1], 128), jnp.int32),
             pltpu.VMEM((GROUP * rows, keys), F32),
-            pltpu.VMEM((GROUP * rows, keys), F32),
         ],
     )
 
 
-def main_specs(queries, keys, pairs):
-    specs = []
-    for turn in turns(pairs):
-        specs += [
-            column_block(queries, 256, turn),
-            column_block(queries, 128, turn),
-            column_block(keys, 256, turn),
-        ]
-    return specs
+def main_specs(queries, keys):
+    return [
+        pl.BlockSpec((queries, 256), lambda i: (0, i)),
+        pl.BlockSpec((queries, 128), lambda i: (0, i)),
+        pl.BlockSpec((keys, 256), lambda i: (0, i)),
+    ]
 
 
 def run_stats(key_blocks, qpos, index_row, qn, qr, kn, krt):
@@ -380,15 +367,14 @@
     return call(
         stats_kernel,
         "main_stats",
-        (pairs // 2,),
-        (key_blocks, qpos, index_row, krt, *[qn, qr, kn] * 3),
-        [smem(), *wholes([qpos, index_row, krt]), *main_specs(queries, keys, pairs)],
+        (pairs,),
+        (key_blocks, qpos, index_row, krt, qn, qr, kn),
+        [smem(), *wholes([qpos, index_row, krt]), *main_specs(queries, keys)],
         floats(shape),
         [whole(shape)],
         [
             pltpu.VMEM((keys, queries), F32),
             pltpu.VMEM((2, keys, 128), BF16),
-            pltpu.VMEM((2, keys, queries), F32),
             pltpu.VMEM((2, keys, queries), F32),
         ],
     )[0]
@@ -399,16 +385,12 @@
     return call(
         probs_kernel,
         "main_probs",
-        (pairs // 2,),
-        (lse, krt, *[qn, qr, kn] * 3),
-        [*wholes([lse, krt]), *main_specs(queries, keys, pairs)],
+        (pairs,),
+        (lse, krt, qn, qr, kn),
+        [*wholes([lse, krt]), *main_specs(queries, keys)],
         floats((queries, keys)),
         [whole((queries, keys))],
-        [
-            pltpu.VMEM((2, keys, 128), BF16),
-            pltpu.VMEM((2, queries, keys), F32),
-            pltpu.VMEM((2, queries, keys), F32),
-        ],
+        [pltpu.VMEM((2, keys, 128), BF16), pltpu.VMEM((2, queries, keys), F32)],
     )[0]
 
 
@@ -430,12 +412,12 @@
         gk_kernel,
         "grad_k",
         (IDX_HEADS // GROUP,),
-        (lg, iq, w, r),
+        (lg, iq, w, *[r] * PIECES),
         [
             whole(lg.shape),
             pl.BlockSpec((rows, GROUP * 128), lambda i: (0, i)),
             whole(w.shape),
-            pl.BlockSpec((1, *r.shape[1:]), lambda i: (i, 0, 0)),
+            *piece_specs(r.shape, lambda i: (i,)),
         ],
         floats(*shapes),
         [whole(s) for s in shapes],
@@ -463,18 +445,18 @@
     )
 
 
-def run_gq(lgs, r, ikb, w, gwy, gwc):
+def run_gq(lgs, r, ikb, w, gws):
     rows, keys = lgs[0].shape
     shape = (N_Z, rows + 16, 256)
     return call(
         gq_kernel,
         "grad_q",
         (2, 4),
-        [*lgs, r, ikb, w, gwy, gwc],
+        [*lgs, *[r] * PIECES, ikb, w, *gws],
         [
             *wholes(lgs),
-            pl.BlockSpec((1, 1, *r.shape[2:]), lambda i, j: (i, j, 0, 0)),
-            *wholes([ikb, w, gwy, gwc]),
+            *piece_specs(r.shape, lambda i, j: (i, j)),
+            *wholes([ikb, w, *gws]),
         ],
         floats(shape),
         [pl.BlockSpec((4, *shape[1:]), lambda i, j: (i, 0, 0))],
@@ -538,9 +520,8 @@
     gks, gw = run_gk(lg, iq, w, r)
     lg_y, gw = lax.optimization_barrier((lg_y, gw))
     lg_yc = ctx_xor(lg_y, 1)
-    gw = gw + ctx_xor(gw, 16)
-    parts = run_gq([lg, lg_c, lg_y, lg_yc], r_group, ikb, w, gw, ctx_xor(gw, 1))
-    gks, parts = lax.optimization_barrier((gks, parts))
+    gws = [gw, *[ctx_xor(gw, bits) for bits in (16, 17, 1)]]
+    parts = run_gq([lg, lg_c, lg_y, lg_yc], r_group, ikb, w, gws)
     groups = [[(y * N_Z + z) * 2 + c for z in range(N_Z)] for y in range(2) for c in range(2)]
     parts = lax.all_to_all(parts, "ctx", 0, 0, axis_index_groups=groups)
     gks = lax.all_to_all(gks, "head", 0, 0)

time: 167 us -> 157 us (0.940)
  blocking collectives: 39.1 us -> 24.6 us
  starting transfers between devices: 22.2 us -> 28.9 us
    all_to_all x1 -> x0, blocking collectives: 15.9 us -> none  [per_device(): gks = lax.all_to_all(gks, 'head', 0, 0)]
    all_to_all x0 -> x1, starting transfers between devices: none -> 5.94 us  [per_device(): gks = lax.all_to_all(gks, 'head', 0, 0)]
    ppermute x10 -> x11, starting transfers between devices: 5.06 us -> 5.75 us  [ctx_xor(): return lax.ppermute(value, 'ctx', [(i, i ^ bits) for i in range(N_CTX)])]
    ppermute x10 -> x11, waiting for transfers between devices: 9.69 us -> 9.76 us  [ctx_xor(): return lax.ppermute(value, 'ctx', [(i, i ^ bits) for i in range(N_CTX)])]
  transfers between devices with their start and end apart: 15 -> 17, of which waited for: 11 -> 11; matrix products, arithmetic and copies ran while one was open for 1% -> 0% of each run, Pallas kernels for 25% -> 33%
where the time goes in v2:
time: 157 us; the launch traced here: 154 us
  Pallas kernels  63.7 us (41%)
  waiting for transfers between devices  29.7 us (19%)
  starting transfers between devices  28.9 us (18%)
  blocking collectives  24.6 us (16%)
  local copies, waits for them, and re-layouts  3.66 us (2%)
  other arithmetic  2.56 us (2%)
    pallas_call x6, Pallas kernels, call(): pl.pallas_call(kernel, grid=grid, in_specs=in_specs, out_specs=out_specs,...  61.7 us
    all_to_all x1, blocking collectives, per_device(): parts = lax.all_to_all(parts, 'ctx', 0, 0, axis_index_groups=groups)  24.6 us
    all_to_all x1, waiting for transfers between devices, per_device(): lax.all_to_all(probs.reshape(N_HEAD, -1, probs.shape[1]), 'head', 0, 0)  10.2 us
    ppermute x4, starting transfers between devices, z_shift(): return lax.ppermute(value, 'ctx', list(enumerate(to)))  9.84 us
    ppermute x11, waiting for transfers between devices, ctx_xor(): return lax.ppermute(value, 'ctx', [(i, i ^ bits) for i in range(N_CTX)])  9.76 us
    ppermute x4, waiting for transfers between devices, z_shift(): return lax.ppermute(value, 'ctx', list(enumerate(to)))  9.73 us
    all_to_all x1, starting transfers between devices, per_device(): lax.all_to_all(probs.reshape(N_HEAD, -1, probs.shape[1]), 'head', 0, 0)  7.32 us
    all_to_all x1, starting transfers between devices, per_device(): gks = lax.all_to_all(gks, 'head', 0, 0)  5.94 us
  transfers between devices with their start and end apart: 17, of which 11 were waited for; matrix products, arithmetic and copies ran while one was open for 0% of the time, Pallas kernels for 33%

profile of v2, /device:TPU:2, one launch (start us, length us, event | category | flops | bytes accessed | tf_op | source)
XLA Modules:
  0.0 154.5 jit_solution(2547019003254973220)
XLA Ops:
  0.6 1.0 convert_element_type.3
  1.6 1.7 %collective-permute-start = (f32[1024,128]{1,0:T(8,128)S(1)}, f32[1024,128]{1,0:T(8,128)}, u32[]{:S(2)}, u32[]{:S(2)}) collective-permute-start(f32[1024,128]{1,0:T(8,128)S(1)} %convert_element_type.3), channel_id=1, source_target_pairs={{0,128},{8,136},{16,144},{24,152},{32,160},{40,168},{48,176},{56,1... | collective-permute-start | bytes 1572872 | tf_op jit(solution)/shard_map/ppermute | solution.py:483
  3.9 9.2 %index_forward.1 = (f32[64,1024]{1,0:T(8,128)}, f32[16,128]{1,0:T(8,128)}, bf16[8,512,1024]{2,1,0:T(8,128)(2,1)}) custom-call(s32[1]{0:T(128)S(6)} %copy.12.base_ref, s32[1,512]{1,0:T(1,128)} %bitcast.6, bf16[64,8192]{1,0:T(8,128)(2,1)} %iq_ref.5, bf16[1024,128]{1,0:T(8,128)(2,1)} %refs_0_.1, f32[64,64]{1,0:T(8,128)} %refs_5_.1), custom_call_target="tpu_custom_call" | custom-call | tf_op jit(solution)/shard_map/index_forward/pallas_call | solution.py:318
  13.2 13.3 %main_stats.1 = f32[16,640]{1,0:T(8,128)} custom-call(s32[1]{0:T(128)S(6)} %copy.12.base_ref, s32[1,512]{1,0:T(1,128)} %bitcast.7, f32[16,128]{1,0:T(8,128)} %get-tuple-element.20.row_ref, bf16[64,1024]{1,0:T(8,128)(2,1)} %bitcast.4, bf16[512,2048]{1,0:T(8,128)(2,1)} %qn_ref.3, bf16[512,1024]{1,0:T(8,128)(2,1)} %qr_ref.3, bf16[1024,2048]{1,0:T(8,128)(2,1)} %kn_ref.3), custom_call_target="tpu_custom_call" | custom-call | tf_op jit(solution)/shard_map/main_stats/pallas_call | solution.py:318
  26.4 0.0 collective-permute-done.refs_2_
  26.4 0.0 collective-permute-start.1
  26.5 1.4 collective-permute-done.1
  27.9 0.8 multiply_add_fusion.4
  28.7 0.5 collective-permute-start.2
  29.2 3.6 %collective-permute-done.2 = f32[16,640]{1,0:T(8,128)S(1)} collective-permute-done((f32[16,640]{1,0:T(8,128)S(1)}, f32[16,640]{1,0:T(8,128)S(1)}, u32[]{:S(2)}, u32[]{:S(2)}) %collective-permute-start.2) | collective-permute-done | bytes 40992 | tf_op jit(solution)/shard_map/ppermute | solution.py:483
  32.8 5.9 %collective-permute-start.4 = (f32[16,640]{1,0:T(8,128)S(1)}, f32[16,640]{1,0:T(8,128)S(1)}, u32[]{:S(2)}, u32[]{:S(2)}) collective-permute-start(f32[16,640]{1,0:T(8,128)S(1)} %multiply_add_fusion.3), channel_id=1, source_target_pairs={{0,112},{8,120},{16,0},{24,8},{32,16},{40,24},{48,32},{56,40},{64,... | collective-permute-start | bytes 122888 | tf_op jit(solution)/shard_map/ppermute | solution.py:488
  38.8 1.7 %collective-permute-done.4 = f32[16,640]{1,0:T(8,128)S(1)} collective-permute-done((f32[16,640]{1,0:T(8,128)S(1)}, f32[16,640]{1,0:T(8,128)S(1)}, u32[]{:S(2)}, u32[]{:S(2)}) %collective-permute-start.4) | collective-permute-done | bytes 40992 | tf_op jit(solution)/shard_map/ppermute | solution.py:488
  40.4 3.5 %collective-permute-done.3 = f32[16,640]{1,0:T(8,128)S(1)} collective-permute-done((f32[16,640]{1,0:T(8,128)S(1)}, f32[16,640]{1,0:T(8,128)S(1)}, u32[]{:S(2)}, u32[]{:S(2)}) %collective-permute-start.3) | collective-permute-done | bytes 40992 | tf_op jit(solution)/shard_map/ppermute | solution.py:488
  44.0 0.1 multiply_add_fusion.2
  44.0 0.8 collective-permute-start.6
  44.8 3.1 %collective-permute-start.5 = (f32[16,640]{1,0:T(8,128)S(1)}, f32[16,640]{1,0:T(8,128)S(1)}, u32[]{:S(2)}, u32[]{:S(2)}) collective-permute-start(f32[16,640]{1,0:T(8,128)S(1)} %get-tuple-element.37), channel_id=1, source_target_pairs={{0,48},{8,56},{16,64},{24,72},{32,80},{40,88},{48,96},{56,104},{64... | collective-permute-start | bytes 122888 | tf_op jit(solution)/shard_map/ppermute | solution.py:488
  47.9 2.3 %collective-permute-done.6 = f32[16,640]{1,0:T(8,128)S(1)} collective-permute-done((f32[16,640]{1,0:T(8,128)S(1)}, f32[16,640]{1,0:T(8,128)S(1)}, u32[]{:S(2)}, u32[]{:S(2)}) %collective-permute-start.6) | collective-permute-done | bytes 40992 | tf_op jit(solution)/shard_map/ppermute | solution.py:488
  50.2 2.3 %collective-permute-done.5 = f32[16,640]{1,0:T(8,128)S(1)} collective-permute-done((f32[16,640]{1,0:T(8,128)S(1)}, f32[16,640]{1,0:T(8,128)S(1)}, u32[]{:S(2)}, u32[]{:S(2)}) %collective-permute-start.5) | collective-permute-done | bytes 40992 | tf_op jit(solution)/shard_map/ppermute | solution.py:488
  52.4 0.7 multiply_add_fusion.lse_ref
  53.1 10.7 %main_probs.1 = f32[512,1024]{1,0:T(8,128)} custom-call(f32[16,640]{1,0:T(8,128)} %multiply_add_fusion.lse_ref, bf16[64,1024]{1,0:T(8,128)(2,1)} %bitcast.5, bf16[512,2048]{1,0:T(8,128)(2,1)} %qn_ref.3, bf16[512,1024]{1,0:T(8,128)(2,1)} %qr_ref.3, bf16[1024,2048]{1,0:T(8,128)(2,1)} %kn_ref.3), custom_call_target="tpu_custom_call" | custom-call | tf_op jit(solution)/shard_map/main_probs/pallas_call | solution.py:318
  63.8 7.3 %all-to-all-start = ((f32[8,64,1024]{2,1,0:T(8,128)}), f32[8,64,1024]{2,1,0:T(8,128)S(1)}, u32[]{:S(2)}, u32[]{:S(2)}) async-start(f32[8,64,1024]{2,1,0:T(8,128)} %bitcast.3), calls=%async_computation | async-start | bytes 4194304 | tf_op jit(solution)/shard_map/all_to_all | solution.py:514
  71.2 0.5 collective-permute-start.8
  71.7 0.7 slice.4.lse_ref
  72.4 1.4 collective-permute-done.7.refs_1_
  73.8 0.2 collective-permute-done.8.refs_3_
  74.0 0.5 copy-done.3
  74.6 0.8 copy-done.4
  75.4 8.4 %inner_group.1 = (bf16[2,4,512,1024]{3,2,1,0:T(8,128)(2,1)}, bf16[4,1024,128]{2,1,0:T(8,128)(2,1)}) custom-call(bf16[64,8192]{1,0:T(8,128)(2,1)} %iq_ref.5, bf16[1024,128]{1,0:T(8,128)(2,1)} %refs_0_.1, f32[1024,128]{1,0:T(8,128)} %copy-done.3, f32[1024,128]{1,0:T(8,128)} %collective-permute-done.refs_2_, f32[1024,128]{1,0:T(8,128)} %copy-done.4), custom_call_target="tpu_custom_call" | custom-call | tf_op jit(solution)/shard_map/inner_group/pallas_call | solution.py:318
  83.7 10.2 %all-to-all-done.target_ref = f32[8,64,1024]{2,1,0:T(8,128)S(1)} async-done(((f32[8,64,1024]{2,1,0:T(8,128)}), f32[8,64,1024]{2,1,0:T(8,128)S(1)}, u32[]{:S(2)}, u32[]{:S(2)}) %all-to-all-start) | async-done | bytes 2097184 | tf_op jit(solution)/shard_map/all_to_all | solution.py:514
  93.9 0.1 logit_grad.1.lg_ref.lg0
  94.1 0.4 collective-permute-start.10
  94.5 0.3 copy-done
  94.8 10.1 %grad_k.1 = (f32[8,128,128]{2,1,0:T(8,128)}, f32[16,256]{1,0:T(8,128)}) custom-call(f32[64,1024]{1,0:T(8,128)} %copy-done, bf16[64,8192]{1,0:T(8,128)(2,1)} %iq_ref.5, f32[64,64]{1,0:T(8,128)} %refs_5_.1, bf16[8,512,1024]{2,1,0:T(8,128)(2,1)} %get-tuple-element.30.refs_0_.refs_1_.refs_2_.refs_3_, ...), custom_call_target="tpu_custom_call" | custom-call | tf_op jit(solution)/shard_map/grad_k/pallas_call | solution.py:318
  104.9 5.9 %all-to-all-start.2 = ((f32[8,128,128]{2,1,0:T(8,128)}), f32[8,128,128]{2,1,0:T(8,128)S(1)}, u32[]{:S(2)}, u32[]{:S(2)}) async-start(f32[8,128,128]{2,1,0:T(8,128)} %get-tuple-element.36), calls=%async_computation.2 | async-start | bytes 1048576 | tf_op jit(solution)/shard_map/all_to_all | solution.py:527
  110.9 0.5 collective-permute-start.11
  111.4 0.1 collective-permute-start.14
  111.5 1.2 collective-permute-start.13
  112.7 0.8 collective-permute-start.12
  113.5 0.0 collective-permute-done.9.lg1
  113.5 0.0 collective-permute-done.14.refs_9_
  113.5 2.1 %collective-permute-done.13.refs_8_ = f32[16,256]{1,0:T(8,128)S(1)} collective-permute-done((f32[16,256]{1,0:T(8,128)}, f32[16,256]{1,0:T(8,128)S(1)}, u32[]{:S(2)}, u32[]{:S(2)}) %collective-permute-start.13) | collective-permute-done | bytes 16416 | tf_op jit(solution)/shard_map/ppermute | solution.py:483
  115.7 0.9 collective-permute-done.12.refs_7_
  116.6 0.0 collective-permute-done.11.lg3
  116.7 0.6 copy-done.10
  117.2 0.7 copy-done.7
  117.9 10.0 %grad_q.1 = f32[8,80,256]{2,1,0:T(8,128)} custom-call(f32[64,1024]{1,0:T(8,128)} %copy-done, f32[64,1024]{1,0:T(8,128)} %copy-done.6, f32[64,1024]{1,0:T(8,128)} %copy-done.5, f32[64,1024]{1,0:T(8,128)} %copy-done.7, bf16[2,4,512,1024]{3,2,1,0:T(8,128)(2,1)} %get-tuple-element.33.refs_0_.refs_1_.refs_2_.refs_3_, ...), custom_call_target="tpu_custom_call" | custom-call | tf_op jit(solution)/shard_map/grad_q/pallas_call | solution.py:318
  127.9 24.6 %all_to_all.15.parts_ref = f32[8,80,256]{2,1,0:T(8,128)} all-to-all(f32[8,80,256]{2,1,0:T(8,128)} %grad_q.1), channel_id=1, replica_groups={{0,16,32,48,64,80,96,112},{8,24,40,56,72,88,104,120},{128,144,160,176,1..., dimensions={0} | all-to-all | bytes 1310720 | tf_op jit(solution)/shard_map/all_to_all | solution.py:526
  152.5 1.9 %finish.1 = (f32[64,256]{1,0:T(8,128)}, f32[128,128]{1,0:T(8,128)}, f32[64,64]{1,0:T(8,128)}) custom-call(f32[8,80,256]{2,1,0:T(8,128)} %all_to_all.15.parts_ref, f32[8,128,128]{2,1,0:T(8,128)} %copy-done.2), custom_call_target="tpu_custom_call" | custom-call | tf_op jit(solution)/shard_map/finish/pallas_call | solution.py:473
  (23 shorter events, 0.1 us)
Async XLA Ops:
  1.6 24.8 %collective-permute-start = (f32[1024,128]{1,0:T(8,128)S(1)}, f32[1024,128]{1,0:T(8,128)}, u32[]{:S(2)}, u32[]{:S(2)}) collective-permute-start(f32[1024,128]{1,0:T(8,128)S(1)} %convert_element_type.3), channel_id=1, source_target_pairs={{0,128},{8,136},{16,144},{24,152},{32,160},{40,168},{48,176},{56,1... | collective-permute-start | bytes 1572872 | tf_op jit(solution)/shard_map/ppermute | solution.py:483
  26.4 1.4 collective-permute-start.1
  28.7 4.1 %collective-permute-start.2 = (f32[16,640]{1,0:T(8,128)S(1)}, f32[16,640]{1,0:T(8,128)S(1)}, u32[]{:S(2)}, u32[]{:S(2)}) collective-permute-start(f32[16,640]{1,0:T(8,128)S(1)} %multiply_add_fusion.4), channel_id=1, source_target_pairs={{0,128},{8,136},{16,144},{24,152},{32,160},{40,168},{48,176},{56,1... | collective-permute-start | bytes 122888 | tf_op jit(solution)/shard_map/ppermute | solution.py:483
  32.8 7.6 %collective-permute-start.4 = (f32[16,640]{1,0:T(8,128)S(1)}, f32[16,640]{1,0:T(8,128)S(1)}, u32[]{:S(2)}, u32[]{:S(2)}) collective-permute-start(f32[16,640]{1,0:T(8,128)S(1)} %multiply_add_fusion.3), channel_id=1, source_target_pairs={{0,112},{8,120},{16,0},{24,8},{32,16},{40,24},{48,32},{56,40},{64,... | collective-permute-start | bytes 122888 | tf_op jit(solution)/shard_map/ppermute | solution.py:488
  38.8 5.2 %collective-permute-start.3 = (f32[16,640]{1,0:T(8,128)S(1)}, f32[16,640]{1,0:T(8,128)S(1)}, u32[]{:S(2)}, u32[]{:S(2)}) collective-permute-start(f32[16,640]{1,0:T(8,128)S(1)} %multiply_add_fusion.3), channel_id=1, source_target_pairs={{0,16},{8,24},{16,32},{24,40},{32,48},{40,56},{48,64},{56,72},{64,... | collective-permute-start | bytes 122888 | tf_op jit(solution)/shard_map/ppermute | solution.py:488
  44.0 6.2 %collective-permute-start.6 = (f32[16,640]{1,0:T(8,128)S(1)}, f32[16,640]{1,0:T(8,128)S(1)}, u32[]{:S(2)}, u32[]{:S(2)}) collective-permute-start(f32[16,640]{1,0:T(8,128)S(1)} %get-tuple-element.38), channel_id=1, source_target_pairs={{0,80},{8,88},{16,96},{24,104},{32,112},{40,120},{48,0},{56,8},{64... | collective-permute-start | bytes 122888 | tf_op jit(solution)/shard_map/ppermute | solution.py:488
  44.8 7.7 %collective-permute-start.5 = (f32[16,640]{1,0:T(8,128)S(1)}, f32[16,640]{1,0:T(8,128)S(1)}, u32[]{:S(2)}, u32[]{:S(2)}) collective-permute-start(f32[16,640]{1,0:T(8,128)S(1)} %get-tuple-element.37), channel_id=1, source_target_pairs={{0,48},{8,56},{16,64},{24,72},{32,80},{40,88},{48,96},{56,104},{64... | collective-permute-start | bytes 122888 | tf_op jit(solution)/shard_map/ppermute | solution.py:488
  63.8 30.1 %copy-start.1 = (f32[64,1024]{1,0:T(8,128)S(1)}, f32[64,1024]{1,0:T(8,128)}, u32[]{:S(2)}) copy-start(f32[64,1024]{1,0:T(8,128)} %get-tuple-element.22.logits_ref) | copy-start | bytes 786436
  63.8 30.1 %all-to-all-start = ((f32[8,64,1024]{2,1,0:T(8,128)}), f32[8,64,1024]{2,1,0:T(8,128)S(1)}, u32[]{:S(2)}, u32[]{:S(2)}) async-start(f32[8,64,1024]{2,1,0:T(8,128)} %bitcast.3), calls=%async_computation | async-start | bytes 4194304 | tf_op jit(solution)/shard_map/all_to_all | solution.py:514
  71.2 2.6 %collective-permute-start.7 = (f32[1024,128]{1,0:T(8,128)S(1)}, f32[1024,128]{1,0:T(8,128)S(1)}, u32[]{:S(2)}, u32[]{:S(2)}) collective-permute-start(f32[1024,128]{1,0:T(8,128)S(1)} %convert_element_type.3), channel_id=1, source_target_pairs={{0,8},{8,0},{16,24},{24,16},{32,40},{40,32},{48,56},{56,48},{64,72... | collective-permute-start | bytes 1572872 | tf_op jit(solution)/shard_map/ppermute | solution.py:483
  71.2 2.9 %collective-permute-start.8 = (f32[1024,128]{1,0:T(8,128)}, f32[1024,128]{1,0:T(8,128)S(1)}, u32[]{:S(2)}, u32[]{:S(2)}) collective-permute-start(f32[1024,128]{1,0:T(8,128)} %collective-permute-done.refs_2_), channel_id=1, source_target_pairs={{0,8},{8,0},{16,24},{24,16},{32,40},{40,32},{48,56},{56,48},{64,72... | collective-permute-start | bytes 1572872 | tf_op jit(solution)/shard_map/ppermute | solution.py:483
  73.8 0.8 copy-start.3
  74.6 0.8 copy-start.4
  94.1 0.7 copy-start
  94.1 16.8 %collective-permute-start.10 = (f32[64,1024]{1,0:T(8,128)S(1)}, f32[64,1024]{1,0:T(8,128)S(1)}, u32[]{:S(2)}, u32[]{:S(2)}) collective-permute-start(f32[64,1024]{1,0:T(8,128)S(1)} %logit_grad.1.lg_ref.lg0), channel_id=1, source_target_pairs={{0,128},{8,136},{16,144},{24,152},{32,160},{40,168},{48,176},{56,1... | collective-permute-start | bytes 786440 | tf_op jit(solution)/shard_map/ppermute | solution.py:483
  104.9 23.0 %all-to-all-start.2 = ((f32[8,128,128]{2,1,0:T(8,128)}), f32[8,128,128]{2,1,0:T(8,128)S(1)}, u32[]{:S(2)}, u32[]{:S(2)}) async-start(f32[8,128,128]{2,1,0:T(8,128)} %get-tuple-element.36), calls=%async_computation.2 | async-start | bytes 1048576 | tf_op jit(solution)/shard_map/all_to_all | solution.py:527
  110.8 2.7 %collective-permute-start.9 = (f32[64,1024]{1,0:T(8,128)}, f32[64,1024]{1,0:T(8,128)S(1)}, u32[]{:S(2)}, u32[]{:S(2)}) collective-permute-start(f32[64,1024]{1,0:T(8,128)} %copy-done), channel_id=1, source_target_pairs={{0,8},{8,0},{16,24},{24,16},{32,40},{40,32},{48,56},{56,48},{64,72... | collective-permute-start | bytes 786440 | tf_op jit(solution)/shard_map/ppermute | solution.py:483
  110.8 5.8 %copy-start.5 = (f32[64,1024]{1,0:T(8,128)}, f32[64,1024]{1,0:T(8,128)S(1)}, u32[]{:S(2)}) copy-start(f32[64,1024]{1,0:T(8,128)S(1)} %collective-permute-done.10.lg2) | copy-start | bytes 786436
  110.9 5.8 %collective-permute-start.11 = (f32[64,1024]{1,0:T(8,128)S(1)}, f32[64,1024]{1,0:T(8,128)S(1)}, u32[]{:S(2)}, u32[]{:S(2)}) collective-permute-start(f32[64,1024]{1,0:T(8,128)S(1)} %collective-permute-done.10.lg2), channel_id=1, source_target_pairs={{0,8},{8,0},{16,24},{24,16},{32,40},{40,32},{48,56},{56,48},{64,72... | collective-permute-start | bytes 786440 | tf_op jit(solution)/shard_map/ppermute | solution.py:483
  111.4 2.2 %collective-permute-start.14 = (f32[16,256]{1,0:T(8,128)}, f32[16,256]{1,0:T(8,128)S(1)}, u32[]{:S(2)}, u32[]{:S(2)}) collective-permute-start(f32[16,256]{1,0:T(8,128)} %get-tuple-element.35.refs_6_), channel_id=1, source_target_pairs={{0,8},{8,0},{16,24},{24,16},{32,40},{40,32},{48,56},{56,48},{64,72... | collective-permute-start | bytes 49160 | tf_op jit(solution)/shard_map/ppermute | solution.py:483
  111.5 4.2 %collective-permute-start.13 = (f32[16,256]{1,0:T(8,128)}, f32[16,256]{1,0:T(8,128)S(1)}, u32[]{:S(2)}, u32[]{:S(2)}) collective-permute-start(f32[16,256]{1,0:T(8,128)} %get-tuple-element.35.refs_6_), channel_id=1, source_target_pairs={{0,136},{8,128},{16,152},{24,144},{32,168},{40,160},{48,184},{56,1... | collective-permute-start | bytes 49160 | tf_op jit(solution)/shard_map/ppermute | solution.py:483
  112.7 3.9 %collective-permute-start.12 = (f32[16,256]{1,0:T(8,128)}, f32[16,256]{1,0:T(8,128)S(1)}, u32[]{:S(2)}, u32[]{:S(2)}) collective-permute-start(f32[16,256]{1,0:T(8,128)} %get-tuple-element.35.refs_6_), channel_id=1, source_target_pairs={{0,128},{8,136},{16,144},{24,152},{32,160},{40,168},{48,176},{56,1... | collective-permute-start | bytes 49160 | tf_op jit(solution)/shard_map/ppermute | solution.py:483
  113.5 3.1 %copy-start.6 = (f32[64,1024]{1,0:T(8,128)}, f32[64,1024]{1,0:T(8,128)S(1)}, u32[]{:S(2)}) copy-start(f32[64,1024]{1,0:T(8,128)S(1)} %collective-permute-done.9.lg1) | copy-start | bytes 786436
  113.5 3.1 %copy-start.8 = (f32[16,256]{1,0:T(8,128)}, f32[16,256]{1,0:T(8,128)S(1)}, u32[]{:S(2)}) copy-start(f32[16,256]{1,0:T(8,128)S(1)} %collective-permute-done.14.refs_9_) | copy-start | bytes 49156
  115.7 1.0 copy-start.9
  116.6 0.6 copy-start.10
  117.2 0.7 copy-start.7
  127.9 24.6 %copy-start.2 = (f32[8,128,128]{2,1,0:T(8,128)}, f32[8,128,128]{2,1,0:T(8,128)S(1)}, u32[]{:S(2)}) copy-start(f32[8,128,128]{2,1,0:T(8,128)S(1)} %all-to-all-done.2.gks_ref) | copy-start | bytes 1572868

commit v3 on v2

--- a/solution.py
+++ b/solution.py
@@ -60,35 +60,36 @@
     return jnp.concatenate([block[:, i * 128 : (i + 1) * 128] for i in range(count)], axis=0)
 
 
-def index_kernel(
-    base_ref, qpos_ref, iq_ref, ik_ref, w_ref, logits_ref, row_ref, r_ref, wb, qcol, s_ref
-):
+def index_kernel(base_ref, qpos_ref, iq_ref, ik_ref, w_ref, logits_ref, row_ref, wp, qcol, s_ref, acc):
     step = pl.program_id(0)
     rows, keys = logits_ref.shape
 
     @pl.when(step == 0)
     def _():
-        fill_weights(w_ref, wb)
-        logits_ref[...] = jnp.zeros_like(logits_ref)
+        wt = w_ref[...].T
+        for i in range(IDX_HEADS // 2):
+            pair = [wt[2 * i : 2 * i + 1], wt[2 * i + 1 : 2 * i + 2]]
+            wp[i : i + 1, :] = jnp.concatenate(pair, axis=1)
+        acc[...] = jnp.zeros_like(acc)
         qcol[...] = column(qpos_ref[...])
 
-    s_ref[...] = dot(stacked(iq_ref[...]), ik_ref[...], NT)
-    for kc in range(keys // 128):
-        cols = slice(kc * 128, (kc + 1) * 128)
-        total = logits_ref[:, cols]
-        for i in range(GROUP):
-            mine = slice(i * rows, (i + 1) * rows)
-            inner = s_ref[mine, cols]
-            r_ref[0, mine, cols] = inner.astype(BF16)
-            total = total + jnp.maximum(inner, 0.0) * wb[step * GROUP + i]
-        logits_ref[:, cols] = total
+    s_ref[...] = dot(ik_ref[...], stacked(iq_ref[...]), NT)
+    weights = [wp[pl.ds(step * GROUP // 2 + i, 1), :] for i in range(GROUP // 2)]
+    for r in range(keys // 64):
+        at = slice(r * 64, (r + 1) * 64)
+        total = acc[at, :]
+        for i, weight in enumerate(weights):
+            total = total + jnp.maximum(s_ref[at, i * 128 : (i + 1) * 128], 0.0) * weight
+        acc[at, :] = total
 
     @pl.when(step == pl.num_programs(0) - 1)
     def _():
+        turned = acc[...].T
         key = lax.broadcasted_iota(jnp.int32, (rows, keys), 1) + base_ref[0] * keys
         start = pl.multiple_of(lax.axis_index("head") * rows, rows)
         limit = lanes_of(qcol[pl.ds(start, rows), :], keys)
-        logits = jnp.where(key <= limit, logits_ref[...] * (INV_ROOT * LOG2E), NEG)
+        logits = (turned[:rows] + turned[rows:]) * (INV_ROOT * LOG2E)
+        logits = jnp.where(key <= limit, logits, NEG)
         logits_ref[...] = logits
         top = jnp.max(logits, axis=1, keepdims=True)
         total = jnp.sum(jnp.exp2(logits - top), axis=1, keepdims=True)
@@ -165,7 +166,7 @@
 
 def lg_kernel(lse_ref, logits_ref, target_ref, lg_ref):
     rows, width = lg_ref.shape
-    lse = column(lse_ref[:1, :])[:rows]
+    lse = column(lse_ref[:1, lse_ref.shape[1] - 128 :])[:rows]
     for c in range(width // 128):
         cols = slice(c * 128, (c + 1) * 128)
         target = target_ref[0, :, cols]
@@ -176,97 +177,79 @@
         lg_ref[:, cols] = jnp.where(logits > 0.5 * NEG, lg, 0.0)
 
 
-def masked_lg(r, lg):
-    lg = jnp.concatenate([lg] * (r.shape[0] // lg.shape[0]), axis=0)
-    return jnp.where(r > 0, lg, jnp.zeros_like(lg))
-
-
-def gk_kernel(lg_ref, iq_ref, w_ref, *refs):
-    rs, (gk_ref, gw_out, wb, lgb_ref, gkt_ref, gw_ref) = refs[:PIECES], refs[PIECES:]
+def gk_kernel(
+    lg_ref, iq_ref, ik_ref, w_ref, keep_ref, send_ref, gw_out, wb, lgt_ref, m_ref, gk_ref, gwt_ref
+):
     step = pl.program_id(0)
     rows, keys = lg_ref.shape
+    width = GROUP * rows
 
     @pl.when(step == 0)
     def _():
         fill_weights(w_ref, wb)
-        lgb_ref[...] = lg_ref[...].astype(BF16)
-        gkt_ref[...] = jnp.zeros_like(gkt_ref)
-        gw_ref[...] = jnp.zeros_like(gw_ref)
+        lgt_ref[...] = jnp.concatenate([lg_ref[...]] * (128 // rows), axis=0).T
+        gk_ref[...] = jnp.zeros_like(gk_ref)
 
     q = stacked(iq_ref[...])
     w = jnp.concatenate([wb[step * GROUP + i] for i in range(GROUP)], axis=0)
-    wqt = (q.astype(F32) * w).astype(BF16).T
-    totals = [jnp.zeros((rows, 128), F32) for _ in range(GROUP)]
-    for kc in range(keys // 256):
-        cols = slice(kc * 256, (kc + 1) * 256)
-        r = jnp.concatenate([r_ref[0, :, cols] for r_ref in rs], axis=0)
-        gkt_ref[:, cols] += dot(wqt, masked_lg(r, lgb_ref[:, cols]), NN)
-        lg = lg_ref[:, cols]
-        for i in range(GROUP):
-            active = jnp.maximum(r[i * rows : (i + 1) * rows].astype(F32), 0.0) * lg
-            totals[i] = totals[i] + active[:, :128] + active[:, 128:]
-    lane = lax.broadcasted_iota(jnp.int32, (rows, IDX_HEADS), 1)
-    new = gw_ref[...]
+    wq = (q.astype(F32) * w).astype(BF16)
+    gw = jnp.zeros((8, width), F32)
+    for c in range(2):
+        inner = dot(ik_ref[c * 512 : (c + 1) * 512, :], q, NT)
+        for r in range(16):
+            at = slice(c * 512 + r * 32, c * 512 + (r + 1) * 32)
+            part = inner[r * 32 : (r + 1) * 32]
+            masked = jnp.where(part > 0.0, lanes_of(lgt_ref[at, :], width), 0.0)
+            m_ref[at, :] = masked.astype(BF16)
+            gw = gw + jnp.sum((part * masked).reshape(4, 8, width), axis=0)
+        at = slice(c * 512, (c + 1) * 512)
+        gk_ref[at, :] += dot(m_ref[at, :], wq, NN)
+    gw = jnp.sum(gw, axis=0, keepdims=True) * INV_ROOT
     for i in range(GROUP):
-        value = jnp.sum(totals[i], axis=1, keepdims=True) * INV_ROOT
-        new = jnp.where(lane == step * GROUP + i, value, new)
-    gw_ref[...] = new
+        gwt_ref[pl.ds(step * GROUP + i, 1), :] = gw[:, i * rows : (i + 1) * rows]
 
     @pl.when(step == pl.num_programs(0) - 1)
     def _():
-        for c in range(keys // 128):
-            gk_ref[c] = gkt_ref[:, c * 128 : (c + 1) * 128].T * INV_ROOT
-        gw_out[...] = jnp.concatenate([gw_ref[i * 16 : (i + 1) * 16, :] for i in range(4)], axis=1)
-
-
-def group_dests(part):
+        me = lax.axis_index("head")
+        size = keys // N_HEAD
+        for out, slots in ((keep_ref, (0, 1, 6, 7)), (send_ref, (2, 3, 4, 5))):
+            for n, m in enumerate(slots):
+                start = pl.multiple_of((me ^ m) * size, size)
+                out[n] = gk_ref[pl.ds(start, size), :] * INV_ROOT
+        gw_out[...] = jnp.concatenate([gwt_ref[i * 16 : (i + 1) * 16] for i in range(4)], axis=1)
+
+
+def gq_kernel(*refs):
+    lgs, iks, (iq_ref, w_ref), gws = refs[:4], refs[4:8], refs[8:10], refs[10:14]
+    gq_ref, wb, lg_ref, ikb_ref, q_ref, g_ref = refs[14:]
+    source = pl.program_id(0)
+    rows, keys = lgs[0].shape
+    count = q_ref.shape[0] // rows
     y_lo, _, core = ctx_place()
-    return [(y_lo * N_Z + part * 4 + i) * 2 + core for i in range(4)]
-
-
-def inner_kernel(iq_ref, *refs):
-    iks, (r_ref, ikb_ref) = refs[:4], refs[4:]
-    part, source = pl.program_id(0), pl.program_id(1)
-
-    @pl.when((part == 0) & (source == 0))
-    def _():
+    dests = [(y_lo * N_Z + i) * 2 + core for i in range(N_Z)]
+
+    @pl.when(source == 0)
+    def _():
+        fill_weights(w_ref, wb)
+        g_ref[...] = jnp.zeros_like(g_ref)
         for i in range(4):
+            lg_ref[i] = lgs[i][...]
             ikb_ref[i] = iks[i][...].astype(BF16)
-
-    dests = group_dests(part)
-    blocks = [iq_ref[:, pl.ds(pl.multiple_of(c * 256, 256), 256)] for c in dests]
-    q = jnp.concatenate([stacked(block) for block in blocks], axis=0)
-    r_ref[0, 0] = dot(q, ikb_ref[source], NT).astype(BF16)
-
-
-def gq_kernel(lg0, lg1, lg2, lg3, *refs):
-    rs, (ikb_ref, w_ref, *gws) = refs[:PIECES], refs[PIECES : PIECES + 6]
-    gq_ref, wb, lgb_ref, g_ref = refs[PIECES + 6 :]
-    part, source = pl.program_id(0), pl.program_id(1)
-    rows = lg0.shape[0]
-
-    @pl.when((part == 0) & (source == 0))
-    def _():
-        fill_weights(w_ref, wb)
-        for i, lg in enumerate((lg0, lg1, lg2, lg3)):
-            lgb_ref[i] = lg[...].astype(BF16)
-
-    r = jnp.concatenate([r_ref[0, 0] for r_ref in rs], axis=0)
-    grown = dot(masked_lg(r, lgb_ref[source]), ikb_ref[source], NN)
-
-    @pl.when(source == 0)
-    def _():
-        g_ref[...] = grown
-
-    @pl.when(source > 0)
-    def _():
-        g_ref[...] += grown
+        for i in range(N_Z):
+            block = iq_ref[:, pl.ds(pl.multiple_of(dests[i] * 256, 256), 256)]
+            q_ref[2 * i * rows : 2 * (i + 1) * rows, :] = stacked(block)
+
+    for c in range(4):
+        cols = slice(c * 256, (c + 1) * 256)
+        k = ikb_ref[source, cols, :]
+        inner = dot(q_ref[...], k, NT)
+        lg = jnp.concatenate([lg_ref[source, :, cols]] * count, axis=0)
+        g_ref[...] += dot(jnp.where(inner > 0.0, lg, 0.0).astype(BF16), k, NN)
 
     @pl.when(source == 3)
     def _():
         gw = (gws[0][...] + gws[1][...]) + (gws[2][...] + gws[3][...])
-        dests = group_dests(part)
-        for i in range(4):
+        for i in range(N_Z):
             pair = []
             for n in range(2):
                 at = (2 * i + n) * rows
@@ -275,14 +258,14 @@
             gq_ref[i, rows:, :] = gw
 
 
-def finish_kernel(parts_ref, gks_ref, gq_ref, gk_ref, gw_ref):
-    total, keys = parts_ref[0], gks_ref[0]
-    for i in range(1, 8):
+def finish_kernel(parts_ref, mine_ref, got_ref, gq_ref, gk_ref, gw_ref):
+    total = parts_ref[0]
+    for i in range(1, N_Z):
         total = total + parts_ref[i]
-        keys = keys + gks_ref[i]
     gq_ref[...] = total[:64]
-    gk_ref[...] = keys
-    gw_ref[...] = jnp.concatenate([total[64:, i * 64 : (i + 1) * 64] for i in range(4)], axis=0)
+    gk_ref[...] = mine_ref[...] + got_ref[...]
+    gwt = jnp.concatenate([total[64:, i * 64 : (i + 1) * 64] for i in range(4)], axis=0)
+    gw_ref[...] = gwt.T
 
 
 def smem():
@@ -299,15 +282,6 @@
 
 def floats(*shapes):
     return [jax.ShapeDtypeStruct(s, F32) for s in shapes]
-
-
-PIECES = 4
-
-
-def piece_specs(shape, index):
-    *lead, rows, width = shape
-    block = (*[1] * len(lead), rows // PIECES, width)
-    return [pl.BlockSpec(block, lambda *at, n=n: (*index(*at), n, 0)) for n in range(PIECES)]
 
 
 def in_vmem():
@@ -331,7 +305,6 @@
     rows, keys = iq.shape[0], ik.shape[0]
     groups = IDX_HEADS // GROUP
     shapes = [(rows, keys), (16, 128)]
-    stored = (groups, GROUP * rows, keys)
     return call(
         index_kernel,
         "index_forward",
@@ -343,12 +316,13 @@
             pl.BlockSpec((rows, GROUP * 128), lambda i: (0, i)),
             *wholes([ik, w]),
         ],
-        [*floats(*shapes), jax.ShapeDtypeStruct(stored, BF16)],
-        [*[whole(s) for s in shapes], pl.BlockSpec((1, *stored[1:]), lambda i: (i, 0, 0))],
+        floats(*shapes),
+        [whole(s) for s in shapes],
         [
-            pltpu.VMEM((IDX_HEADS, rows, 128), F32),
+            pltpu.VMEM((IDX_HEADS // 2, 128), F32),
             pltpu.VMEM((qpos.shape[1], 128), jnp.int32),
-            pltpu.VMEM((GROUP * rows, keys), F32),
+            pltpu.VMEM((keys, GROUP * rows), F32),
+            pltpu.VMEM((keys, 128), F32),
         ],
     )
 
@@ -391,6 +365,7 @@
         floats((queries, keys)),
         [whole((queries, keys))],
         [pltpu.VMEM((2, keys, 128), BF16), pltpu.VMEM((2, queries, keys), F32)],
+        24,
     )[0]
 
 
@@ -405,78 +380,69 @@
     )(lse, logits, target)
 
 
-def run_gk(lg, iq, w, r):
+def run_gk(lg, iq, ik, w):
     rows, keys = lg.shape
-    shapes = [(keys // 128, 128, IDX_DIM), (16, 256)]
+    size = keys // N_HEAD
+    shapes = [(4, size, IDX_DIM), (4, size, IDX_DIM), (16, 256)]
     return call(
         gk_kernel,
         "grad_k",
         (IDX_HEADS // GROUP,),
-        (lg, iq, w, *[r] * PIECES),
+        (lg, iq, ik, w),
         [
             whole(lg.shape),
             pl.BlockSpec((rows, GROUP * 128), lambda i: (0, i)),
-            whole(w.shape),
-            *piece_specs(r.shape, lambda i: (i,)),
+            *wholes([ik, w]),
         ],
         floats(*shapes),
         [whole(s) for s in shapes],
         [
             pltpu.VMEM((IDX_HEADS, rows, 128), F32),
-            pltpu.VMEM((rows, keys), BF16),
-            pltpu.VMEM((IDX_DIM, keys), F32),
-            pltpu.VMEM((rows, IDX_HEADS), F32),
+            pltpu.VMEM((keys, 128), F32),
+            pltpu.VMEM((keys, GROUP * rows), BF16),
+            pltpu.VMEM((keys, IDX_DIM), F32),
+            pltpu.VMEM((IDX_HEADS, rows), F32),
         ],
+        20,
     )
 
 
-def run_inner(iq, iks):
-    rows, keys = iq.shape[0], iks[0].shape[0]
-    stored, kept = (2, 4, 8 * rows, keys), (4, keys, IDX_DIM)
-    return call(
-        inner_kernel,
-        "inner_group",
-        (2, 4),
-        [iq, *iks],
-        wholes([iq, *iks]),
-        [jax.ShapeDtypeStruct(stored, BF16), jax.ShapeDtypeStruct(kept, BF16)],
-        [pl.BlockSpec((1, 1, *stored[2:]), lambda i, j: (i, j, 0, 0)), whole(kept)],
-        [],
-    )
-
-
-def run_gq(lgs, r, ikb, w, gws):
+def run_gq(lgs, iks, iq, w, gws):
     rows, keys = lgs[0].shape
     shape = (N_Z, rows + 16, 256)
+    ins = [*lgs, *iks, iq, w, *gws]
     return call(
         gq_kernel,
         "grad_q",
-        (2, 4),
-        [*lgs, *[r] * PIECES, ikb, w, *gws],
-        [
-            *wholes(lgs),
-            *piece_specs(r.shape, lambda i, j: (i, j)),
-            *wholes([ikb, w, *gws]),
-        ],
+        (4,),
+        ins,
+        wholes(ins),
         floats(shape),
-        [pl.BlockSpec((4, *shape[1:]), lambda i, j: (i, 0, 0))],
+        [whole(shape)],
         [
             pltpu.VMEM((IDX_HEADS, rows, 128), F32),
-            pltpu.VMEM((4, rows, keys), BF16),
-            pltpu.VMEM((8 * rows, IDX_DIM), F32),
+            pltpu.VMEM((4, rows, keys), F32),
+            pltpu.VMEM((4, keys, IDX_DIM), BF16),
+            pltpu.VMEM((2 * N_Z * rows, IDX_DIM), BF16),
+            pltpu.VMEM((2 * N_Z * rows, IDX_DIM), F32),
         ],
+        28,
     )[0]
 
 
-def run_finish(parts, gks):
+def run_finish(*ins):
     shapes = [(64, 256), (128, 128), (64, 64)]
     return pl.pallas_call(
         finish_kernel,
-        in_specs=[in_vmem()] * 2,
+        in_specs=[in_vmem()] * 3,
         out_specs=[in_vmem()] * 3,
         out_shape=floats(*shapes),
         name="finish",
-    )(parts, gks)
+    )(*ins)
+
+
+def head_xor(value, bits):
+    return lax.ppermute(value, "head", [(i, i ^ bits) for i in range(N_HEAD)])
 
 
 def ctx_xor(value, bits):
@@ -501,7 +467,7 @@
     krt = kr.T
     ikf = ik.astype(F32)
     ikf_y = ctx_xor(ikf, 16)
-    logits, index_row, r = run_index(key_blocks, qpos, iq, ik, w)
+    logits, index_row = run_index(key_blocks, qpos, iq, ik, w)
     lse = run_stats(key_blocks, qpos, index_row, qn, qr, kn, krt)
     lse, ikf_y = lax.optimization_barrier((lse, ikf_y))
     lse = merged(lse, ctx_xor(lse, 1))
@@ -512,20 +478,23 @@
     probs = run_probs(lse, qn, qr, kn, krt)
     probs, ikf, ikf_y = lax.optimization_barrier((probs, ikf, ikf_y))
     target = lax.all_to_all(probs.reshape(N_HEAD, -1, probs.shape[1]), "head", 0, 0)
-    r_group, ikb = run_inner(iq, [ik, ctx_xor(ikf, 1), ikf_y, ctx_xor(ikf_y, 1)])
-
-    target, r_group, ikb = lax.optimization_barrier((target, r_group, ikb))
-    lg = run_lg(lse[:8, qn.shape[0] :], logits, target)
+    ikf_c, ikf_yc = ctx_xor(ikf, 1), ctx_xor(ikf_y, 1)
+    target, ikf_c, ikf_yc = lax.optimization_barrier((target, ikf_c, ikf_yc))
+
+    lg = run_lg(lse, logits, target)
     lg_y, lg_c = ctx_xor(lg, 16), ctx_xor(lg, 1)
-    gks, gw = run_gk(lg, iq, w, r)
-    lg_y, gw = lax.optimization_barrier((lg_y, gw))
+    keep, send, gw = run_gk(lg, iq, ik, w)
+    lg_y, lg_c, send, gw = lax.optimization_barrier((lg_y, lg_c, send, gw))
     lg_yc = ctx_xor(lg_y, 1)
     gws = [gw, *[ctx_xor(gw, bits) for bits in (16, 17, 1)]]
-    parts = run_gq([lg, lg_c, lg_y, lg_yc], r_group, ikb, w, gws)
+    got = head_xor(send, 2)
+    parts = run_gq([lg, lg_c, lg_y, lg_yc], [ik, ikf_c, ikf_y, ikf_yc], iq, w, gws)
+    got, parts = lax.optimization_barrier((got, parts))
+    got = head_xor(keep[2:] + got[2:], 6) + (keep[:2] + got[:2])
+    got, mine = head_xor(got[1], 1), got[0]
     groups = [[(y * N_Z + z) * 2 + c for z in range(N_Z)] for y in range(2) for c in range(2)]
     parts = lax.all_to_all(parts, "ctx", 0, 0, axis_index_groups=groups)
-    gks = lax.all_to_all(gks, "head", 0, 0)
-    return run_finish(parts, gks)
+    return run_finish(parts, mine, got)
 
 
 def solution(mesh):

time: 157 us -> 143 us (0.911)
  waiting for transfers between devices: 29.7 us -> 56.2 us
  blocking collectives: 24.6 us -> 0 us
  Pallas kernels: 63.7 us -> 45.6 us
  local copies, waits for them, and re-layouts: 3.66 us -> 5.44 us
    all_to_all x1 -> x0, blocking collectives: 24.6 us -> none  [per_device(): parts = lax.all_to_all(parts, 'ctx', 0, 0, axis_index_groups=groups)]
    pallas_call x6 -> x5, Pallas kernels: 61.7 us -> 43.5 us  [call(): pl.pallas_call(kernel, grid=grid, in_specs=in_specs, out_specs=out_specs,...]
    ppermute x0 -> x3, waiting for transfers between devices: none -> 8.94 us  [head_xor(): return lax.ppermute(value, 'head', [(i, i ^ bits) for i in range(N_HEAD)])]
    all_to_all x1, waiting for transfers between devices: 10.2 us -> 18.9 us  [per_device(): lax.all_to_all(probs.reshape(N_HEAD, -1, probs.shape[1]), 'head', 0, 0)]
    all_to_all x1, waiting for transfers between devices: 0.01 us -> 8.26 us  [per_device(): parts = lax.all_to_all(parts, 'ctx', 0, 0, axis_index_groups=groups)]
    ppermute x0 -> x3, starting transfers between devices: none -> 4.01 us  [head_xor(): return lax.ppermute(value, 'head', [(i, i ^ bits) for i in range(N_HEAD)])]
    all_to_all x1, starting transfers between devices: 5.94 us -> 3.95 us  [per_device(): parts = lax.all_to_all(parts, 'ctx', 0, 0, axis_index_groups=groups)]
    unnamed x22 -> x34, local copies, waits for them, and re-layouts: 2.98 us -> 4.8 us
  transfers between devices with their start and end apart: 17 -> 20, of which waited for: 11 -> 14; matrix products, arithmetic and copies ran while one was open for 0% -> 0% of each run, Pallas kernels for 33% -> 25%
where the time goes in v3:
time: 143 us; the launch traced here: 142 us
  waiting for transfers between devices  56.2 us (39%)
  Pallas kernels  45.6 us (32%)
  starting transfers between devices  30.4 us (21%)
  local copies, waits for them, and re-layouts  5.44 us (4%)
  other arithmetic  2.79 us (2%)
  between operations  1.47 us (1%)
    pallas_call x5, Pallas kernels, call(): pl.pallas_call(kernel, grid=grid, in_specs=in_specs, out_specs=out_specs,...  43.5 us
    all_to_all x1, waiting for transfers between devices, per_device(): lax.all_to_all(probs.reshape(N_HEAD, -1, probs.shape[1]), 'head', 0, 0)  18.9 us
    ppermute x11, waiting for transfers between devices, ctx_xor(): return lax.ppermute(value, 'ctx', [(i, i ^ bits) for i in range(N_CTX)])  10.4 us
    ppermute x4, starting transfers between devices, z_shift(): return lax.ppermute(value, 'ctx', list(enumerate(to)))  9.83 us
    ppermute x4, waiting for transfers between devices, z_shift(): return lax.ppermute(value, 'ctx', list(enumerate(to)))  9.73 us
    ppermute x3, waiting for transfers between devices, head_xor(): return lax.ppermute(value, 'head', [(i, i ^ bits) for i in range(N_HEAD)])  8.94 us
    all_to_all x1, waiting for transfers between devices, per_device(): parts = lax.all_to_all(parts, 'ctx', 0, 0, axis_index_groups=groups)  8.26 us
    all_to_all x1, starting transfers between devices, per_device(): lax.all_to_all(probs.reshape(N_HEAD, -1, probs.shape[1]), 'head', 0, 0)  7.21 us
  transfers between devices with their start and end apart: 20, of which 14 were waited for; matrix products, arithmetic and copies ran while one was open for 0% of the time, Pallas kernels for 25%

profile of v3, /device:TPU:2, one launch (start us, length us, event | category | flops | bytes accessed | tf_op | source)
XLA Modules:
  0.0 141.9 jit_solution(7970639420461113149)
XLA Ops:
  0.6 1.8 %convert_element_type.3 = f32[1024,128]{1,0:T(8,128)} convert(bf16[1024,128]{1,0:T(8,128)(2,1)} %refs_4_.1) | non-fusion elementwise | flops 131072 | bytes 786432 | tf_op jit(solution)/shard_map/convert_element_type | solution.py:468
  2.4 1.6 %collective-permute-start = (f32[1024,128]{1,0:T(8,128)}, f32[1024,128]{1,0:T(8,128)S(1)}, u32[]{:S(2)}, u32[]{:S(2)}) collective-permute-start(f32[1024,128]{1,0:T(8,128)} %convert_element_type.3), channel_id=1, source_target_pairs={{0,128},{8,136},{16,144},{24,152},{32,160},{40,168},{48,176},{56,1... | collective-permute-start | bytes 1572872 | tf_op jit(solution)/shard_map/ppermute | solution.py:449
  4.7 7.5 %index_forward.1 = (f32[64,1024]{1,0:T(8,128)}, f32[16,128]{1,0:T(8,128)}) custom-call(s32[1]{0:T(128)S(6)} %copy.12.base_ref, s32[1,512]{1,0:T(1,128)} %bitcast.10, bf16[64,8192]{1,0:T(8,128)(2,1)} %refs_8_.1, bf16[1024,128]{1,0:T(8,128)(2,1)} %refs_4_.1, f32[64,64]{1,0:T(8,128)} %refs_9_.1), custom_call_target="tpu_custom_call" | custom-call | tf_op jit(solution)/shard_map/index_forward/pallas_call | solution.py:292
  12.2 13.4 %main_stats.1 = f32[16,640]{1,0:T(8,128)} custom-call(s32[1]{0:T(128)S(6)} %copy.12.base_ref, s32[1,512]{1,0:T(1,128)} %bitcast.11, f32[16,128]{1,0:T(8,128)} %get-tuple-element.22.row_ref, bf16[64,1024]{1,0:T(8,128)(2,1)} %bitcast.8, bf16[512,2048]{1,0:T(8,128)(2,1)} %qn_ref.3, bf16[512,1024]{1,0:T(8,128)(2,1)} %qr_ref.3, bf16[1024,2048]{1,0:T(8,128)(2,1)} %kn_ref.3), custom_call_target="tpu_custom_call" | custom-call | tf_op jit(solution)/shard_map/main_stats/pallas_call | solution.py:292
  25.6 0.1 collective-permute-start.1
  25.7 1.4 collective-permute-done.1
  27.1 0.8 multiply_add_fusion.4
  27.9 0.5 collective-permute-start.2
  28.5 3.6 %collective-permute-done.2 = f32[16,640]{1,0:T(8,128)S(1)} collective-permute-done((f32[16,640]{1,0:T(8,128)S(1)}, f32[16,640]{1,0:T(8,128)S(1)}, u32[]{:S(2)}, u32[]{:S(2)}) %collective-permute-start.2) | collective-permute-done | bytes 40992 | tf_op jit(solution)/shard_map/ppermute | solution.py:449
  32.0 5.9 %collective-permute-start.4 = (f32[16,640]{1,0:T(8,128)S(1)}, f32[16,640]{1,0:T(8,128)S(1)}, u32[]{:S(2)}, u32[]{:S(2)}) collective-permute-start(f32[16,640]{1,0:T(8,128)S(1)} %multiply_add_fusion.3), channel_id=1, source_target_pairs={{0,112},{8,120},{16,0},{24,8},{32,16},{40,24},{48,32},{56,40},{64,... | collective-permute-start | bytes 122888 | tf_op jit(solution)/shard_map/ppermute | solution.py:454
  38.0 1.7 %collective-permute-done.4 = f32[16,640]{1,0:T(8,128)S(1)} collective-permute-done((f32[16,640]{1,0:T(8,128)S(1)}, f32[16,640]{1,0:T(8,128)S(1)}, u32[]{:S(2)}, u32[]{:S(2)}) %collective-permute-start.4) | collective-permute-done | bytes 40992 | tf_op jit(solution)/shard_map/ppermute | solution.py:454
  39.7 3.5 %collective-permute-done.3 = f32[16,640]{1,0:T(8,128)S(1)} collective-permute-done((f32[16,640]{1,0:T(8,128)S(1)}, f32[16,640]{1,0:T(8,128)S(1)}, u32[]{:S(2)}, u32[]{:S(2)}) %collective-permute-start.3) | collective-permute-done | bytes 40992 | tf_op jit(solution)/shard_map/ppermute | solution.py:454
  43.2 0.1 multiply_add_fusion.2
  43.2 0.7 collective-permute-start.6
  44.0 3.2 %collective-permute-start.5 = (f32[16,640]{1,0:T(8,128)S(1)}, f32[16,640]{1,0:T(8,128)S(1)}, u32[]{:S(2)}, u32[]{:S(2)}) collective-permute-start(f32[16,640]{1,0:T(8,128)S(1)} %get-tuple-element.43), channel_id=1, source_target_pairs={{0,48},{8,56},{16,64},{24,72},{32,80},{40,88},{48,96},{56,104},{64... | collective-permute-start | bytes 122888 | tf_op jit(solution)/shard_map/ppermute | solution.py:454
  47.2 2.3 %collective-permute-done.6 = f32[16,640]{1,0:T(8,128)S(1)} collective-permute-done((f32[16,640]{1,0:T(8,128)S(1)}, f32[16,640]{1,0:T(8,128)S(1)}, u32[]{:S(2)}, u32[]{:S(2)}) %collective-permute-start.6) | collective-permute-done | bytes 40992 | tf_op jit(solution)/shard_map/ppermute | solution.py:454
  49.4 2.2 %collective-permute-done.5 = f32[16,640]{1,0:T(8,128)S(1)} collective-permute-done((f32[16,640]{1,0:T(8,128)S(1)}, f32[16,640]{1,0:T(8,128)S(1)}, u32[]{:S(2)}, u32[]{:S(2)}) %collective-permute-start.5) | collective-permute-done | bytes 40992 | tf_op jit(solution)/shard_map/ppermute | solution.py:454
  51.8 8.0 %main_probs.1 = f32[512,1024]{1,0:T(8,128)S(1)} custom-call(f32[16,640]{1,0:T(8,128)S(1)} %multiply_add_fusion.lse_ref, bf16[64,1024]{1,0:T(8,128)(2,1)S(1)} %bitcast.9, bf16[512,2048]{1,0:T(8,128)(2,1)S(1)} %copy-done.2, bf16[512,1024]{1,0:T(8,128)(2,1)S(1)} %copy-done.5, bf16[1024,2048]{1,0:T(8,128)(2,1)S(1)} %copy-done), custom_call_target="tpu_custom_call" | custom-call | tf_op jit(solution)/shard_map/main_probs/pallas_call | solution.py:292
  59.7 1.4 copy-done.3
  61.1 7.2 %all-to-all-start = ((f32[8,64,1024]{2,1,0:T(8,128)}), f32[8,64,1024]{2,1,0:T(8,128)S(1)}, u32[]{:S(2)}, u32[]{:S(2)}) async-start(f32[8,64,1024]{2,1,0:T(8,128)} %bitcast.7), calls=%async_computation | async-start | bytes 4194304 | tf_op jit(solution)/shard_map/all_to_all | solution.py:480
  68.3 0.1 collective-permute-start.7
  68.4 0.5 collective-permute-start.8
  68.9 1.6 %collective-permute-done.7.refs_5_ = f32[1024,128]{1,0:T(8,128)S(1)} collective-permute-done((f32[1024,128]{1,0:T(8,128)}, f32[1024,128]{1,0:T(8,128)S(1)}, u32[]{:S(2)}, u32[]{:S(2)}) %collective-permute-start.7) | collective-permute-done | bytes 524320 | tf_op jit(solution)/shard_map/ppermute | solution.py:449
  70.5 0.8 copy-done.9
  71.3 0.8 copy-done.11
  72.1 18.9 %all-to-all-done.target_ref = f32[8,64,1024]{2,1,0:T(8,128)S(1)} async-done(((f32[8,64,1024]{2,1,0:T(8,128)}), f32[8,64,1024]{2,1,0:T(8,128)S(1)}, u32[]{:S(2)}, u32[]{:S(2)}) %all-to-all-start) | async-done | bytes 2097184 | tf_op jit(solution)/shard_map/all_to_all | solution.py:480
  91.1 0.9 copy-done.14
  92.0 0.1 logit_grad.1.lg_ref.refs_0_
  92.2 0.1 collective-permute-start.10
  92.3 0.4 collective-permute-start.9
  92.7 7.4 %grad_k.1 = (f32[4,128,128]{2,1,0:T(8,128)S(1)}, f32[4,128,128]{2,1,0:T(8,128)S(1)}, f32[16,256]{1,0:T(8,128)S(1)}) custom-call(f32[64,1024]{1,0:T(8,128)S(1)} %logit_grad.1.lg_ref.refs_0_, bf16[64,8192]{1,0:T(8,128)(2,1)S(1)} %copy-done.1, bf16[1024,128]{1,0:T(8,128)(2,1)S(1)} %copy-done.4, f32[64,64]{1,0:T(8,128)S(1)} %copy-done.13), custom_call_target="tpu_custom_call" | custom-call | tf_op jit(solution)/shard_map/grad_k/pallas_call | solution.py:292
  100.1 0.9 collective-permute-done.9.refs_2_
  101.0 2.1 %collective-permute-start.11 = (f32[4,128,128]{2,1,0:T(8,128)S(1)}, f32[4,128,128]{2,1,0:T(8,128)S(1)}, u32[]{:S(2)}, u32[]{:S(2)}) collective-permute-start(f32[4,128,128]{2,1,0:T(8,128)S(1)} %get-tuple-element.32), channel_id=1, source_target_pairs={{0,2},{1,3},{2,0},{3,1},{4,6},{5,7},{6,4},{7,5},{8,10},{9,11},{10,... | collective-permute-start | bytes 786440 | tf_op jit(solution)/shard_map/ppermute | solution.py:445
  103.1 0.2 collective-permute-start.15
  103.3 1.1 collective-permute-start.14
  104.4 0.8 collective-permute-start.13
  105.3 1.2 collective-permute-done.14.refs_12_
  106.5 1.7 %collective-permute-done.13.refs_11_ = f32[16,256]{1,0:T(8,128)S(1)} collective-permute-done((f32[16,256]{1,0:T(8,128)S(1)}, f32[16,256]{1,0:T(8,128)S(1)}, u32[]{:S(2)}, u32[]{:S(2)}) %collective-permute-start.13) | collective-permute-done | bytes 16416 | tf_op jit(solution)/shard_map/ppermute | solution.py:449
  108.2 7.3 %grad_q.1 = f32[8,80,256]{2,1,0:T(8,128)} custom-call(f32[64,1024]{1,0:T(8,128)S(1)} %logit_grad.1.lg_ref.refs_0_, f32[64,1024]{1,0:T(8,128)S(1)} %collective-permute-done.10.refs_1_, f32[64,1024]{1,0:T(8,128)S(1)} %collective-permute-done.9.refs_2_, f32[64,1024]{1,0:T(8,128)S(1)} %collective-permute-done.12.refs_3_, bf16[1024,128]{1,0:T(8,128)(2,1)S(1)} %copy-done.4, ...), custom_call_target="tpu_custom_call" | custom-call | tf_op jit(solution)/shard_map/grad_q/pallas_call | solution.py:292
  115.5 3.9 %all-to-all-start.1 = ((f32[8,80,256]{2,1,0:T(8,128)}), f32[8,80,256]{2,1,0:T(8,128)S(1)}, u32[]{:S(2)}, u32[]{:S(2)}) async-start(f32[8,80,256]{2,1,0:T(8,128)} %grad_q.1), calls=%async_computation.1 | async-start | bytes 1310720 | tf_op jit(solution)/shard_map/all_to_all | solution.py:496
  119.4 0.1 collective-permute-start.16
  119.5 5.0 %collective-permute-done.16 = f32[2,128,128]{2,1,0:T(8,128)S(1)} collective-permute-done((f32[2,128,128]{2,1,0:T(8,128)S(1)}, f32[2,128,128]{2,1,0:T(8,128)S(1)}, u32[]{:S(2)}, u32[]{:S(2)}) %collective-permute-start.16) | collective-permute-done | bytes 131104 | tf_op jit(solution)/shard_map/ppermute | solution.py:445
  124.5 0.6 slice_bitcast_fusion
  125.2 1.8 %collective-permute-start.17 = (f32[128,128]{1,0:T(8,128)S(1)}, f32[128,128]{1,0:T(8,128)S(1)}, u32[]{:S(2)}, u32[]{:S(2)}) collective-permute-start(f32[128,128]{1,0:T(8,128)S(1)} %get-tuple-element.41), channel_id=1, source_target_pairs={{0,1},{1,0},{2,3},{3,2},{4,5},{5,4},{6,7},{7,6},{8,9},{9,8},{10,11... | collective-permute-start | bytes 196616 | tf_op jit(solution)/shard_map/ppermute | solution.py:445
  126.9 4.0 %collective-permute-done.17.got_ref = f32[128,128]{1,0:T(8,128)S(1)} collective-permute-done((f32[128,128]{1,0:T(8,128)S(1)}, f32[128,128]{1,0:T(8,128)S(1)}, u32[]{:S(2)}, u32[]{:S(2)}) %collective-permute-start.17) | collective-permute-done | bytes 65568 | tf_op jit(solution)/shard_map/ppermute | solution.py:445
  130.9 8.3 %all-to-all-done.1.parts_ref = f32[8,80,256]{2,1,0:T(8,128)S(1)} async-done(((f32[8,80,256]{2,1,0:T(8,128)}), f32[8,80,256]{2,1,0:T(8,128)S(1)}, u32[]{:S(2)}, u32[]{:S(2)}) %all-to-all-start.1) | async-done | bytes 655392 | tf_op jit(solution)/shard_map/all_to_all | solution.py:496
  139.2 0.8 copy-done.15
  140.1 1.9 %finish.1 = (f32[64,256]{1,0:T(8,128)}, f32[128,128]{1,0:T(8,128)}, f32[64,64]{1,0:T(8,128)}) custom-call(f32[8,80,256]{2,1,0:T(8,128)} %copy-done.15, f32[128,128]{1,0:T(8,128)} %get-tuple-element.42.mine_ref, f32[128,128]{1,0:T(8,128)} %copy-done.16), custom_call_target="tpu_custom_call" | custom-call | tf_op jit(solution)/shard_map/finish/pallas_call | solution.py:435
  (41 shorter events, 0.2 us)
Async XLA Ops:
  2.4 23.2 %collective-permute-start = (f32[1024,128]{1,0:T(8,128)}, f32[1024,128]{1,0:T(8,128)S(1)}, u32[]{:S(2)}, u32[]{:S(2)}) collective-permute-start(f32[1024,128]{1,0:T(8,128)} %convert_element_type.3), channel_id=1, source_target_pairs={{0,128},{8,136},{16,144},{24,152},{32,160},{40,168},{48,176},{56,1... | collective-permute-start | bytes 1572872 | tf_op jit(solution)/shard_map/ppermute | solution.py:449
  12.1 39.6 %copy-start = (bf16[1024,2048]{1,0:T(8,128)(2,1)S(1)}, bf16[1024,2048]{1,0:T(8,128)(2,1)}, u32[]{:S(2)}) copy-start(bf16[1024,2048]{1,0:T(8,128)(2,1)} %kn_ref.3) | copy-start | bytes 12582916
  12.1 39.6 %copy-start.2 = (bf16[512,2048]{1,0:T(8,128)(2,1)S(1)}, bf16[512,2048]{1,0:T(8,128)(2,1)}, u32[]{:S(2)}) copy-start(bf16[512,2048]{1,0:T(8,128)(2,1)} %qn_ref.3) | copy-start | bytes 6291460
  12.1 39.6 %copy-start.5 = (bf16[512,1024]{1,0:T(8,128)(2,1)S(1)}, bf16[512,1024]{1,0:T(8,128)(2,1)}, u32[]{:S(2)}) copy-start(bf16[512,1024]{1,0:T(8,128)(2,1)} %qr_ref.3) | copy-start | bytes 3145732
  12.1 39.6 %copy-start.6 = (bf16[1024,64]{0,1:T(8,128)(2,1)S(1)}, bf16[1024,64]{0,1:T(8,128)(2,1)}, u32[]{:S(2)}) copy-start(bf16[1024,64]{0,1:T(8,128)(2,1)} %param.12) | copy-start | bytes 393220
  25.6 34.1 %copy-start.7 = (f32[1024,128]{1,0:T(8,128)}, f32[1024,128]{1,0:T(8,128)S(1)}, u32[]{:S(2)}) copy-start(f32[1024,128]{1,0:T(8,128)S(1)} %collective-permute-done.refs_6_) | copy-start | bytes 1572868
  25.6 1.5 %collective-permute-start.1 = (f32[16,640]{1,0:T(8,128)}, f32[16,640]{1,0:T(8,128)S(1)}, u32[]{:S(2)}, u32[]{:S(2)}) collective-permute-start(f32[16,640]{1,0:T(8,128)} %main_stats.1), channel_id=1, source_target_pairs={{0,8},{8,0},{16,24},{24,16},{32,40},{40,32},{48,56},{56,48},{64,72... | collective-permute-start | bytes 122888 | tf_op jit(solution)/shard_map/ppermute | solution.py:449
  27.9 4.1 %collective-permute-start.2 = (f32[16,640]{1,0:T(8,128)S(1)}, f32[16,640]{1,0:T(8,128)S(1)}, u32[]{:S(2)}, u32[]{:S(2)}) collective-permute-start(f32[16,640]{1,0:T(8,128)S(1)} %multiply_add_fusion.4), channel_id=1, source_target_pairs={{0,128},{8,136},{16,144},{24,152},{32,160},{40,168},{48,176},{56,1... | collective-permute-start | bytes 122888 | tf_op jit(solution)/shard_map/ppermute | solution.py:449
  32.0 7.6 %collective-permute-start.4 = (f32[16,640]{1,0:T(8,128)S(1)}, f32[16,640]{1,0:T(8,128)S(1)}, u32[]{:S(2)}, u32[]{:S(2)}) collective-permute-start(f32[16,640]{1,0:T(8,128)S(1)} %multiply_add_fusion.3), channel_id=1, source_target_pairs={{0,112},{8,120},{16,0},{24,8},{32,16},{40,24},{48,32},{56,40},{64,... | collective-permute-start | bytes 122888 | tf_op jit(solution)/shard_map/ppermute | solution.py:454
  38.0 5.2 %collective-permute-start.3 = (f32[16,640]{1,0:T(8,128)S(1)}, f32[16,640]{1,0:T(8,128)S(1)}, u32[]{:S(2)}, u32[]{:S(2)}) collective-permute-start(f32[16,640]{1,0:T(8,128)S(1)} %multiply_add_fusion.3), channel_id=1, source_target_pairs={{0,16},{8,24},{16,32},{24,40},{32,48},{40,56},{48,64},{56,72},{64,... | collective-permute-start | bytes 122888 | tf_op jit(solution)/shard_map/ppermute | solution.py:454
  43.2 6.2 %collective-permute-start.6 = (f32[16,640]{1,0:T(8,128)S(1)}, f32[16,640]{1,0:T(8,128)S(1)}, u32[]{:S(2)}, u32[]{:S(2)}) collective-permute-start(f32[16,640]{1,0:T(8,128)S(1)} %get-tuple-element.44), channel_id=1, source_target_pairs={{0,80},{8,88},{16,96},{24,104},{32,112},{40,120},{48,0},{56,8},{64... | collective-permute-start | bytes 122888 | tf_op jit(solution)/shard_map/ppermute | solution.py:454
  44.0 7.7 %collective-permute-start.5 = (f32[16,640]{1,0:T(8,128)S(1)}, f32[16,640]{1,0:T(8,128)S(1)}, u32[]{:S(2)}, u32[]{:S(2)}) collective-permute-start(f32[16,640]{1,0:T(8,128)S(1)} %get-tuple-element.43), channel_id=1, source_target_pairs={{0,48},{8,56},{16,64},{24,72},{32,80},{40,88},{48,96},{56,104},{64... | collective-permute-start | bytes 122888 | tf_op jit(solution)/shard_map/ppermute | solution.py:454
  59.7 1.4 copy-start.3
  61.1 29.9 %all-to-all-start = ((f32[8,64,1024]{2,1,0:T(8,128)}), f32[8,64,1024]{2,1,0:T(8,128)S(1)}, u32[]{:S(2)}, u32[]{:S(2)}) async-start(f32[8,64,1024]{2,1,0:T(8,128)} %bitcast.7), calls=%async_computation | async-start | bytes 4194304 | tf_op jit(solution)/shard_map/all_to_all | solution.py:480
  68.3 24.4 %copy-start.1 = (bf16[64,8192]{1,0:T(8,128)(2,1)S(1)}, bf16[64,8192]{1,0:T(8,128)(2,1)}, u32[]{:S(2)}) copy-start(bf16[64,8192]{1,0:T(8,128)(2,1)} %refs_8_.1) | copy-start | bytes 3145732
  68.3 24.4 %copy-start.4 = (bf16[1024,128]{1,0:T(8,128)(2,1)S(1)}, bf16[1024,128]{1,0:T(8,128)(2,1)}, u32[]{:S(2)}) copy-start(bf16[1024,128]{1,0:T(8,128)(2,1)} %refs_4_.1) | copy-start | bytes 786436
  68.3 24.4 %copy-start.13 = (f32[64,64]{1,0:T(8,128)S(1)}, f32[64,64]{1,0:T(8,128)}, u32[]{:S(2)}) copy-start(f32[64,64]{1,0:T(8,128)} %refs_9_.1) | copy-start | bytes 49156
  68.3 2.2 %collective-permute-start.7 = (f32[1024,128]{1,0:T(8,128)}, f32[1024,128]{1,0:T(8,128)S(1)}, u32[]{:S(2)}, u32[]{:S(2)}) collective-permute-start(f32[1024,128]{1,0:T(8,128)} %convert_element_type.3), channel_id=1, source_target_pairs={{0,8},{8,0},{16,24},{24,16},{32,40},{40,32},{48,56},{56,48},{64,72... | collective-permute-start | bytes 1572872 | tf_op jit(solution)/shard_map/ppermute | solution.py:449
  68.4 2.9 %collective-permute-start.8 = (f32[1024,128]{1,0:T(8,128)}, f32[1024,128]{1,0:T(8,128)S(1)}, u32[]{:S(2)}, u32[]{:S(2)}) collective-permute-start(f32[1024,128]{1,0:T(8,128)} %copy-done.7), channel_id=1, source_target_pairs={{0,8},{8,0},{16,24},{24,16},{32,40},{40,32},{48,56},{56,48},{64,72... | collective-permute-start | bytes 1572872 | tf_op jit(solution)/shard_map/ppermute | solution.py:449
  70.5 0.8 copy-start.9
  71.3 0.8 copy-start.11
  91.1 1.0 copy-start.14
  92.0 16.2 %copy-start.8 = (f32[1024,128]{1,0:T(8,128)S(1)}, f32[1024,128]{1,0:T(8,128)}, u32[]{:S(2)}) copy-start(f32[1024,128]{1,0:T(8,128)} %copy-done.7) | copy-start | bytes 1572868
  92.0 16.2 %copy-start.10 = (f32[1024,128]{1,0:T(8,128)S(1)}, f32[1024,128]{1,0:T(8,128)}, u32[]{:S(2)}) copy-start(f32[1024,128]{1,0:T(8,128)} %copy-done.9) | copy-start | bytes 1572868
  92.0 16.2 %copy-start.12 = (f32[1024,128]{1,0:T(8,128)S(1)}, f32[1024,128]{1,0:T(8,128)}, u32[]{:S(2)}) copy-start(f32[1024,128]{1,0:T(8,128)} %copy-done.11) | copy-start | bytes 1572868
  92.2 7.9 %collective-permute-start.10 = (f32[64,1024]{1,0:T(8,128)S(1)}, f32[64,1024]{1,0:T(8,128)S(1)}, u32[]{:S(2)}, u32[]{:S(2)}) collective-permute-start(f32[64,1024]{1,0:T(8,128)S(1)} %logit_grad.1.lg_ref.refs_0_), channel_id=1, source_target_pairs={{0,8},{8,0},{16,24},{24,16},{32,40},{40,32},{48,56},{56,48},{64,72... | collective-permute-start | bytes 786440 | tf_op jit(solution)/shard_map/ppermute | solution.py:449
  92.3 8.7 %collective-permute-start.9 = (f32[64,1024]{1,0:T(8,128)S(1)}, f32[64,1024]{1,0:T(8,128)S(1)}, u32[]{:S(2)}, u32[]{:S(2)}) collective-permute-start(f32[64,1024]{1,0:T(8,128)S(1)} %logit_grad.1.lg_ref.refs_0_), channel_id=1, source_target_pairs={{0,128},{8,136},{16,144},{24,152},{32,160},{40,168},{48,176},{56,1... | collective-permute-start | bytes 786440 | tf_op jit(solution)/shard_map/ppermute | solution.py:449
  101.0 7.2 %collective-permute-start.12 = (f32[64,1024]{1,0:T(8,128)S(1)}, f32[64,1024]{1,0:T(8,128)S(1)}, u32[]{:S(2)}, u32[]{:S(2)}) collective-permute-start(f32[64,1024]{1,0:T(8,128)S(1)} %collective-permute-done.9.refs_2_), channel_id=1, source_target_pairs={{0,8},{8,0},{16,24},{24,16},{32,40},{40,32},{48,56},{56,48},{64,72... | collective-permute-start | bytes 786440 | tf_op jit(solution)/shard_map/ppermute | solution.py:449
  101.0 14.5 %collective-permute-start.11 = (f32[4,128,128]{2,1,0:T(8,128)S(1)}, f32[4,128,128]{2,1,0:T(8,128)S(1)}, u32[]{:S(2)}, u32[]{:S(2)}) collective-permute-start(f32[4,128,128]{2,1,0:T(8,128)S(1)} %get-tuple-element.32), channel_id=1, source_target_pairs={{0,2},{1,3},{2,0},{3,1},{4,6},{5,7},{6,4},{7,5},{8,10},{9,11},{10,... | collective-permute-start | bytes 786440 | tf_op jit(solution)/shard_map/ppermute | solution.py:445
  103.1 2.1 %collective-permute-start.15 = (f32[16,256]{1,0:T(8,128)S(1)}, f32[16,256]{1,0:T(8,128)S(1)}, u32[]{:S(2)}, u32[]{:S(2)}) collective-permute-start(f32[16,256]{1,0:T(8,128)S(1)} %get-tuple-element.37.refs_10_), channel_id=1, source_target_pairs={{0,8},{8,0},{16,24},{24,16},{32,40},{40,32},{48,56},{56,48},{64,72... | collective-permute-start | bytes 49160 | tf_op jit(solution)/shard_map/ppermute | solution.py:449
  103.3 3.2 %collective-permute-start.14 = (f32[16,256]{1,0:T(8,128)S(1)}, f32[16,256]{1,0:T(8,128)S(1)}, u32[]{:S(2)}, u32[]{:S(2)}) collective-permute-start(f32[16,256]{1,0:T(8,128)S(1)} %get-tuple-element.37.refs_10_), channel_id=1, source_target_pairs={{0,136},{8,128},{16,152},{24,144},{32,168},{40,160},{48,184},{56,1... | collective-permute-start | bytes 49160 | tf_op jit(solution)/shard_map/ppermute | solution.py:449
  104.4 3.7 %collective-permute-start.13 = (f32[16,256]{1,0:T(8,128)S(1)}, f32[16,256]{1,0:T(8,128)S(1)}, u32[]{:S(2)}, u32[]{:S(2)}) collective-permute-start(f32[16,256]{1,0:T(8,128)S(1)} %get-tuple-element.37.refs_10_), channel_id=1, source_target_pairs={{0,128},{8,136},{16,144},{24,152},{32,160},{40,168},{48,176},{56,1... | collective-permute-start | bytes 49160 | tf_op jit(solution)/shard_map/ppermute | solution.py:449
  115.5 23.7 %all-to-all-start.1 = ((f32[8,80,256]{2,1,0:T(8,128)}), f32[8,80,256]{2,1,0:T(8,128)S(1)}, u32[]{:S(2)}, u32[]{:S(2)}) async-start(f32[8,80,256]{2,1,0:T(8,128)} %grad_q.1), calls=%async_computation.1 | async-start | bytes 1310720 | tf_op jit(solution)/shard_map/all_to_all | solution.py:496
  119.4 5.1 %collective-permute-start.16 = (f32[2,128,128]{2,1,0:T(8,128)S(1)}, f32[2,128,128]{2,1,0:T(8,128)S(1)}, u32[]{:S(2)}, u32[]{:S(2)}) collective-permute-start(f32[2,128,128]{2,1,0:T(8,128)S(1)} %slice_add_fusion), channel_id=1, source_target_pairs={{0,6},{1,7},{2,4},{3,5},{4,2},{5,3},{6,0},{7,1},{8,14},{9,15},{10,... | collective-permute-start | bytes 393224 | tf_op jit(solution)/shard_map/ppermute | solution.py:445
  125.2 5.8 %collective-permute-start.17 = (f32[128,128]{1,0:T(8,128)S(1)}, f32[128,128]{1,0:T(8,128)S(1)}, u32[]{:S(2)}, u32[]{:S(2)}) collective-permute-start(f32[128,128]{1,0:T(8,128)S(1)} %get-tuple-element.41), channel_id=1, source_target_pairs={{0,1},{1,0},{2,3},{3,2},{4,5},{5,4},{6,7},{7,6},{8,9},{9,8},{10,11... | collective-permute-start | bytes 196616 | tf_op jit(solution)/shard_map/ppermute | solution.py:445
  130.9 8.3 %copy-start.16 = (f32[128,128]{1,0:T(8,128)}, f32[128,128]{1,0:T(8,128)S(1)}, u32[]{:S(2)}) copy-start(f32[128,128]{1,0:T(8,128)S(1)} %collective-permute-done.17.got_ref) | copy-start | bytes 196612
  139.2 0.8 copy-start.15

commit v4 on v3

--- a/solution.py
+++ b/solution.py
@@ -60,43 +60,6 @@
     return jnp.concatenate([block[:, i * 128 : (i + 1) * 128] for i in range(count)], axis=0)
 
 
-def index_kernel(base_ref, qpos_ref, iq_ref, ik_ref, w_ref, logits_ref, row_ref, wp, qcol, s_ref, acc):
-    step = pl.program_id(0)
-    rows, keys = logits_ref.shape
-
-    @pl.when(step == 0)
-    def _():
-        wt = w_ref[...].T
-        for i in range(IDX_HEADS // 2):
-            pair = [wt[2 * i : 2 * i + 1], wt[2 * i + 1 : 2 * i + 2]]
-            wp[i : i + 1, :] = jnp.concatenate(pair, axis=1)
-        acc[...] = jnp.zeros_like(acc)
-        qcol[...] = column(qpos_ref[...])
-
-    s_ref[...] = dot(ik_ref[...], stacked(iq_ref[...]), NT)
-    weights = [wp[pl.ds(step * GROUP // 2 + i, 1), :] for i in range(GROUP // 2)]
-    for r in range(keys // 64):
-        at = slice(r * 64, (r + 1) * 64)
-        total = acc[at, :]
-        for i, weight in enumerate(weights):
-            total = total + jnp.maximum(s_ref[at, i * 128 : (i + 1) * 128], 0.0) * weight
-        acc[at, :] = total
-
-    @pl.when(step == pl.num_programs(0) - 1)
-    def _():
-        turned = acc[...].T
-        key = lax.broadcasted_iota(jnp.int32, (rows, keys), 1) + base_ref[0] * keys
-        start = pl.multiple_of(lax.axis_index("head") * rows, rows)
-        limit = lanes_of(qcol[pl.ds(start, rows), :], keys)
-        logits = (turned[:rows] + turned[rows:]) * (INV_ROOT * LOG2E)
-        logits = jnp.where(key <= limit, logits, NEG)
-        logits_ref[...] = logits
-        top = jnp.max(logits, axis=1, keepdims=True)
-        total = jnp.sum(jnp.exp2(logits - top), axis=1, keepdims=True)
-        lse = jnp.broadcast_to(top + jnp.log2(total), (rows, 128)).T
-        row_ref[...] = jnp.concatenate([lse[:16, :rows], jnp.zeros((16, 128 - rows), F32)], axis=1)
-
-
 def pair_operands(refs, krp, p):
     qn_ref, qr_ref, kn_ref = refs
     part = slice(p * 128, (p + 1) * 128)
@@ -120,36 +83,74 @@
     return best * SCORE_SCALE + jnp.log2(total)
 
 
-def stats_kernel(
-    base_ref, qpos_ref, row_ref, krt_ref, qn_ref, qr_ref, kn_ref, out_ref, bias, krp, s_ref
+def front_kernel(
+    base_ref, qpos_ref, krt_ref, ik_ref, w_ref, iq_ref, qn_ref, qr_ref, kn_ref, out_ref, logits_ref,
+    bias, krp, s_ref, wp, qcol, si_ref, acc,
 ):
     step = pl.program_id(0)
     keys, queries = bias.shape
+    rows = logits_ref.shape[0]
 
     @pl.when(step == 0)
     def _():
         key = lax.broadcasted_iota(jnp.int32, bias.shape, 0) + base_ref[0] * keys
         bias[...] = jnp.where(key <= qpos_ref[...], 0.0, NEG)
         fill_rope(krt_ref, krp)
-        out_ref[:, queries:] = row_ref[...]
-
-    for p in range(2):
+        wt = w_ref[...].T
+        for i in range(IDX_HEADS // 2):
+            pair = [wt[2 * i : 2 * i + 1], wt[2 * i + 1 : 2 * i + 2]]
+            wp[i : i + 1, :] = jnp.concatenate(pair, axis=1)
+        acc[...] = jnp.zeros_like(acc)
+        qcol[...] = column(qpos_ref[...])
+
+    def scores(p):
         q, k = pair_operands((qn_ref, qr_ref, kn_ref), krp, p)
         s_ref[p] = dot(k, q, NT)
-    for p in range(2):
+
+    def statistics(p):
         for qc in range(queries // 256):
             cols = slice(qc * 256, (qc + 1) * 256)
             out_ref[pl.ds(2 * step + p, 1), cols] = online_lse(s_ref.at[p], bias, cols)
 
-
-def probs_kernel(lse_ref, krt_ref, qn_ref, qr_ref, kn_ref, out_ref, krp, s_ref):
+    scores(0)
+    si_ref[...] = dot(ik_ref[...], stacked(iq_ref[...]), NT)
+    statistics(0)
+    scores(1)
+    weights = [wp[pl.ds(step * GROUP // 2 + i, 1), :] for i in range(GROUP // 2)]
+    for r in range(keys // 64):
+        at = slice(r * 64, (r + 1) * 64)
+        total = acc[at, :]
+        for i, weight in enumerate(weights):
+            total = total + jnp.maximum(si_ref[at, i * 128 : (i + 1) * 128], 0.0) * weight
+        acc[at, :] = total
+    statistics(1)
+
+    @pl.when(step == pl.num_programs(0) - 1)
+    def _():
+        turned = acc[...].T
+        key = lax.broadcasted_iota(jnp.int32, (rows, keys), 1) + base_ref[0] * keys
+        start = pl.multiple_of(lax.axis_index("head") * rows, rows)
+        limit = lanes_of(qcol[pl.ds(start, rows), :], keys)
+        logits = (turned[:rows] + turned[rows:]) * (INV_ROOT * LOG2E)
+        logits = jnp.where(key <= limit, logits, NEG)
+        logits_ref[...] = logits
+        top = jnp.max(logits, axis=1, keepdims=True)
+        total = jnp.sum(jnp.exp2(logits - top), axis=1, keepdims=True)
+        lse = jnp.broadcast_to(top + jnp.log2(total), (rows, 128)).T
+        row = [lse[:16, :rows], jnp.zeros((16, 128 - rows), F32)]
+        out_ref[:, queries:] = jnp.concatenate(row, axis=1)
+
+
+def probs_kernel(lse_ref, krt_ref, qn_ref, qr_ref, kn_ref, out_hbm, krp, s_ref, acc, sems):
     step = pl.program_id(0)
-    queries, keys = out_ref.shape
+    last = pl.num_programs(0) - 1
+    queries, keys = acc.shape
+    size = queries // N_HEAD
 
     @pl.when(step == 0)
     def _():
         fill_rope(krt_ref, krp)
-        out_ref[...] = jnp.zeros_like(out_ref)
+        acc[...] = jnp.zeros_like(acc)
 
     lse = []
     for p in range(2):
@@ -157,11 +158,22 @@
         lse.append(column(lse_ref[pl.ds(2 * step + p, 1), :queries]))
     for r in range(queries // 32):
         rows = slice(r * 32, (r + 1) * 32)
-        total = out_ref[rows, :]
+        total = acc[rows, :]
         for p in range(2):
             s = s_ref[p, rows, :] * SCORE_SCALE - lanes_of(lse[p][rows], keys)
             total = total + jnp.exp2(s)
-        out_ref[rows, :] = total
+        acc[rows, :] = total
+
+    @pl.when(step == last)
+    def _():
+        copies = []
+        for h in range(N_HEAD):
+            rows = pl.ds(h * size, size)
+            copies.append(pltpu.make_async_copy(acc.at[rows], out_hbm.at[rows], sems.at[h]))
+        for copy in copies:
+            copy.start()
+        for copy in copies:
+            copy.wait()
 
 
 def lg_kernel(lse_ref, logits_ref, target_ref, lg_ref):
@@ -301,32 +313,6 @@
     )(*ins)
 
 
-def run_index(key_blocks, qpos, iq, ik, w):
-    rows, keys = iq.shape[0], ik.shape[0]
-    groups = IDX_HEADS // GROUP
-    shapes = [(rows, keys), (16, 128)]
-    return call(
-        index_kernel,
-        "index_forward",
-        (groups,),
-        (key_blocks, qpos, iq, ik, w),
-        [
-            smem(),
-            whole(qpos.shape),
-            pl.BlockSpec((rows, GROUP * 128), lambda i: (0, i)),
-            *wholes([ik, w]),
-        ],
-        floats(*shapes),
-        [whole(s) for s in shapes],
-        [
-            pltpu.VMEM((IDX_HEADS // 2, 128), F32),
-            pltpu.VMEM((qpos.shape[1], 128), jnp.int32),
-            pltpu.VMEM((keys, GROUP * rows), F32),
-            pltpu.VMEM((keys, 128), F32),
-        ],
-    )
-
-
 def main_specs(queries, keys):
     return [
         pl.BlockSpec((queries, 256), lambda i: (0, i)),
@@ -335,23 +321,33 @@
     ]
 
 
-def run_stats(key_blocks, qpos, index_row, qn, qr, kn, krt):
+def run_front(key_blocks, qpos, krt, ik, w, iq, qn, qr, kn):
     queries, keys, pairs = qn.shape[0], kn.shape[0], qn.shape[1] // 256
-    shape = (2 * pairs, queries + 128)
+    rows = iq.shape[0]
+    shapes = [(2 * pairs, queries + 128), (rows, keys)]
     return call(
-        stats_kernel,
-        "main_stats",
+        front_kernel,
+        "front",
         (pairs,),
-        (key_blocks, qpos, index_row, krt, qn, qr, kn),
-        [smem(), *wholes([qpos, index_row, krt]), *main_specs(queries, keys)],
-        floats(shape),
-        [whole(shape)],
+        (key_blocks, qpos, krt, ik, w, iq, qn, qr, kn),
+        [
+            smem(),
+            *wholes([qpos, krt, ik, w]),
+            pl.BlockSpec((rows, GROUP * 128), lambda i: (0, i)),
+            *main_specs(queries, keys),
+        ],
+        floats(*shapes),
+        [whole(s) for s in shapes],
         [
             pltpu.VMEM((keys, queries), F32),
             pltpu.VMEM((2, keys, 128), BF16),
             pltpu.VMEM((2, keys, queries), F32),
+            pltpu.VMEM((IDX_HEADS // 2, 128), F32),
+            pltpu.VMEM((queries, 128), jnp.int32),
+            pltpu.VMEM((keys, GROUP * rows), F32),
+            pltpu.VMEM((keys, 128), F32),
         ],
-    )[0]
+    )
 
 
 def run_probs(lse, qn, qr, kn, krt):
@@ -363,8 +359,13 @@
         (lse, krt, qn, qr, kn),
         [*wholes([lse, krt]), *main_specs(queries, keys)],
         floats((queries, keys)),
-        [whole((queries, keys))],
-        [pltpu.VMEM((2, keys, 128), BF16), pltpu.VMEM((2, queries, keys), F32)],
+        [pl.BlockSpec(memory_space=pltpu.HBM)],
+        [
+            pltpu.VMEM((2, keys, 128), BF16),
+            pltpu.VMEM((2, queries, keys), F32),
+            pltpu.VMEM((queries, keys), F32),
+            pltpu.SemaphoreType.DMA((N_HEAD,)),
+        ],
         24,
     )[0]
 
@@ -437,6 +438,7 @@
         in_specs=[in_vmem()] * 3,
         out_specs=[in_vmem()] * 3,
         out_shape=floats(*shapes),
+        compiler_params=pltpu.CompilerParams(vmem_limit_bytes=8 * 1024 * 1024),
         name="finish",
     )(*ins)
 
@@ -462,24 +464,27 @@
     return top + jnp.log2(total)
 
 
+def over_z(lse):
+    below, above = z_shift(lse, 1), z_shift(lse, -1)
+    two, three = merged(lse, below), merged(lse, below, above)
+    return merged(three, z_shift(three, 3), z_shift(two, -3))
+
+
 def per_device(qn, qr, kn, kr, iq, ik, w, query_pos, key_blocks):
     qpos = query_pos[None, :]
     krt = kr.T
-    ikf = ik.astype(F32)
-    ikf_y = ctx_xor(ikf, 16)
-    logits, index_row = run_index(key_blocks, qpos, iq, ik, w)
-    lse = run_stats(key_blocks, qpos, index_row, qn, qr, kn, krt)
-    lse, ikf_y = lax.optimization_barrier((lse, ikf_y))
+    lse, logits = run_front(key_blocks, qpos, krt, ik, w, iq, qn, qr, kn)
     lse = merged(lse, ctx_xor(lse, 1))
     lse = merged(lse, ctx_xor(lse, 16))
-    below, above = z_shift(lse, 1), z_shift(lse, -1)
-    two, three = merged(lse, below), merged(lse, below, above)
-    lse = merged(three, z_shift(three, 3), z_shift(two, -3))
+    lse, ik_later = lax.optimization_barrier((lse, ik))
+    ikf = ik_later.astype(F32)
+    ikf_y, ikf_c = ctx_xor(ikf, 16), ctx_xor(ikf, 1)
+    lse, ikf_y, ikf_c = lax.optimization_barrier((over_z(lse), ikf_y, ikf_c))
     probs = run_probs(lse, qn, qr, kn, krt)
-    probs, ikf, ikf_y = lax.optimization_barrier((probs, ikf, ikf_y))
+    probs, ikf_y = lax.optimization_barrier((probs, ikf_y))
     target = lax.all_to_all(probs.reshape(N_HEAD, -1, probs.shape[1]), "head", 0, 0)
-    ikf_c, ikf_yc = ctx_xor(ikf, 1), ctx_xor(ikf_y, 1)
-    target, ikf_c, ikf_yc = lax.optimization_barrier((target, ikf_c, ikf_yc))
+    ikf_yc = ctx_xor(ikf_y, 1)
+    target, ikf_yc = lax.optimization_barrier((target, ikf_yc))
 
     lg = run_lg(lse, logits, target)
     lg_y, lg_c = ctx_xor(lg, 16), ctx_xor(lg, 1)

time: 143 us -> 142 us (level)
  Pallas kernels: 45.6 us -> 40.6 us
  waiting for transfers between devices: 56.2 us -> 61.2 us
  starting transfers between devices: 30.4 us -> 32.9 us
  local copies, waits for them, and re-layouts: 5.44 us -> 3.16 us
  other arithmetic: 2.79 us -> 1.03 us
    all_to_all x1, waiting for transfers between devices: 18.9 us -> 25.2 us  [per_device(): lax.all_to_all(probs.reshape(N_HEAD, -1, probs.shape[1]), 'head', 0, 0)]
    pallas_call x5 -> x4, Pallas kernels: 43.5 us -> 39.7 us  [call(): pl.pallas_call(kernel, grid=grid, in_specs=in_specs, out_specs=out_specs,...]
    convert_element_type x1, other arithmetic: 1.79 us -> 0.04 us  [per_device(): ikf = ik_later.astype(F32)]
    unnamed x34 -> x26, local copies, waits for them, and re-layouts: 4.8 us -> 3.14 us
    ppermute x4, waiting for transfers between devices: 9.73 us -> 8.23 us  [z_shift(): return lax.ppermute(value, 'ctx', list(enumerate(to)))]
  transfers between devices with their start and end apart: 20 -> 20, of which waited for: 14 -> 14; matrix products, arithmetic and copies ran while one was open for 0% -> 0% of each run, Pallas kernels for 25% -> 11%
where the time goes in v4:
time: 142 us; the launch traced here: 140 us
  waiting for transfers between devices  61.2 us (43%)
  Pallas kernels  40.6 us (29%)
  starting transfers between devices  32.9 us (23%)
  local copies, waits for them, and re-layouts  3.16 us (2%)
  between operations  1.47 us (1%)
    pallas_call x4, Pallas kernels, call(): pl.pallas_call(kernel, grid=grid, in_specs=in_specs, out_specs=out_specs,...  39.7 us
    all_to_all x1, waiting for transfers between devices, per_device(): lax.all_to_all(probs.reshape(N_HEAD, -1, probs.shape[1]), 'head', 0, 0)  25.2 us
    ppermute x4, starting transfers between devices, z_shift(): return lax.ppermute(value, 'ctx', list(enumerate(to)))  9.83 us
    ppermute x11, waiting for transfers between devices, ctx_xor(): return lax.ppermute(value, 'ctx', [(i, i ^ bits) for i in range(N_CTX)])  9.74 us
    ppermute x3, waiting for transfers between devices, head_xor(): return lax.ppermute(value, 'head', [(i, i ^ bits) for i in range(N_HEAD)])  9.26 us
    all_to_all x1, waiting for transfers between devices, per_device(): parts = lax.all_to_all(parts, 'ctx', 0, 0, axis_index_groups=groups)  8.8 us
    ppermute x4, waiting for transfers between devices, z_shift(): return lax.ppermute(value, 'ctx', list(enumerate(to)))  8.23 us
    all_to_all x1, starting transfers between devices, per_device(): lax.all_to_all(probs.reshape(N_HEAD, -1, probs.shape[1]), 'head', 0, 0)  7.46 us
  transfers between devices with their start and end apart: 20, of which 14 were waited for; matrix products, arithmetic and copies ran while one was open for 0% of the time, Pallas kernels for 11%

profile of v4, /device:TPU:2, one launch (start us, length us, event | category | flops | bytes accessed | tf_op | source)
XLA Modules:
  0.0 140.4 jit_solution(15838764547233756619)
XLA Ops:
  1.3 15.8 %front.1 = (f32[16,640]{1,0:T(8,128)}, f32[64,1024]{1,0:T(8,128)}) custom-call(s32[1]{0:T(128)S(6)} %copy.12.base_ref, s32[1,512]{1,0:T(1,128)} %bitcast.10, bf16[64,1024]{1,0:T(8,128)(2,1)} %bitcast.8, bf16[1024,128]{1,0:T(8,128)(2,1)} %refs_4_.1, f32[64,64]{1,0:T(8,128)} %refs_9_.1, bf16[64,8192]{1,0:T(8,128)(2,1)} %refs_8_.1, bf16[512,2048]{1,0:T(8,128)(2,1)} %qn_ref.3, ...), custom_call_target="tpu_custom_call" | custom-call | tf_op jit(solution)/shard_map/front/pallas_call | solution.py:304
  17.2 0.1 collective-permute-start
  17.2 1.4 %collective-permute-done = f32[16,640]{1,0:T(8,128)S(1)} collective-permute-done((f32[16,640]{1,0:T(8,128)}, f32[16,640]{1,0:T(8,128)S(1)}, u32[]{:S(2)}, u32[]{:S(2)}) %collective-permute-start) | collective-permute-done | bytes 40992 | tf_op jit(solution)/shard_map/ppermute | solution.py:451
  18.7 0.8 multiply_add_fusion.4
  19.5 1.7 %collective-permute-start.1 = (f32[16,640]{1,0:T(8,128)S(1)}, f32[16,640]{1,0:T(8,128)S(1)}, u32[]{:S(2)}, u32[]{:S(2)}) collective-permute-start(f32[16,640]{1,0:T(8,128)S(1)} %multiply_add_fusion.4), channel_id=1, source_target_pairs={{0,128},{8,136},{16,144},{24,152},{32,160},{40,168},{48,176},{56,1... | collective-permute-start | bytes 122888 | tf_op jit(solution)/shard_map/ppermute | solution.py:451
  21.1 2.4 %collective-permute-done.1 = f32[16,640]{1,0:T(8,128)S(1)} collective-permute-done((f32[16,640]{1,0:T(8,128)S(1)}, f32[16,640]{1,0:T(8,128)S(1)}, u32[]{:S(2)}, u32[]{:S(2)}) %collective-permute-start.1) | collective-permute-done | bytes 40992 | tf_op jit(solution)/shard_map/ppermute | solution.py:451
  23.6 5.9 %collective-permute-start.3 = (f32[16,640]{1,0:T(8,128)S(1)}, f32[16,640]{1,0:T(8,128)S(1)}, u32[]{:S(2)}, u32[]{:S(2)}) collective-permute-start(f32[16,640]{1,0:T(8,128)S(1)} %multiply_add_fusion.3), channel_id=1, source_target_pairs={{0,112},{8,120},{16,0},{24,8},{32,16},{40,24},{48,32},{56,40},{64,... | collective-permute-start | bytes 122888 | tf_op jit(solution)/shard_map/ppermute | solution.py:456
  29.5 0.0 collective-permute-start.2
  29.6 0.1 collective-permute-start.7
  29.7 1.7 %collective-permute-start.6 = (f32[1024,128]{1,0:T(8,128)S(1)}, f32[1024,128]{1,0:T(8,128)}, u32[]{:S(2)}, u32[]{:S(2)}) collective-permute-start(f32[1024,128]{1,0:T(8,128)S(1)} %convert_element_type.3), channel_id=1, source_target_pairs={{0,128},{8,136},{16,144},{24,152},{32,160},{40,168},{48,176},{56,1... | collective-permute-start | bytes 1572872 | tf_op jit(solution)/shard_map/ppermute | solution.py:451
  31.3 0.0 collective-permute-done.3
  31.3 3.4 %collective-permute-done.2 = f32[16,640]{1,0:T(8,128)S(1)} collective-permute-done((f32[16,640]{1,0:T(8,128)S(1)}, f32[16,640]{1,0:T(8,128)S(1)}, u32[]{:S(2)}, u32[]{:S(2)}) %collective-permute-start.2) | collective-permute-done | bytes 40992 | tf_op jit(solution)/shard_map/ppermute | solution.py:456
  34.7 0.1 multiply_add_fusion.2
  34.8 0.8 collective-permute-start.5
  35.6 3.1 %collective-permute-start.4 = (f32[16,640]{1,0:T(8,128)S(1)}, f32[16,640]{1,0:T(8,128)S(1)}, u32[]{:S(2)}, u32[]{:S(2)}) collective-permute-start(f32[16,640]{1,0:T(8,128)S(1)} %get-tuple-element.45), channel_id=1, source_target_pairs={{0,48},{8,56},{16,64},{24,72},{32,80},{40,88},{48,96},{56,104},{64... | collective-permute-start | bytes 122888 | tf_op jit(solution)/shard_map/ppermute | solution.py:456
  38.7 2.3 %collective-permute-done.5 = f32[16,640]{1,0:T(8,128)S(1)} collective-permute-done((f32[16,640]{1,0:T(8,128)S(1)}, f32[16,640]{1,0:T(8,128)S(1)}, u32[]{:S(2)}, u32[]{:S(2)}) %collective-permute-start.5) | collective-permute-done | bytes 40992 | tf_op jit(solution)/shard_map/ppermute | solution.py:456
  41.0 2.6 %collective-permute-done.4 = f32[16,640]{1,0:T(8,128)S(1)} collective-permute-done((f32[16,640]{1,0:T(8,128)S(1)}, f32[16,640]{1,0:T(8,128)S(1)}, u32[]{:S(2)}, u32[]{:S(2)}) %collective-permute-start.4) | collective-permute-done | bytes 40992 | tf_op jit(solution)/shard_map/ppermute | solution.py:456
  43.6 0.5 collective-permute-done.6.refs_6_
  44.1 8.1 %main_probs.1 = f32[512,1024]{1,0:T(8,128)S(1)} custom-call(f32[16,640]{1,0:T(8,128)S(1)} %multiply_add_fusion.lse_ref, bf16[64,1024]{1,0:T(8,128)(2,1)S(1)} %bitcast.9, bf16[512,2048]{1,0:T(8,128)(2,1)S(1)} %copy-done.2, bf16[512,1024]{1,0:T(8,128)(2,1)S(1)} %copy-done.5, bf16[1024,2048]{1,0:T(8,128)(2,1)S(1)} %copy-done), custom_call_target="tpu_custom_call" | custom-call | tf_op jit(solution)/shard_map/main_probs/pallas_call | solution.py:304
  52.3 1.4 copy-done.3
  53.7 7.5 %all-to-all-start = ((f32[8,64,1024]{2,1,0:T(8,128)}), f32[8,64,1024]{2,1,0:T(8,128)S(1)}, u32[]{:S(2)}, u32[]{:S(2)}) async-start(f32[8,64,1024]{2,1,0:T(8,128)} %bitcast.7), calls=%async_computation | async-start | bytes 4194304 | tf_op jit(solution)/shard_map/all_to_all | solution.py:485
  61.1 2.1 %collective-permute-done.8.refs_7_ = f32[1024,128]{1,0:T(8,128)S(1)} collective-permute-done((f32[1024,128]{1,0:T(8,128)}, f32[1024,128]{1,0:T(8,128)S(1)}, u32[]{:S(2)}, u32[]{:S(2)}) %collective-permute-start.8) | collective-permute-done | bytes 524320 | tf_op jit(solution)/shard_map/ppermute | solution.py:451
  63.2 0.8 copy-done.9
  64.0 25.2 %all-to-all-done.target_ref = f32[8,64,1024]{2,1,0:T(8,128)S(1)} async-done(((f32[8,64,1024]{2,1,0:T(8,128)}), f32[8,64,1024]{2,1,0:T(8,128)S(1)}, u32[]{:S(2)}, u32[]{:S(2)}) %all-to-all-start) | async-done | bytes 2097184 | tf_op jit(solution)/shard_map/all_to_all | solution.py:485
  89.2 0.9 copy-done.12
  90.2 0.1 logit_grad.1.lg_ref.refs_0_
  90.3 0.1 collective-permute-start.10
  90.4 0.9 collective-permute-start.9
  91.4 7.4 %grad_k.1 = (f32[4,128,128]{2,1,0:T(8,128)S(1)}, f32[4,128,128]{2,1,0:T(8,128)S(1)}, f32[16,256]{1,0:T(8,128)S(1)}) custom-call(f32[64,1024]{1,0:T(8,128)S(1)} %logit_grad.1.lg_ref.refs_0_, bf16[64,8192]{1,0:T(8,128)(2,1)S(1)} %copy-done.1, bf16[1024,128]{1,0:T(8,128)(2,1)S(1)} %copy-done.4, f32[64,64]{1,0:T(8,128)S(1)} %copy-done.11), custom_call_target="tpu_custom_call" | custom-call | tf_op jit(solution)/shard_map/grad_k/pallas_call | solution.py:304
  98.8 0.0 collective-permute-done.10.refs_1_
  98.8 0.3 collective-permute-done.9.refs_2_
  99.2 0.0 collective-permute-start.12
  99.2 2.7 %collective-permute-start.11 = (f32[4,128,128]{2,1,0:T(8,128)S(1)}, f32[4,128,128]{2,1,0:T(8,128)S(1)}, u32[]{:S(2)}, u32[]{:S(2)}) collective-permute-start(f32[4,128,128]{2,1,0:T(8,128)S(1)} %get-tuple-element.34), channel_id=1, source_target_pairs={{0,2},{1,3},{2,0},{3,1},{4,6},{5,7},{6,4},{7,5},{8,10},{9,11},{10,... | collective-permute-start | bytes 786440 | tf_op jit(solution)/shard_map/ppermute | solution.py:447
  101.9 0.2 collective-permute-start.15
  102.1 1.1 collective-permute-start.14
  103.2 0.8 collective-permute-start.13
  104.0 1.2 collective-permute-done.14.refs_12_
  105.3 1.7 %collective-permute-done.13.refs_11_ = f32[16,256]{1,0:T(8,128)S(1)} collective-permute-done((f32[16,256]{1,0:T(8,128)S(1)}, f32[16,256]{1,0:T(8,128)S(1)}, u32[]{:S(2)}, u32[]{:S(2)}) %collective-permute-start.13) | collective-permute-done | bytes 16416 | tf_op jit(solution)/shard_map/ppermute | solution.py:451
  106.9 0.0 collective-permute-done.12.refs_3_
  106.9 8.3 %grad_q.1 = f32[8,80,256]{2,1,0:T(8,128)} custom-call(f32[64,1024]{1,0:T(8,128)S(1)} %logit_grad.1.lg_ref.refs_0_, f32[64,1024]{1,0:T(8,128)S(1)} %collective-permute-done.10.refs_1_, f32[64,1024]{1,0:T(8,128)S(1)} %collective-permute-done.9.refs_2_, f32[64,1024]{1,0:T(8,128)S(1)} %collective-permute-done.12.refs_3_, bf16[1024,128]{1,0:T(8,128)(2,1)S(1)} %copy-done.4, ...), custom_call_target="tpu_custom_call" | custom-call | tf_op jit(solution)/shard_map/grad_q/pallas_call | solution.py:304
  115.3 0.0 collective-permute-done.11
  115.3 4.6 %all-to-all-start.1 = ((f32[8,80,256]{2,1,0:T(8,128)}), f32[8,80,256]{2,1,0:T(8,128)S(1)}, u32[]{:S(2)}, u32[]{:S(2)}) async-start(f32[8,80,256]{2,1,0:T(8,128)} %grad_q.1), calls=%async_computation.1 | async-start | bytes 1310720 | tf_op jit(solution)/shard_map/all_to_all | solution.py:501
  119.9 0.1 collective-permute-start.16
  120.0 5.0 %collective-permute-done.16 = f32[2,128,128]{2,1,0:T(8,128)S(1)} collective-permute-done((f32[2,128,128]{2,1,0:T(8,128)S(1)}, f32[2,128,128]{2,1,0:T(8,128)S(1)}, u32[]{:S(2)}, u32[]{:S(2)}) %collective-permute-start.16) | collective-permute-done | bytes 131104 | tf_op jit(solution)/shard_map/ppermute | solution.py:447
  125.0 1.6 %collective-permute-start.17 = (f32[128,128]{1,0:T(8,128)S(1)}, f32[128,128]{1,0:T(8,128)S(1)}, u32[]{:S(2)}, u32[]{:S(2)}) collective-permute-start(f32[128,128]{1,0:T(8,128)S(1)} %get-tuple-element.43), channel_id=1, source_target_pairs={{0,1},{1,0},{2,3},{3,2},{4,5},{5,4},{6,7},{7,6},{8,9},{9,8},{10,11... | collective-permute-start | bytes 196616 | tf_op jit(solution)/shard_map/ppermute | solution.py:447
  126.6 4.3 %collective-permute-done.17.got_ref = f32[128,128]{1,0:T(8,128)S(1)} collective-permute-done((f32[128,128]{1,0:T(8,128)S(1)}, f32[128,128]{1,0:T(8,128)S(1)}, u32[]{:S(2)}, u32[]{:S(2)}) %collective-permute-start.17) | collective-permute-done | bytes 65568 | tf_op jit(solution)/shard_map/ppermute | solution.py:447
  130.9 8.8 %all-to-all-done.1.parts_ref = f32[8,80,256]{2,1,0:T(8,128)S(1)} async-done(((f32[8,80,256]{2,1,0:T(8,128)}), f32[8,80,256]{2,1,0:T(8,128)S(1)}, u32[]{:S(2)}, u32[]{:S(2)}) %all-to-all-start.1) | async-done | bytes 655392 | tf_op jit(solution)/shard_map/all_to_all | solution.py:501
  139.7 0.8 finish.1
  (32 shorter events, 0.2 us)
Async XLA Ops:
  1.3 28.3 %copy-start.4 = (bf16[1024,128]{1,0:T(8,128)(2,1)S(1)}, bf16[1024,128]{1,0:T(8,128)(2,1)}, u32[]{:S(2)}) copy-start(bf16[1024,128]{1,0:T(8,128)(2,1)} %refs_4_.1) | copy-start | bytes 786436
  1.3 42.8 %copy-start = (bf16[1024,2048]{1,0:T(8,128)(2,1)S(1)}, bf16[1024,2048]{1,0:T(8,128)(2,1)}, u32[]{:S(2)}) copy-start(bf16[1024,2048]{1,0:T(8,128)(2,1)} %kn_ref.3) | copy-start | bytes 12582916
  1.3 42.8 %copy-start.2 = (bf16[512,2048]{1,0:T(8,128)(2,1)S(1)}, bf16[512,2048]{1,0:T(8,128)(2,1)}, u32[]{:S(2)}) copy-start(bf16[512,2048]{1,0:T(8,128)(2,1)} %qn_ref.3) | copy-start | bytes 6291460
  1.3 42.8 %copy-start.6 = (bf16[1024,64]{0,1:T(8,128)(2,1)S(1)}, bf16[1024,64]{0,1:T(8,128)(2,1)}, u32[]{:S(2)}) copy-start(bf16[1024,64]{0,1:T(8,128)(2,1)} %param.12) | copy-start | bytes 393220
  17.2 27.0 %copy-start.5 = (bf16[512,1024]{1,0:T(8,128)(2,1)S(1)}, bf16[512,1024]{1,0:T(8,128)(2,1)}, u32[]{:S(2)}) copy-start(bf16[512,1024]{1,0:T(8,128)(2,1)} %qr_ref.3) | copy-start | bytes 3145732
  17.2 1.5 %collective-permute-start = (f32[16,640]{1,0:T(8,128)}, f32[16,640]{1,0:T(8,128)S(1)}, u32[]{:S(2)}, u32[]{:S(2)}) collective-permute-start(f32[16,640]{1,0:T(8,128)} %get-tuple-element.23), channel_id=1, source_target_pairs={{0,8},{8,0},{16,24},{24,16},{32,40},{40,32},{48,56},{56,48},{64,72... | collective-permute-start | bytes 122888 | tf_op jit(solution)/shard_map/ppermute | solution.py:451
  19.5 4.1 %collective-permute-start.1 = (f32[16,640]{1,0:T(8,128)S(1)}, f32[16,640]{1,0:T(8,128)S(1)}, u32[]{:S(2)}, u32[]{:S(2)}) collective-permute-start(f32[16,640]{1,0:T(8,128)S(1)} %multiply_add_fusion.4), channel_id=1, source_target_pairs={{0,128},{8,136},{16,144},{24,152},{32,160},{40,168},{48,176},{56,1... | collective-permute-start | bytes 122888 | tf_op jit(solution)/shard_map/ppermute | solution.py:451
  23.6 7.7 %collective-permute-start.3 = (f32[16,640]{1,0:T(8,128)S(1)}, f32[16,640]{1,0:T(8,128)S(1)}, u32[]{:S(2)}, u32[]{:S(2)}) collective-permute-start(f32[16,640]{1,0:T(8,128)S(1)} %multiply_add_fusion.3), channel_id=1, source_target_pairs={{0,112},{8,120},{16,0},{24,8},{32,16},{40,24},{48,32},{56,40},{64,... | collective-permute-start | bytes 122888 | tf_op jit(solution)/shard_map/ppermute | solution.py:456
  29.5 5.2 %collective-permute-start.2 = (f32[16,640]{1,0:T(8,128)S(1)}, f32[16,640]{1,0:T(8,128)S(1)}, u32[]{:S(2)}, u32[]{:S(2)}) collective-permute-start(f32[16,640]{1,0:T(8,128)S(1)} %multiply_add_fusion.3), channel_id=1, source_target_pairs={{0,16},{8,24},{16,32},{24,40},{32,48},{40,56},{48,64},{56,72},{64,... | collective-permute-start | bytes 122888 | tf_op jit(solution)/shard_map/ppermute | solution.py:456
  29.6 14.0 %collective-permute-start.7 = (f32[1024,128]{1,0:T(8,128)S(1)}, f32[1024,128]{1,0:T(8,128)S(1)}, u32[]{:S(2)}, u32[]{:S(2)}) collective-permute-start(f32[1024,128]{1,0:T(8,128)S(1)} %convert_element_type.3), channel_id=1, source_target_pairs={{0,8},{8,0},{16,24},{24,16},{32,40},{40,32},{48,56},{56,48},{64,72... | collective-permute-start | bytes 1572872 | tf_op jit(solution)/shard_map/ppermute | solution.py:451
  29.7 14.4 %collective-permute-start.6 = (f32[1024,128]{1,0:T(8,128)S(1)}, f32[1024,128]{1,0:T(8,128)}, u32[]{:S(2)}, u32[]{:S(2)}) collective-permute-start(f32[1024,128]{1,0:T(8,128)S(1)} %convert_element_type.3), channel_id=1, source_target_pairs={{0,128},{8,136},{16,144},{24,152},{32,160},{40,168},{48,176},{56,1... | collective-permute-start | bytes 1572872 | tf_op jit(solution)/shard_map/ppermute | solution.py:451
  34.8 6.2 %collective-permute-start.5 = (f32[16,640]{1,0:T(8,128)S(1)}, f32[16,640]{1,0:T(8,128)S(1)}, u32[]{:S(2)}, u32[]{:S(2)}) collective-permute-start(f32[16,640]{1,0:T(8,128)S(1)} %get-tuple-element.46), channel_id=1, source_target_pairs={{0,80},{8,88},{16,96},{24,104},{32,112},{40,120},{48,0},{56,8},{64... | collective-permute-start | bytes 122888 | tf_op jit(solution)/shard_map/ppermute | solution.py:456
  35.6 8.0 %collective-permute-start.4 = (f32[16,640]{1,0:T(8,128)S(1)}, f32[16,640]{1,0:T(8,128)S(1)}, u32[]{:S(2)}, u32[]{:S(2)}) collective-permute-start(f32[16,640]{1,0:T(8,128)S(1)} %get-tuple-element.45), channel_id=1, source_target_pairs={{0,48},{8,56},{16,64},{24,72},{32,80},{40,88},{48,96},{56,104},{64... | collective-permute-start | bytes 122888 | tf_op jit(solution)/shard_map/ppermute | solution.py:456
  43.6 8.7 %copy-start.7 = (f32[1024,128]{1,0:T(8,128)}, f32[1024,128]{1,0:T(8,128)S(1)}, u32[]{:S(2)}) copy-start(f32[1024,128]{1,0:T(8,128)S(1)} %collective-permute-done.7.refs_5_) | copy-start | bytes 1572868
  52.3 1.4 copy-start.3
  53.7 35.6 %all-to-all-start = ((f32[8,64,1024]{2,1,0:T(8,128)}), f32[8,64,1024]{2,1,0:T(8,128)S(1)}, u32[]{:S(2)}, u32[]{:S(2)}) async-start(f32[8,64,1024]{2,1,0:T(8,128)} %bitcast.7), calls=%async_computation | async-start | bytes 4194304 | tf_op jit(solution)/shard_map/all_to_all | solution.py:485
  61.1 30.3 %copy-start.1 = (bf16[64,8192]{1,0:T(8,128)(2,1)S(1)}, bf16[64,8192]{1,0:T(8,128)(2,1)}, u32[]{:S(2)}) copy-start(bf16[64,8192]{1,0:T(8,128)(2,1)} %refs_8_.1) | copy-start | bytes 3145732
  61.1 30.3 %copy-start.11 = (f32[64,64]{1,0:T(8,128)S(1)}, f32[64,64]{1,0:T(8,128)}, u32[]{:S(2)}) copy-start(f32[64,64]{1,0:T(8,128)} %refs_9_.1) | copy-start | bytes 49156
  61.1 2.1 %collective-permute-start.8 = (f32[1024,128]{1,0:T(8,128)}, f32[1024,128]{1,0:T(8,128)S(1)}, u32[]{:S(2)}, u32[]{:S(2)}) collective-permute-start(f32[1024,128]{1,0:T(8,128)} %collective-permute-done.6.refs_6_), channel_id=1, source_target_pairs={{0,8},{8,0},{16,24},{24,16},{32,40},{40,32},{48,56},{56,48},{64,72... | collective-permute-start | bytes 1572872 | tf_op jit(solution)/shard_map/ppermute | solution.py:451
  63.2 0.8 copy-start.9
  89.2 1.0 copy-start.12
  90.2 16.7 %copy-start.8 = (f32[1024,128]{1,0:T(8,128)S(1)}, f32[1024,128]{1,0:T(8,128)}, u32[]{:S(2)}) copy-start(f32[1024,128]{1,0:T(8,128)} %copy-done.7) | copy-start | bytes 1572868
  90.2 16.7 %copy-start.10 = (f32[1024,128]{1,0:T(8,128)S(1)}, f32[1024,128]{1,0:T(8,128)}, u32[]{:S(2)}) copy-start(f32[1024,128]{1,0:T(8,128)} %copy-done.9) | copy-start | bytes 1572868
  90.3 8.5 %collective-permute-start.10 = (f32[64,1024]{1,0:T(8,128)S(1)}, f32[64,1024]{1,0:T(8,128)S(1)}, u32[]{:S(2)}, u32[]{:S(2)}) collective-permute-start(f32[64,1024]{1,0:T(8,128)S(1)} %logit_grad.1.lg_ref.refs_0_), channel_id=1, source_target_pairs={{0,8},{8,0},{16,24},{24,16},{32,40},{40,32},{48,56},{56,48},{64,72... | collective-permute-start | bytes 786440 | tf_op jit(solution)/shard_map/ppermute | solution.py:451
  90.4 8.7 %collective-permute-start.9 = (f32[64,1024]{1,0:T(8,128)S(1)}, f32[64,1024]{1,0:T(8,128)S(1)}, u32[]{:S(2)}, u32[]{:S(2)}) collective-permute-start(f32[64,1024]{1,0:T(8,128)S(1)} %logit_grad.1.lg_ref.refs_0_), channel_id=1, source_target_pairs={{0,128},{8,136},{16,144},{24,152},{32,160},{40,168},{48,176},{56,1... | collective-permute-start | bytes 786440 | tf_op jit(solution)/shard_map/ppermute | solution.py:451
  99.2 7.8 %collective-permute-start.12 = (f32[64,1024]{1,0:T(8,128)S(1)}, f32[64,1024]{1,0:T(8,128)S(1)}, u32[]{:S(2)}, u32[]{:S(2)}) collective-permute-start(f32[64,1024]{1,0:T(8,128)S(1)} %collective-permute-done.9.refs_2_), channel_id=1, source_target_pairs={{0,8},{8,0},{16,24},{24,16},{32,40},{40,32},{48,56},{56,48},{64,72... | collective-permute-start | bytes 786440 | tf_op jit(solution)/shard_map/ppermute | solution.py:451
  99.2 16.1 %collective-permute-start.11 = (f32[4,128,128]{2,1,0:T(8,128)S(1)}, f32[4,128,128]{2,1,0:T(8,128)S(1)}, u32[]{:S(2)}, u32[]{:S(2)}) collective-permute-start(f32[4,128,128]{2,1,0:T(8,128)S(1)} %get-tuple-element.34), channel_id=1, source_target_pairs={{0,2},{1,3},{2,0},{3,1},{4,6},{5,7},{6,4},{7,5},{8,10},{9,11},{10,... | collective-permute-start | bytes 786440 | tf_op jit(solution)/shard_map/ppermute | solution.py:447
  101.9 2.1 %collective-permute-start.15 = (f32[16,256]{1,0:T(8,128)S(1)}, f32[16,256]{1,0:T(8,128)S(1)}, u32[]{:S(2)}, u32[]{:S(2)}) collective-permute-start(f32[16,256]{1,0:T(8,128)S(1)} %get-tuple-element.39.refs_10_), channel_id=1, source_target_pairs={{0,8},{8,0},{16,24},{24,16},{32,40},{40,32},{48,56},{56,48},{64,72... | collective-permute-start | bytes 49160 | tf_op jit(solution)/shard_map/ppermute | solution.py:451
  102.1 3.2 %collective-permute-start.14 = (f32[16,256]{1,0:T(8,128)S(1)}, f32[16,256]{1,0:T(8,128)S(1)}, u32[]{:S(2)}, u32[]{:S(2)}) collective-permute-start(f32[16,256]{1,0:T(8,128)S(1)} %get-tuple-element.39.refs_10_), channel_id=1, source_target_pairs={{0,136},{8,128},{16,152},{24,144},{32,168},{40,160},{48,184},{56,1... | collective-permute-start | bytes 49160 | tf_op jit(solution)/shard_map/ppermute | solution.py:451
  103.2 3.7 %collective-permute-start.13 = (f32[16,256]{1,0:T(8,128)S(1)}, f32[16,256]{1,0:T(8,128)S(1)}, u32[]{:S(2)}, u32[]{:S(2)}) collective-permute-start(f32[16,256]{1,0:T(8,128)S(1)} %get-tuple-element.39.refs_10_), channel_id=1, source_target_pairs={{0,128},{8,136},{16,144},{24,152},{32,160},{40,168},{48,176},{56,1... | collective-permute-start | bytes 49160 | tf_op jit(solution)/shard_map/ppermute | solution.py:451
  115.3 24.4 %all-to-all-start.1 = ((f32[8,80,256]{2,1,0:T(8,128)}), f32[8,80,256]{2,1,0:T(8,128)S(1)}, u32[]{:S(2)}, u32[]{:S(2)}) async-start(f32[8,80,256]{2,1,0:T(8,128)} %grad_q.1), calls=%async_computation.1 | async-start | bytes 1310720 | tf_op jit(solution)/shard_map/all_to_all | solution.py:501
  119.9 5.1 %collective-permute-start.16 = (f32[2,128,128]{2,1,0:T(8,128)S(1)}, f32[2,128,128]{2,1,0:T(8,128)S(1)}, u32[]{:S(2)}, u32[]{:S(2)}) collective-permute-start(f32[2,128,128]{2,1,0:T(8,128)S(1)} %slice_add_fusion), channel_id=1, source_target_pairs={{0,6},{1,7},{2,4},{3,5},{4,2},{5,3},{6,0},{7,1},{8,14},{9,15},{10,... | collective-permute-start | bytes 393224 | tf_op jit(solution)/shard_map/ppermute | solution.py:447
  125.0 5.9 %collective-permute-start.17 = (f32[128,128]{1,0:T(8,128)S(1)}, f32[128,128]{1,0:T(8,128)S(1)}, u32[]{:S(2)}, u32[]{:S(2)}) collective-permute-start(f32[128,128]{1,0:T(8,128)S(1)} %get-tuple-element.43), channel_id=1, source_target_pairs={{0,1},{1,0},{2,3},{3,2},{4,5},{5,4},{6,7},{7,6},{8,9},{9,8},{10,11... | collective-permute-start | bytes 196616 | tf_op jit(solution)/shard_map/ppermute | solution.py:447

commit v5 on v4

--- a/solution.py
+++ b/solution.py
@@ -141,7 +141,10 @@
         out_ref[:, queries:] = jnp.concatenate(row, axis=1)
 
 
-def probs_kernel(lse_ref, krt_ref, qn_ref, qr_ref, kn_ref, out_hbm, krp, s_ref, acc, sems):
+def probs_kernel(
+    lse_ref, logits_hbm, krt_ref, qn_ref, qr_ref, kn_ref, out_hbm, index_ref,
+    krp, s_ref, acc, logits_ref, sems,
+):
     step = pl.program_id(0)
     last = pl.num_programs(0) - 1
     queries, keys = acc.shape
@@ -151,6 +154,7 @@
     def _():
         fill_rope(krt_ref, krp)
         acc[...] = jnp.zeros_like(acc)
+        pltpu.make_async_copy(logits_hbm, logits_ref, sems.at[N_HEAD]).start()
 
     lse = []
     for p in range(2):
@@ -172,21 +176,22 @@
             copies.append(pltpu.make_async_copy(acc.at[rows], out_hbm.at[rows], sems.at[h]))
         for copy in copies:
             copy.start()
+        pltpu.make_async_copy(logits_hbm, logits_ref, sems.at[N_HEAD]).wait()
+        logits = logits_ref[...]
+        top = lanes_of(column(lse_ref[:1, queries:])[:size], keys)
+        index_ref[...] = jnp.where(logits > 0.5 * NEG, jnp.exp2(logits - top), -1.0)
         for copy in copies:
             copy.wait()
 
 
-def lg_kernel(lse_ref, logits_ref, target_ref, lg_ref):
-    rows, width = lg_ref.shape
-    lse = column(lse_ref[:1, lse_ref.shape[1] - 128 :])[:rows]
-    for c in range(width // 128):
+def lg_kernel(index_ref, target_ref, lg_ref):
+    for c in range(lg_ref.shape[1] // 128):
         cols = slice(c * 128, (c + 1) * 128)
         target = target_ref[0, :, cols]
         for h in range(1, N_HEAD):
             target = target + target_ref[h, :, cols]
-        logits = logits_ref[:, cols]
-        lg = jnp.exp2(logits - lse) - target * (1.0 / HEADS)
-        lg_ref[:, cols] = jnp.where(logits > 0.5 * NEG, lg, 0.0)
+        prob = index_ref[:, cols]
+        lg_ref[:, cols] = jnp.where(prob >= 0.0, prob - target * (1.0 / HEADS), 0.0)
 
 
 def gk_kernel(
@@ -232,8 +237,8 @@
 
 
 def gq_kernel(*refs):
-    lgs, iks, (iq_ref, w_ref), gws = refs[:4], refs[4:8], refs[8:10], refs[10:14]
-    gq_ref, wb, lg_ref, ikb_ref, q_ref, g_ref = refs[14:]
+    lgs, iks, (iq_ref, w_ref) = refs[:4], refs[4:8], refs[8:10]
+    gq_ref, wt, lg_ref, ikb_ref, q_ref, g_ref = refs[10:]
     source = pl.program_id(0)
     rows, keys = lgs[0].shape
     count = q_ref.shape[0] // rows
@@ -242,7 +247,7 @@
 
     @pl.when(source == 0)
     def _():
-        fill_weights(w_ref, wb)
+        wt[...] = w_ref[...].T * INV_ROOT
         g_ref[...] = jnp.zeros_like(g_ref)
         for i in range(4):
             lg_ref[i] = lgs[i][...]
@@ -260,14 +265,19 @@
 
     @pl.when(source == 3)
     def _():
-        gw = (gws[0][...] + gws[1][...]) + (gws[2][...] + gws[3][...])
         for i in range(N_Z):
             pair = []
             for n in range(2):
                 at = (2 * i + n) * rows
-                pair.append(g_ref[at : at + rows, :] * wb[dests[i] * 2 + n] * INV_ROOT)
+                weight = column(wt[pl.ds(dests[i] * 2 + n, 1), :])
+                pair.append(g_ref[at : at + rows, :] * weight)
             gq_ref[i, :rows, :] = jnp.concatenate(pair, axis=1)
-            gq_ref[i, rows:, :] = gw
+
+
+def gw_rows_kernel(gw0, gw1, gw2, gw3, gq_ref, out_ref):
+    gw = (gw0[...] + gw1[...]) + (gw2[...] + gw3[...])
+    for i in range(N_Z):
+        out_ref[i] = gw
 
 
 def finish_kernel(parts_ref, mine_ref, got_ref, gq_ref, gk_ref, gw_ref):
@@ -350,35 +360,41 @@
     )
 
 
-def run_probs(lse, qn, qr, kn, krt):
+def run_probs(lse, logits, qn, qr, kn, krt):
     queries, keys, pairs = qn.shape[0], kn.shape[0], qn.shape[1] // 256
     return call(
         probs_kernel,
         "main_probs",
         (pairs,),
-        (lse, krt, qn, qr, kn),
-        [*wholes([lse, krt]), *main_specs(queries, keys)],
-        floats((queries, keys)),
-        [pl.BlockSpec(memory_space=pltpu.HBM)],
+        (lse, logits, krt, qn, qr, kn),
+        [
+            whole(lse.shape),
+            pl.BlockSpec(memory_space=pltpu.HBM),
+            whole(krt.shape),
+            *main_specs(queries, keys),
+        ],
+        floats((queries, keys), logits.shape),
+        [pl.BlockSpec(memory_space=pltpu.HBM), whole(logits.shape)],
         [
             pltpu.VMEM((2, keys, 128), BF16),
             pltpu.VMEM((2, queries, keys), F32),
             pltpu.VMEM((queries, keys), F32),
-            pltpu.SemaphoreType.DMA((N_HEAD,)),
+            pltpu.VMEM(logits.shape, F32),
+            pltpu.SemaphoreType.DMA((N_HEAD + 1,)),
         ],
         24,
-    )[0]
-
-
-def run_lg(lse, logits, target):
+    )
+
+
+def run_lg(index_probs, target):
     return pl.pallas_call(
         lg_kernel,
-        in_specs=[in_vmem()] * 3,
+        in_specs=[in_vmem()] * 2,
         out_specs=in_vmem(),
-        out_shape=floats(logits.shape)[0],
+        out_shape=floats(index_probs.shape)[0],
         compiler_params=pltpu.CompilerParams(vmem_limit_bytes=8 * 1024 * 1024),
         name="logit_grad",
-    )(lse, logits, target)
+    )(index_probs, target)
 
 
 def run_gk(lg, iq, ik, w):
@@ -408,10 +424,10 @@
     )
 
 
-def run_gq(lgs, iks, iq, w, gws):
+def run_gq(lgs, iks, iq, w):
     rows, keys = lgs[0].shape
     shape = (N_Z, rows + 16, 256)
-    ins = [*lgs, *iks, iq, w, *gws]
+    ins = [*lgs, *iks, iq, w]
     return call(
         gq_kernel,
         "grad_q",
@@ -421,7 +437,7 @@
         floats(shape),
         [whole(shape)],
         [
-            pltpu.VMEM((IDX_HEADS, rows, 128), F32),
+            pltpu.VMEM(w.shape, F32),
             pltpu.VMEM((4, rows, keys), F32),
             pltpu.VMEM((4, keys, IDX_DIM), BF16),
             pltpu.VMEM((2 * N_Z * rows, IDX_DIM), BF16),
@@ -429,6 +445,20 @@
         ],
         28,
     )[0]
+
+
+def run_gw_rows(parts, gws):
+    rows = gws[0].shape[0]
+    return pl.pallas_call(
+        gw_rows_kernel,
+        grid=(1,),
+        in_specs=[*wholes(gws), pl.BlockSpec(memory_space=pl.ANY)],
+        out_specs=pl.BlockSpec((N_Z, rows, 256), lambda i: (0, 64 // rows, 0)),
+        out_shape=floats(parts.shape)[0],
+        input_output_aliases={4: 0},
+        compiler_params=pltpu.CompilerParams(vmem_limit_bytes=8 * 1024 * 1024),
+        name="grad_w_rows",
+    )(*gws, parts)
 
 
 def run_finish(*ins):
@@ -479,21 +509,22 @@
     lse, ik_later = lax.optimization_barrier((lse, ik))
     ikf = ik_later.astype(F32)
     ikf_y, ikf_c = ctx_xor(ikf, 16), ctx_xor(ikf, 1)
-    lse, ikf_y, ikf_c = lax.optimization_barrier((over_z(lse), ikf_y, ikf_c))
-    probs = run_probs(lse, qn, qr, kn, krt)
+    lse, ikf_c = lax.optimization_barrier((over_z(lse), ikf_c))
+    probs, index_probs = run_probs(lse, logits, qn, qr, kn, krt)
     probs, ikf_y = lax.optimization_barrier((probs, ikf_y))
     target = lax.all_to_all(probs.reshape(N_HEAD, -1, probs.shape[1]), "head", 0, 0)
     ikf_yc = ctx_xor(ikf_y, 1)
     target, ikf_yc = lax.optimization_barrier((target, ikf_yc))
 
-    lg = run_lg(lse, logits, target)
+    lg = run_lg(index_probs, target)
     lg_y, lg_c = ctx_xor(lg, 16), ctx_xor(lg, 1)
     keep, send, gw = run_gk(lg, iq, ik, w)
     lg_y, lg_c, send, gw = lax.optimization_barrier((lg_y, lg_c, send, gw))
     lg_yc = ctx_xor(lg_y, 1)
     gws = [gw, *[ctx_xor(gw, bits) for bits in (16, 17, 1)]]
     got = head_xor(send, 2)
-    parts = run_gq([lg, lg_c, lg_y, lg_yc], [ik, ikf_c, ikf_y, ikf_yc], iq, w, gws)
+    parts = run_gq([lg, lg_c, lg_y, lg_yc], [ik, ikf_c, ikf_y, ikf_yc], iq, w)
+    parts = run_gw_rows(parts, gws)
     got, parts = lax.optimization_barrier((got, parts))
     got = head_xor(keep[2:] + got[2:], 6) + (keep[:2] + got[:2])
     got, mine = head_xor(got[1], 1), got[0]

time: 142 us -> 137 us (0.965)
  waiting for transfers between devices: 61.2 us -> 55.1 us
  local copies, waits for them, and re-layouts: 3.16 us -> 5.56 us
    all_to_all x1, waiting for transfers between devices: 25.2 us -> 20.5 us  [per_device(): lax.all_to_all(probs.reshape(N_HEAD, -1, probs.shape[1]), 'head', 0, 0)]
    ppermute x11, waiting for transfers between devices: 9.74 us -> 6.8 us  [ctx_xor(): return lax.ppermute(value, 'ctx', [(i, i ^ bits) for i in range(N_CTX)])]
    unnamed x26 -> x30, local copies, waits for them, and re-layouts: 3.14 us -> 5.54 us
  transfers between devices with their start and end apart: 20 -> 20, of which waited for: 14 -> 11; matrix products, arithmetic and copies ran while one was open for 0% -> 0% of each run, Pallas kernels for 11% -> 18%
where the time goes in v5:
time: 137 us; the launch traced here: 136 us
  waiting for transfers between devices  55.1 us (40%)
  Pallas kernels  41.1 us (30%)
  starting transfers between devices  31.7 us (23%)
  local copies, waits for them, and re-layouts  5.56 us (4%)
  between operations  1.47 us (1%)
    pallas_call x4, Pallas kernels, call(): pl.pallas_call(kernel, grid=grid, in_specs=in_specs, out_specs=out_specs,...  39.4 us
    all_to_all x1, waiting for transfers between devices, per_device(): lax.all_to_all(probs.reshape(N_HEAD, -1, probs.shape[1]), 'head', 0, 0)  20.5 us
    ppermute x3, waiting for transfers between devices, head_xor(): return lax.ppermute(value, 'head', [(i, i ^ bits) for i in range(N_HEAD)])  10.3 us
    ppermute x4, starting transfers between devices, z_shift(): return lax.ppermute(value, 'ctx', list(enumerate(to)))  9.83 us
    all_to_all x1, waiting for transfers between devices, per_device(): parts = lax.all_to_all(parts, 'ctx', 0, 0, axis_index_groups=groups)  9.34 us
    ppermute x4, waiting for transfers between devices, z_shift(): return lax.ppermute(value, 'ctx', list(enumerate(to)))  8.23 us
    all_to_all x1, starting transfers between devices, per_device(): lax.all_to_all(probs.reshape(N_HEAD, -1, probs.shape[1]), 'head', 0, 0)  7.33 us
    ppermute x11, waiting for transfers between devices, ctx_xor(): return lax.ppermute(value, 'ctx', [(i, i ^ bits) for i in range(N_CTX)])  6.8 us
  transfers between devices with their start and end apart: 20, of which 11 were waited for; matrix products, arithmetic and copies ran while one was open for 0% of the time, Pallas kernels for 18%

profile of v5, /device:TPU:2, one launch (start us, length us, event | category | flops | bytes accessed | tf_op | source)
XLA Modules:
  0.0 135.9 jit_solution(12260667910869048195)
XLA Ops:
  1.3 15.8 %front.1 = (f32[16,640]{1,0:T(8,128)}, f32[64,1024]{1,0:T(8,128)}) custom-call(s32[1]{0:T(128)S(6)} %copy.14.base_ref, s32[1,512]{1,0:T(1,128)} %bitcast.10, bf16[64,1024]{1,0:T(8,128)(2,1)} %bitcast.8, bf16[1024,128]{1,0:T(8,128)(2,1)} %refs_4_.1, f32[64,64]{1,0:T(8,128)} %refs_9_.1, bf16[64,8192]{1,0:T(8,128)(2,1)} %refs_8_.1, bf16[512,2048]{1,0:T(8,128)(2,1)} %qn_ref.3, ...), custom_call_target="tpu_custom_call" | custom-call | tf_op jit(solution)/shard_map/front/pallas_call | solution.py:314
  17.2 0.1 collective-permute-start
  17.2 1.4 %collective-permute-done = f32[16,640]{1,0:T(8,128)S(1)} collective-permute-done((f32[16,640]{1,0:T(8,128)}, f32[16,640]{1,0:T(8,128)S(1)}, u32[]{:S(2)}, u32[]{:S(2)}) %collective-permute-start) | collective-permute-done | bytes 40992 | tf_op jit(solution)/shard_map/ppermute | solution.py:481
  18.7 0.8 multiply_add_fusion.4
  19.5 1.7 %collective-permute-start.1 = (f32[16,640]{1,0:T(8,128)S(1)}, f32[16,640]{1,0:T(8,128)S(1)}, u32[]{:S(2)}, u32[]{:S(2)}) collective-permute-start(f32[16,640]{1,0:T(8,128)S(1)} %multiply_add_fusion.4), channel_id=1, source_target_pairs={{0,128},{8,136},{16,144},{24,152},{32,160},{40,168},{48,176},{56,1... | collective-permute-start | bytes 122888 | tf_op jit(solution)/shard_map/ppermute | solution.py:481
  21.1 2.4 %collective-permute-done.1 = f32[16,640]{1,0:T(8,128)S(1)} collective-permute-done((f32[16,640]{1,0:T(8,128)S(1)}, f32[16,640]{1,0:T(8,128)S(1)}, u32[]{:S(2)}, u32[]{:S(2)}) %collective-permute-start.1) | collective-permute-done | bytes 40992 | tf_op jit(solution)/shard_map/ppermute | solution.py:481
  23.6 5.9 %collective-permute-start.3 = (f32[16,640]{1,0:T(8,128)S(1)}, f32[16,640]{1,0:T(8,128)S(1)}, u32[]{:S(2)}, u32[]{:S(2)}) collective-permute-start(f32[16,640]{1,0:T(8,128)S(1)} %multiply_add_fusion.3), channel_id=1, source_target_pairs={{0,112},{8,120},{16,0},{24,8},{32,16},{40,24},{48,32},{56,40},{64,... | collective-permute-start | bytes 122888 | tf_op jit(solution)/shard_map/ppermute | solution.py:486
  29.5 0.0 collective-permute-start.2
  29.6 0.1 collective-permute-start.6
  29.7 1.7 %collective-permute-start.7 = (f32[1024,128]{1,0:T(8,128)S(1)}, f32[1024,128]{1,0:T(8,128)}, u32[]{:S(2)}, u32[]{:S(2)}) collective-permute-start(f32[1024,128]{1,0:T(8,128)S(1)} %convert_element_type.3), channel_id=1, source_target_pairs={{0,128},{8,136},{16,144},{24,152},{32,160},{40,168},{48,176},{56,1... | collective-permute-start | bytes 1572872 | tf_op jit(solution)/shard_map/ppermute | solution.py:481
  31.3 0.0 collective-permute-done.3
  31.3 3.4 %collective-permute-done.2 = f32[16,640]{1,0:T(8,128)S(1)} collective-permute-done((f32[16,640]{1,0:T(8,128)S(1)}, f32[16,640]{1,0:T(8,128)S(1)}, u32[]{:S(2)}, u32[]{:S(2)}) %collective-permute-start.2) | collective-permute-done | bytes 40992 | tf_op jit(solution)/shard_map/ppermute | solution.py:486
  34.7 0.1 multiply_add_fusion.2
  34.8 0.8 collective-permute-start.5
  35.6 3.1 %collective-permute-start.4 = (f32[16,640]{1,0:T(8,128)S(1)}, f32[16,640]{1,0:T(8,128)S(1)}, u32[]{:S(2)}, u32[]{:S(2)}) collective-permute-start(f32[16,640]{1,0:T(8,128)S(1)} %get-tuple-element.47), channel_id=1, source_target_pairs={{0,48},{8,56},{16,64},{24,72},{32,80},{40,88},{48,96},{56,104},{64... | collective-permute-start | bytes 122888 | tf_op jit(solution)/shard_map/ppermute | solution.py:486
  38.7 2.3 %collective-permute-done.5 = f32[16,640]{1,0:T(8,128)S(1)} collective-permute-done((f32[16,640]{1,0:T(8,128)S(1)}, f32[16,640]{1,0:T(8,128)S(1)}, u32[]{:S(2)}, u32[]{:S(2)}) %collective-permute-start.5) | collective-permute-done | bytes 40992 | tf_op jit(solution)/shard_map/ppermute | solution.py:486
  41.0 2.6 %collective-permute-done.4 = f32[16,640]{1,0:T(8,128)S(1)} collective-permute-done((f32[16,640]{1,0:T(8,128)S(1)}, f32[16,640]{1,0:T(8,128)S(1)}, u32[]{:S(2)}, u32[]{:S(2)}) %collective-permute-start.4) | collective-permute-done | bytes 40992 | tf_op jit(solution)/shard_map/ppermute | solution.py:486
  43.6 0.8 copy-done.7
  44.4 0.9 copy-done.12
  45.3 8.2 %main_probs.1 = (f32[512,1024]{1,0:T(8,128)S(1)}, f32[64,1024]{1,0:T(8,128)S(1)}) custom-call(f32[16,640]{1,0:T(8,128)S(1)} %multiply_add_fusion.lse_ref, f32[64,1024]{1,0:T(8,128)S(1)} %copy-done.12, bf16[64,1024]{1,0:T(8,128)(2,1)S(1)} %bitcast.9, bf16[512,2048]{1,0:T(8,128)(2,1)S(1)} %copy-done.2, bf16[512,1024]{1,0:T(8,128)(2,1)S(1)} %copy-done.3, ...), custom_call_target="tpu_custom_call" | custom-call | tf_op jit(solution)/shard_map/main_probs/pallas_call | solution.py:314
  53.6 1.3 copy-done.5
  55.0 0.7 copy-done.13
  55.7 0.0 collective-permute-done.7.refs_6_
  55.7 7.3 %all-to-all-start = ((f32[8,64,1024]{2,1,0:T(8,128)}), f32[8,64,1024]{2,1,0:T(8,128)S(1)}, u32[]{:S(2)}, u32[]{:S(2)}) async-start(f32[8,64,1024]{2,1,0:T(8,128)} %bitcast.7), calls=%async_computation | async-start | bytes 4194304 | tf_op jit(solution)/shard_map/all_to_all | solution.py:515
  63.0 0.0 collective-permute-start.8
  63.0 2.1 %collective-permute-done.8.refs_7_ = f32[1024,128]{1,0:T(8,128)S(1)} collective-permute-done((f32[1024,128]{1,0:T(8,128)}, f32[1024,128]{1,0:T(8,128)S(1)}, u32[]{:S(2)}, u32[]{:S(2)}) %collective-permute-start.8) | collective-permute-done | bytes 524320 | tf_op jit(solution)/shard_map/ppermute | solution.py:481
  65.1 0.8 copy-done.9
  65.9 20.5 %all-to-all-done.target_ref = f32[8,64,1024]{2,1,0:T(8,128)S(1)} async-done(((f32[8,64,1024]{2,1,0:T(8,128)}), f32[8,64,1024]{2,1,0:T(8,128)S(1)}, u32[]{:S(2)}, u32[]{:S(2)}) %all-to-all-start) | async-done | bytes 2097184 | tf_op jit(solution)/shard_map/all_to_all | solution.py:515
  86.4 0.9 copy-done.14
  87.3 0.2 logit_grad.1.lg_ref.refs_0_
  87.5 0.1 collective-permute-start.10
  87.6 0.5 collective-permute-start.9
  88.1 7.4 %grad_k.1 = (f32[4,128,128]{2,1,0:T(8,128)S(1)}, f32[4,128,128]{2,1,0:T(8,128)S(1)}, f32[16,256]{1,0:T(8,128)S(1)}) custom-call(f32[64,1024]{1,0:T(8,128)S(1)} %logit_grad.1.lg_ref.refs_0_, bf16[64,8192]{1,0:T(8,128)(2,1)S(1)} %copy-done.1, bf16[1024,128]{1,0:T(8,128)(2,1)S(1)} %copy-done.4, f32[64,64]{1,0:T(8,128)S(1)} %copy-done.11), custom_call_target="tpu_custom_call" | custom-call | tf_op jit(solution)/shard_map/grad_k/pallas_call | solution.py:314
  95.5 0.0 collective-permute-done.10.refs_1_
  95.5 0.8 collective-permute-done.9.refs_2_
  96.3 2.3 %collective-permute-start.11 = (f32[4,128,128]{2,1,0:T(8,128)S(1)}, f32[4,128,128]{2,1,0:T(8,128)S(1)}, u32[]{:S(2)}, u32[]{:S(2)}) collective-permute-start(f32[4,128,128]{2,1,0:T(8,128)S(1)} %get-tuple-element.36), channel_id=1, source_target_pairs={{0,2},{1,3},{2,0},{3,1},{4,6},{5,7},{6,4},{7,5},{8,10},{9,11},{10,... | collective-permute-start | bytes 786440 | tf_op jit(solution)/shard_map/ppermute | solution.py:477
  98.7 0.2 collective-permute-start.14
  98.9 1.1 collective-permute-start.13
  100.0 0.8 collective-permute-start.12
  100.8 8.0 %grad_q.1.gq_ref = f32[8,80,256]{2,1,0:T(8,128)} custom-call(f32[64,1024]{1,0:T(8,128)S(1)} %logit_grad.1.lg_ref.refs_0_, f32[64,1024]{1,0:T(8,128)S(1)} %collective-permute-done.10.refs_1_, f32[64,1024]{1,0:T(8,128)S(1)} %collective-permute-done.9.refs_2_, f32[64,1024]{1,0:T(8,128)S(1)} %collective-permute-done.15.refs_3_, bf16[1024,128]{1,0:T(8,128)(2,1)S(1)} %copy-done.4, ...), custom_call_target="tpu_custom_call" | custom-call | tf_op jit(solution)/shard_map/grad_q/pallas_call | solution.py:314
  108.8 0.7 grad_w_rows.1
  109.5 5.3 %all-to-all-start.1 = ((f32[8,80,256]{2,1,0:T(8,128)}), f32[8,80,256]{2,1,0:T(8,128)S(1)}, u32[]{:S(2)}, u32[]{:S(2)}) async-start(f32[8,80,256]{2,1,0:T(8,128)} %grad_w_rows.1), calls=%async_computation.1 | async-start | bytes 1310720 | tf_op jit(solution)/shard_map/all_to_all | solution.py:532
  114.8 0.1 collective-permute-start.16
  114.9 5.1 %collective-permute-done.16 = f32[2,128,128]{2,1,0:T(8,128)S(1)} collective-permute-done((f32[2,128,128]{2,1,0:T(8,128)S(1)}, f32[2,128,128]{2,1,0:T(8,128)S(1)}, u32[]{:S(2)}, u32[]{:S(2)}) %collective-permute-start.16) | collective-permute-done | bytes 131104 | tf_op jit(solution)/shard_map/ppermute | solution.py:477
  120.0 0.6 collective-permute-start.17
  120.6 5.2 %collective-permute-done.17.got_ref = f32[128,128]{1,0:T(8,128)S(1)} collective-permute-done((f32[128,128]{1,0:T(8,128)S(1)}, f32[128,128]{1,0:T(8,128)S(1)}, u32[]{:S(2)}, u32[]{:S(2)}) %collective-permute-start.17) | collective-permute-done | bytes 65568 | tf_op jit(solution)/shard_map/ppermute | solution.py:477
  125.8 9.3 %all-to-all-done.1.parts_ref = f32[8,80,256]{2,1,0:T(8,128)S(1)} async-done(((f32[8,80,256]{2,1,0:T(8,128)}), f32[8,80,256]{2,1,0:T(8,128)S(1)}, u32[]{:S(2)}, u32[]{:S(2)}) %all-to-all-start.1) | async-done | bytes 655392 | tf_op jit(solution)/shard_map/all_to_all | solution.py:532
  135.1 0.8 finish.1
  (37 shorter events, 0.2 us)
Async XLA Ops:
  1.3 28.3 %copy-start.4 = (bf16[1024,128]{1,0:T(8,128)(2,1)S(1)}, bf16[1024,128]{1,0:T(8,128)(2,1)}, u32[]{:S(2)}) copy-start(bf16[1024,128]{1,0:T(8,128)(2,1)} %refs_4_.1) | copy-start | bytes 786436
  1.3 43.1 %copy-start = (bf16[1024,2048]{1,0:T(8,128)(2,1)S(1)}, bf16[1024,2048]{1,0:T(8,128)(2,1)}, u32[]{:S(2)}) copy-start(bf16[1024,2048]{1,0:T(8,128)(2,1)} %kn_ref.3) | copy-start | bytes 12582916
  1.3 43.1 %copy-start.2 = (bf16[512,2048]{1,0:T(8,128)(2,1)S(1)}, bf16[512,2048]{1,0:T(8,128)(2,1)}, u32[]{:S(2)}) copy-start(bf16[512,2048]{1,0:T(8,128)(2,1)} %qn_ref.3) | copy-start | bytes 6291460
  1.3 43.1 %copy-start.6 = (bf16[1024,64]{0,1:T(8,128)(2,1)S(1)}, bf16[1024,64]{0,1:T(8,128)(2,1)}, u32[]{:S(2)}) copy-start(bf16[1024,64]{0,1:T(8,128)(2,1)} %param.12) | copy-start | bytes 393220
  17.2 27.2 %copy-start.3 = (bf16[512,1024]{1,0:T(8,128)(2,1)S(1)}, bf16[512,1024]{1,0:T(8,128)(2,1)}, u32[]{:S(2)}) copy-start(bf16[512,1024]{1,0:T(8,128)(2,1)} %qr_ref.3) | copy-start | bytes 3145732
  17.2 1.5 %collective-permute-start = (f32[16,640]{1,0:T(8,128)}, f32[16,640]{1,0:T(8,128)S(1)}, u32[]{:S(2)}, u32[]{:S(2)}) collective-permute-start(f32[16,640]{1,0:T(8,128)} %get-tuple-element.24), channel_id=1, source_target_pairs={{0,8},{8,0},{16,24},{24,16},{32,40},{40,32},{48,56},{56,48},{64,72... | collective-permute-start | bytes 122888 | tf_op jit(solution)/shard_map/ppermute | solution.py:481
  19.5 4.1 %collective-permute-start.1 = (f32[16,640]{1,0:T(8,128)S(1)}, f32[16,640]{1,0:T(8,128)S(1)}, u32[]{:S(2)}, u32[]{:S(2)}) collective-permute-start(f32[16,640]{1,0:T(8,128)S(1)} %multiply_add_fusion.4), channel_id=1, source_target_pairs={{0,128},{8,136},{16,144},{24,152},{32,160},{40,168},{48,176},{56,1... | collective-permute-start | bytes 122888 | tf_op jit(solution)/shard_map/ppermute | solution.py:481
  23.6 7.7 %collective-permute-start.3 = (f32[16,640]{1,0:T(8,128)S(1)}, f32[16,640]{1,0:T(8,128)S(1)}, u32[]{:S(2)}, u32[]{:S(2)}) collective-permute-start(f32[16,640]{1,0:T(8,128)S(1)} %multiply_add_fusion.3), channel_id=1, source_target_pairs={{0,112},{8,120},{16,0},{24,8},{32,16},{40,24},{48,32},{56,40},{64,... | collective-permute-start | bytes 122888 | tf_op jit(solution)/shard_map/ppermute | solution.py:486
  29.5 5.2 %collective-permute-start.2 = (f32[16,640]{1,0:T(8,128)S(1)}, f32[16,640]{1,0:T(8,128)S(1)}, u32[]{:S(2)}, u32[]{:S(2)}) collective-permute-start(f32[16,640]{1,0:T(8,128)S(1)} %multiply_add_fusion.3), channel_id=1, source_target_pairs={{0,16},{8,24},{16,32},{24,40},{32,48},{40,56},{48,64},{56,72},{64,... | collective-permute-start | bytes 122888 | tf_op jit(solution)/shard_map/ppermute | solution.py:486
  29.6 14.0 %collective-permute-start.6 = (f32[1024,128]{1,0:T(8,128)S(1)}, f32[1024,128]{1,0:T(8,128)S(1)}, u32[]{:S(2)}, u32[]{:S(2)}) collective-permute-start(f32[1024,128]{1,0:T(8,128)S(1)} %convert_element_type.3), channel_id=1, source_target_pairs={{0,8},{8,0},{16,24},{24,16},{32,40},{40,32},{48,56},{56,48},{64,72... | collective-permute-start | bytes 1572872 | tf_op jit(solution)/shard_map/ppermute | solution.py:481
  29.7 26.0 %collective-permute-start.7 = (f32[1024,128]{1,0:T(8,128)S(1)}, f32[1024,128]{1,0:T(8,128)}, u32[]{:S(2)}, u32[]{:S(2)}) collective-permute-start(f32[1024,128]{1,0:T(8,128)S(1)} %convert_element_type.3), channel_id=1, source_target_pairs={{0,128},{8,136},{16,144},{24,152},{32,160},{40,168},{48,176},{56,1... | collective-permute-start | bytes 1572872 | tf_op jit(solution)/shard_map/ppermute | solution.py:481
  34.8 6.2 %collective-permute-start.5 = (f32[16,640]{1,0:T(8,128)S(1)}, f32[16,640]{1,0:T(8,128)S(1)}, u32[]{:S(2)}, u32[]{:S(2)}) collective-permute-start(f32[16,640]{1,0:T(8,128)S(1)} %get-tuple-element.48), channel_id=1, source_target_pairs={{0,80},{8,88},{16,96},{24,104},{32,112},{40,120},{48,0},{56,8},{64... | collective-permute-start | bytes 122888 | tf_op jit(solution)/shard_map/ppermute | solution.py:486
  35.6 8.0 %collective-permute-start.4 = (f32[16,640]{1,0:T(8,128)S(1)}, f32[16,640]{1,0:T(8,128)S(1)}, u32[]{:S(2)}, u32[]{:S(2)}) collective-permute-start(f32[16,640]{1,0:T(8,128)S(1)} %get-tuple-element.47), channel_id=1, source_target_pairs={{0,48},{8,56},{16,64},{24,72},{32,80},{40,88},{48,96},{56,104},{64... | collective-permute-start | bytes 122888 | tf_op jit(solution)/shard_map/ppermute | solution.py:486
  43.6 0.8 copy-start.7
  44.4 1.0 copy-start.12
  53.6 1.4 copy-start.5
  55.0 0.7 copy-start.13
  55.7 30.7 %all-to-all-start = ((f32[8,64,1024]{2,1,0:T(8,128)}), f32[8,64,1024]{2,1,0:T(8,128)S(1)}, u32[]{:S(2)}, u32[]{:S(2)}) async-start(f32[8,64,1024]{2,1,0:T(8,128)} %bitcast.7), calls=%async_computation | async-start | bytes 4194304 | tf_op jit(solution)/shard_map/all_to_all | solution.py:515
  63.0 25.1 %copy-start.1 = (bf16[64,8192]{1,0:T(8,128)(2,1)S(1)}, bf16[64,8192]{1,0:T(8,128)(2,1)}, u32[]{:S(2)}) copy-start(bf16[64,8192]{1,0:T(8,128)(2,1)} %refs_8_.1) | copy-start | bytes 3145732
  63.0 25.1 %copy-start.11 = (f32[64,64]{1,0:T(8,128)S(1)}, f32[64,64]{1,0:T(8,128)}, u32[]{:S(2)}) copy-start(f32[64,64]{1,0:T(8,128)} %refs_9_.1) | copy-start | bytes 49156
  63.0 2.1 %collective-permute-start.8 = (f32[1024,128]{1,0:T(8,128)}, f32[1024,128]{1,0:T(8,128)S(1)}, u32[]{:S(2)}, u32[]{:S(2)}) collective-permute-start(f32[1024,128]{1,0:T(8,128)} %collective-permute-done.7.refs_6_), channel_id=1, source_target_pairs={{0,8},{8,0},{16,24},{24,16},{32,40},{40,32},{48,56},{56,48},{64,72... | collective-permute-start | bytes 1572872 | tf_op jit(solution)/shard_map/ppermute | solution.py:481
  65.1 0.8 copy-start.9
  86.4 1.0 copy-start.14
  87.3 13.5 %copy-start.8 = (f32[1024,128]{1,0:T(8,128)S(1)}, f32[1024,128]{1,0:T(8,128)}, u32[]{:S(2)}) copy-start(f32[1024,128]{1,0:T(8,128)} %copy-done.7) | copy-start | bytes 1572868
  87.3 13.5 %copy-start.10 = (f32[1024,128]{1,0:T(8,128)S(1)}, f32[1024,128]{1,0:T(8,128)}, u32[]{:S(2)}) copy-start(f32[1024,128]{1,0:T(8,128)} %copy-done.9) | copy-start | bytes 1572868
  87.5 8.0 %collective-permute-start.10 = (f32[64,1024]{1,0:T(8,128)S(1)}, f32[64,1024]{1,0:T(8,128)S(1)}, u32[]{:S(2)}, u32[]{:S(2)}) collective-permute-start(f32[64,1024]{1,0:T(8,128)S(1)} %logit_grad.1.lg_ref.refs_0_), channel_id=1, source_target_pairs={{0,8},{8,0},{16,24},{24,16},{32,40},{40,32},{48,56},{56,48},{64,72... | collective-permute-start | bytes 786440 | tf_op jit(solution)/shard_map/ppermute | solution.py:481
  87.6 8.7 %collective-permute-start.9 = (f32[64,1024]{1,0:T(8,128)S(1)}, f32[64,1024]{1,0:T(8,128)S(1)}, u32[]{:S(2)}, u32[]{:S(2)}) collective-permute-start(f32[64,1024]{1,0:T(8,128)S(1)} %logit_grad.1.lg_ref.refs_0_), channel_id=1, source_target_pairs={{0,128},{8,136},{16,144},{24,152},{32,160},{40,168},{48,176},{56,1... | collective-permute-start | bytes 786440 | tf_op jit(solution)/shard_map/ppermute | solution.py:481
  96.3 4.5 %collective-permute-start.15 = (f32[64,1024]{1,0:T(8,128)S(1)}, f32[64,1024]{1,0:T(8,128)S(1)}, u32[]{:S(2)}, u32[]{:S(2)}) collective-permute-start(f32[64,1024]{1,0:T(8,128)S(1)} %collective-permute-done.9.refs_2_), channel_id=1, source_target_pairs={{0,8},{8,0},{16,24},{24,16},{32,40},{40,32},{48,56},{56,48},{64,72... | collective-permute-start | bytes 786440 | tf_op jit(solution)/shard_map/ppermute | solution.py:481
  96.3 13.1 %collective-permute-start.11 = (f32[4,128,128]{2,1,0:T(8,128)S(1)}, f32[4,128,128]{2,1,0:T(8,128)S(1)}, u32[]{:S(2)}, u32[]{:S(2)}) collective-permute-start(f32[4,128,128]{2,1,0:T(8,128)S(1)} %get-tuple-element.36), channel_id=1, source_target_pairs={{0,2},{1,3},{2,0},{3,1},{4,6},{5,7},{6,4},{7,5},{8,10},{9,11},{10,... | collective-permute-start | bytes 786440 | tf_op jit(solution)/shard_map/ppermute | solution.py:477
  98.7 10.1 %collective-permute-start.14 = (f32[16,256]{1,0:T(8,128)S(1)}, f32[16,256]{1,0:T(8,128)S(1)}, u32[]{:S(2)}, u32[]{:S(2)}) collective-permute-start(f32[16,256]{1,0:T(8,128)S(1)} %get-tuple-element.37.gw0), channel_id=1, source_target_pairs={{0,8},{8,0},{16,24},{24,16},{32,40},{40,32},{48,56},{56,48},{64,72... | collective-permute-start | bytes 49160 | tf_op jit(solution)/shard_map/ppermute | solution.py:481
  98.9 9.9 %collective-permute-start.13 = (f32[16,256]{1,0:T(8,128)S(1)}, f32[16,256]{1,0:T(8,128)S(1)}, u32[]{:S(2)}, u32[]{:S(2)}) collective-permute-start(f32[16,256]{1,0:T(8,128)S(1)} %get-tuple-element.37.gw0), channel_id=1, source_target_pairs={{0,136},{8,128},{16,152},{24,144},{32,168},{40,160},{48,184},{56,1... | collective-permute-start | bytes 49160 | tf_op jit(solution)/shard_map/ppermute | solution.py:481
  100.0 8.8 %collective-permute-start.12 = (f32[16,256]{1,0:T(8,128)S(1)}, f32[16,256]{1,0:T(8,128)S(1)}, u32[]{:S(2)}, u32[]{:S(2)}) collective-permute-start(f32[16,256]{1,0:T(8,128)S(1)} %get-tuple-element.37.gw0), channel_id=1, source_target_pairs={{0,128},{8,136},{16,144},{24,152},{32,160},{40,168},{48,176},{56,1... | collective-permute-start | bytes 49160 | tf_op jit(solution)/shard_map/ppermute | solution.py:481
  109.5 25.7 %all-to-all-start.1 = ((f32[8,80,256]{2,1,0:T(8,128)}), f32[8,80,256]{2,1,0:T(8,128)S(1)}, u32[]{:S(2)}, u32[]{:S(2)}) async-start(f32[8,80,256]{2,1,0:T(8,128)} %grad_w_rows.1), calls=%async_computation.1 | async-start | bytes 1310720 | tf_op jit(solution)/shard_map/all_to_all | solution.py:532
  114.8 5.2 %collective-permute-start.16 = (f32[2,128,128]{2,1,0:T(8,128)S(1)}, f32[2,128,128]{2,1,0:T(8,128)S(1)}, u32[]{:S(2)}, u32[]{:S(2)}) collective-permute-start(f32[2,128,128]{2,1,0:T(8,128)S(1)} %slice_add_fusion), channel_id=1, source_target_pairs={{0,6},{1,7},{2,4},{3,5},{4,2},{5,3},{6,0},{7,1},{8,14},{9,15},{10,... | collective-permute-start | bytes 393224 | tf_op jit(solution)/shard_map/ppermute | solution.py:477
  120.0 5.9 %collective-permute-start.17 = (f32[128,128]{1,0:T(8,128)S(1)}, f32[128,128]{1,0:T(8,128)S(1)}, u32[]{:S(2)}, u32[]{:S(2)}) collective-permute-start(f32[128,128]{1,0:T(8,128)S(1)} %get-tuple-element.45), channel_id=1, source_target_pairs={{0,1},{1,0},{2,3},{3,2},{4,5},{5,4},{6,7},{7,6},{8,9},{9,8},{10,11... | collective-permute-start | bytes 196616 | tf_op jit(solution)/shard_map/ppermute | solution.py:477

commit v6 on v5

--- a/solution.py
+++ b/solution.py
@@ -142,8 +142,8 @@
 
 
 def probs_kernel(
-    lse_ref, logits_hbm, krt_ref, qn_ref, qr_ref, kn_ref, out_hbm, index_ref,
-    krp, s_ref, acc, logits_ref, sems,
+    base_ref, qpos_ref, lse_ref, logits_ref, krt_ref, qn_ref, qr_ref, kn_ref, out_hbm,
+    krp, s_ref, acc, sems,
 ):
     step = pl.program_id(0)
     last = pl.num_programs(0) - 1
@@ -154,7 +154,6 @@
     def _():
         fill_rope(krt_ref, krp)
         acc[...] = jnp.zeros_like(acc)
-        pltpu.make_async_copy(logits_hbm, logits_ref, sems.at[N_HEAD]).start()
 
     lse = []
     for p in range(2):
@@ -170,28 +169,31 @@
 
     @pl.when(step == last)
     def _():
+        limit = column(qpos_ref[...]) - base_ref[0] * keys
+        key = lax.broadcasted_iota(jnp.int32, (size, keys), 1)
+        for h in range(N_HEAD):
+            rows = slice(h * size, (h + 1) * size)
+            acc[rows, :] = jnp.where(key <= lanes_of(limit[rows], keys), acc[rows, :], 0.0)
+        top = lanes_of(column(lse_ref[:1, queries:])[:size], keys)
+        mine = pl.ds(pl.multiple_of(lax.axis_index("head") * size, size), size)
+        acc[mine, :] -= jnp.exp2(logits_ref[...] - top) * HEADS
         copies = []
         for h in range(N_HEAD):
             rows = pl.ds(h * size, size)
             copies.append(pltpu.make_async_copy(acc.at[rows], out_hbm.at[rows], sems.at[h]))
         for copy in copies:
             copy.start()
-        pltpu.make_async_copy(logits_hbm, logits_ref, sems.at[N_HEAD]).wait()
-        logits = logits_ref[...]
-        top = lanes_of(column(lse_ref[:1, queries:])[:size], keys)
-        index_ref[...] = jnp.where(logits > 0.5 * NEG, jnp.exp2(logits - top), -1.0)
         for copy in copies:
             copy.wait()
 
 
-def lg_kernel(index_ref, target_ref, lg_ref):
+def lg_kernel(target_ref, lg_ref):
     for c in range(lg_ref.shape[1] // 128):
         cols = slice(c * 128, (c + 1) * 128)
         target = target_ref[0, :, cols]
         for h in range(1, N_HEAD):
             target = target + target_ref[h, :, cols]
-        prob = index_ref[:, cols]
-        lg_ref[:, cols] = jnp.where(prob >= 0.0, prob - target * (1.0 / HEADS), 0.0)
+        lg_ref[:, cols] = target * (-1.0 / HEADS)
 
 
 def gk_kernel(
@@ -360,41 +362,35 @@
     )
 
 
-def run_probs(lse, logits, qn, qr, kn, krt):
+def run_probs(key_blocks, qpos, lse, logits, qn, qr, kn, krt):
     queries, keys, pairs = qn.shape[0], kn.shape[0], qn.shape[1] // 256
     return call(
         probs_kernel,
         "main_probs",
         (pairs,),
-        (lse, logits, krt, qn, qr, kn),
-        [
-            whole(lse.shape),
-            pl.BlockSpec(memory_space=pltpu.HBM),
-            whole(krt.shape),
-            *main_specs(queries, keys),
-        ],
-        floats((queries, keys), logits.shape),
-        [pl.BlockSpec(memory_space=pltpu.HBM), whole(logits.shape)],
+        (key_blocks, qpos, lse, logits, krt, qn, qr, kn),
+        [smem(), *wholes([qpos, lse, logits, krt]), *main_specs(queries, keys)],
+        floats((queries, keys)),
+        [pl.BlockSpec(memory_space=pltpu.HBM)],
         [
             pltpu.VMEM((2, keys, 128), BF16),
             pltpu.VMEM((2, queries, keys), F32),
             pltpu.VMEM((queries, keys), F32),
-            pltpu.VMEM(logits.shape, F32),
-            pltpu.SemaphoreType.DMA((N_HEAD + 1,)),
+            pltpu.SemaphoreType.DMA((N_HEAD,)),
         ],
         24,
-    )
-
-
-def run_lg(index_probs, target):
+    )[0]
+
+
+def run_lg(target):
     return pl.pallas_call(
         lg_kernel,
-        in_specs=[in_vmem()] * 2,
+        in_specs=[in_vmem()],
         out_specs=in_vmem(),
-        out_shape=floats(index_probs.shape)[0],
+        out_shape=floats(target.shape[1:])[0],
         compiler_params=pltpu.CompilerParams(vmem_limit_bytes=8 * 1024 * 1024),
         name="logit_grad",
-    )(index_probs, target)
+    )(target)
 
 
 def run_gk(lg, iq, ik, w):
@@ -509,14 +505,13 @@
     lse, ik_later = lax.optimization_barrier((lse, ik))
     ikf = ik_later.astype(F32)
     ikf_y, ikf_c = ctx_xor(ikf, 16), ctx_xor(ikf, 1)
-    lse, ikf_c = lax.optimization_barrier((over_z(lse), ikf_c))
-    probs, index_probs = run_probs(lse, logits, qn, qr, kn, krt)
-    probs, ikf_y = lax.optimization_barrier((probs, ikf_y))
+    probs = run_probs(key_blocks, qpos, over_z(lse), logits, qn, qr, kn, krt)
+    probs, ikf_y, ikf_c = lax.optimization_barrier((probs, ikf_y, ikf_c))
     target = lax.all_to_all(probs.reshape(N_HEAD, -1, probs.shape[1]), "head", 0, 0)
     ikf_yc = ctx_xor(ikf_y, 1)
     target, ikf_yc = lax.optimization_barrier((target, ikf_yc))
 
-    lg = run_lg(index_probs, target)
+    lg = run_lg(target)
     lg_y, lg_c = ctx_xor(lg, 16), ctx_xor(lg, 1)
     keep, send, gw = run_gk(lg, iq, ik, w)
     lg_y, lg_c, send, gw = lax.optimization_barrier((lg_y, lg_c, send, gw))

time: 137 us -> 136 us (level)
  local copies, waits for them, and re-layouts: 5.56 us -> 3.92 us
    unnamed x30 -> x28, local copies, waits for them, and re-layouts: 5.54 us -> 3.91 us
where the time goes in v6:
time: 136 us; the launch traced here: 134 us
  waiting for transfers between devices  55.2 us (41%)
  Pallas kernels  41.2 us (30%)
  starting transfers between devices  31.6 us (23%)
  local copies, waits for them, and re-layouts  3.92 us (3%)
  between operations  1.49 us (1%)
    pallas_call x4, Pallas kernels, call(): pl.pallas_call(kernel, grid=grid, in_specs=in_specs, out_specs=out_specs,...  39.6 us
    all_to_all x1, waiting for transfers between devices, per_device(): lax.all_to_all(probs.reshape(N_HEAD, -1, probs.shape[1]), 'head', 0, 0)  20.5 us
    ppermute x3, waiting for transfers between devices, head_xor(): return lax.ppermute(value, 'head', [(i, i ^ bits) for i in range(N_HEAD)])  10.3 us
    ppermute x4, starting transfers between devices, z_shift(): return lax.ppermute(value, 'ctx', list(enumerate(to)))  9.83 us
    all_to_all x1, waiting for transfers between devices, per_device(): parts = lax.all_to_all(parts, 'ctx', 0, 0, axis_index_groups=groups)  9.34 us
    ppermute x4, waiting for transfers between devices, z_shift(): return lax.ppermute(value, 'ctx', list(enumerate(to)))  8.23 us
    all_to_all x1, starting transfers between devices, per_device(): lax.all_to_all(probs.reshape(N_HEAD, -1, probs.shape[1]), 'head', 0, 0)  7.33 us
    ppermute x11, waiting for transfers between devices, ctx_xor(): return lax.ppermute(value, 'ctx', [(i, i ^ bits) for i in range(N_CTX)])  6.88 us
  transfers between devices with their start and end apart: 20, of which 11 were waited for; matrix products, arithmetic and copies ran while one was open for 0% of the time, Pallas kernels for 18%

profile of v6, /device:TPU:2, one launch (start us, length us, event | category | flops | bytes accessed | tf_op | source)
XLA Modules:
  0.0 134.4 jit_solution(747844441328004350)
XLA Ops:
  1.3 15.8 %front.1 = (f32[16,640]{1,0:T(8,128)}, f32[64,1024]{1,0:T(8,128)}) custom-call(s32[1]{0:T(128)S(6)} %copy.14.base_ref, s32[1,512]{1,0:T(1,128)} %bitcast.10, bf16[64,1024]{1,0:T(8,128)(2,1)} %bitcast.8, bf16[1024,128]{1,0:T(8,128)(2,1)} %refs_4_.1, f32[64,64]{1,0:T(8,128)} %refs_9_.1, bf16[64,8192]{1,0:T(8,128)(2,1)} %refs_8_.1, bf16[512,2048]{1,0:T(8,128)(2,1)} %qn_ref.3, ...), custom_call_target="tpu_custom_call" | custom-call | tf_op jit(solution)/shard_map/front/pallas_call | solution.py:316
  17.2 0.1 collective-permute-start
  17.2 1.4 %collective-permute-done = f32[16,640]{1,0:T(8,128)S(1)} collective-permute-done((f32[16,640]{1,0:T(8,128)}, f32[16,640]{1,0:T(8,128)S(1)}, u32[]{:S(2)}, u32[]{:S(2)}) %collective-permute-start) | collective-permute-done | bytes 40992 | tf_op jit(solution)/shard_map/ppermute | solution.py:477
  18.7 0.8 multiply_add_fusion.4
  19.5 1.7 %collective-permute-start.1 = (f32[16,640]{1,0:T(8,128)S(1)}, f32[16,640]{1,0:T(8,128)S(1)}, u32[]{:S(2)}, u32[]{:S(2)}) collective-permute-start(f32[16,640]{1,0:T(8,128)S(1)} %multiply_add_fusion.4), channel_id=1, source_target_pairs={{0,128},{8,136},{16,144},{24,152},{32,160},{40,168},{48,176},{56,1... | collective-permute-start | bytes 122888 | tf_op jit(solution)/shard_map/ppermute | solution.py:477
  21.1 2.4 %collective-permute-done.1 = f32[16,640]{1,0:T(8,128)S(1)} collective-permute-done((f32[16,640]{1,0:T(8,128)S(1)}, f32[16,640]{1,0:T(8,128)S(1)}, u32[]{:S(2)}, u32[]{:S(2)}) %collective-permute-start.1) | collective-permute-done | bytes 40992 | tf_op jit(solution)/shard_map/ppermute | solution.py:477
  23.6 5.9 %collective-permute-start.3 = (f32[16,640]{1,0:T(8,128)S(1)}, f32[16,640]{1,0:T(8,128)S(1)}, u32[]{:S(2)}, u32[]{:S(2)}) collective-permute-start(f32[16,640]{1,0:T(8,128)S(1)} %multiply_add_fusion.3), channel_id=1, source_target_pairs={{0,112},{8,120},{16,0},{24,8},{32,16},{40,24},{48,32},{56,40},{64,... | collective-permute-start | bytes 122888 | tf_op jit(solution)/shard_map/ppermute | solution.py:482
  29.5 0.0 collective-permute-start.2
  29.6 0.1 collective-permute-start.7
  29.7 1.7 %collective-permute-start.6 = (f32[1024,128]{1,0:T(8,128)S(1)}, f32[1024,128]{1,0:T(8,128)}, u32[]{:S(2)}, u32[]{:S(2)}) collective-permute-start(f32[1024,128]{1,0:T(8,128)S(1)} %convert_element_type.3), channel_id=1, source_target_pairs={{0,128},{8,136},{16,144},{24,152},{32,160},{40,168},{48,176},{56,1... | collective-permute-start | bytes 1572872 | tf_op jit(solution)/shard_map/ppermute | solution.py:477
  31.3 3.4 %collective-permute-done.2 = f32[16,640]{1,0:T(8,128)S(1)} collective-permute-done((f32[16,640]{1,0:T(8,128)S(1)}, f32[16,640]{1,0:T(8,128)S(1)}, u32[]{:S(2)}, u32[]{:S(2)}) %collective-permute-start.2) | collective-permute-done | bytes 40992 | tf_op jit(solution)/shard_map/ppermute | solution.py:482
  34.7 0.1 multiply_add_fusion.2
  34.8 0.8 collective-permute-start.5
  35.6 3.1 %collective-permute-start.4 = (f32[16,640]{1,0:T(8,128)S(1)}, f32[16,640]{1,0:T(8,128)S(1)}, u32[]{:S(2)}, u32[]{:S(2)}) collective-permute-start(f32[16,640]{1,0:T(8,128)S(1)} %get-tuple-element.41), channel_id=1, source_target_pairs={{0,48},{8,56},{16,64},{24,72},{32,80},{40,88},{48,96},{56,104},{64... | collective-permute-start | bytes 122888 | tf_op jit(solution)/shard_map/ppermute | solution.py:482
  38.7 2.3 %collective-permute-done.5 = f32[16,640]{1,0:T(8,128)S(1)} collective-permute-done((f32[16,640]{1,0:T(8,128)S(1)}, f32[16,640]{1,0:T(8,128)S(1)}, u32[]{:S(2)}, u32[]{:S(2)}) %collective-permute-start.5) | collective-permute-done | bytes 40992 | tf_op jit(solution)/shard_map/ppermute | solution.py:482
  41.0 2.6 %collective-permute-done.4 = f32[16,640]{1,0:T(8,128)S(1)} collective-permute-done((f32[16,640]{1,0:T(8,128)S(1)}, f32[16,640]{1,0:T(8,128)S(1)}, u32[]{:S(2)}, u32[]{:S(2)}) %collective-permute-start.4) | collective-permute-done | bytes 40992 | tf_op jit(solution)/shard_map/ppermute | solution.py:482
  43.6 0.9 copy-done.12
  44.6 8.4 %main_probs.1 = f32[512,1024]{1,0:T(8,128)S(1)} custom-call(s32[1]{0:T(128)S(6)} %copy.14.base_ref, s32[1,512]{1,0:T(1,128)S(1)} %bitcast.11, f32[16,640]{1,0:T(8,128)S(1)} %multiply_add_fusion.lse_ref, f32[64,1024]{1,0:T(8,128)S(1)} %copy-done.12, bf16[64,1024]{1,0:T(8,128)(2,1)S(1)} %bitcast.9, bf16[512,2048]{1,0:T(8,128)(2,1)S(1)} %copy-done.2, ...), custom_call_target="tpu_custom_call" | custom-call | tf_op jit(solution)/shard_map/main_probs/pallas_call | solution.py:316
  53.0 1.4 %copy-done.3 = f32[512,1024]{1,0:T(8,128)} copy-done((f32[512,1024]{1,0:T(8,128)}, f32[512,1024]{1,0:T(8,128)S(1)}, u32[]{:S(2)}) %copy-start.3) | copy-done | bytes 2097176
  54.3 0.0 collective-permute-done.7.refs_5_
  54.3 0.8 copy-done.7
  55.1 0.0 collective-permute-done.6.refs_6_
  55.1 7.3 %all-to-all-start = ((f32[8,64,1024]{2,1,0:T(8,128)}), f32[8,64,1024]{2,1,0:T(8,128)S(1)}, u32[]{:S(2)}, u32[]{:S(2)}) async-start(f32[8,64,1024]{2,1,0:T(8,128)} %bitcast.7), calls=%async_computation | async-start | bytes 4194304 | tf_op jit(solution)/shard_map/all_to_all | solution.py:510
  62.4 0.0 collective-permute-start.8
  62.4 2.1 %collective-permute-done.8.refs_7_ = f32[1024,128]{1,0:T(8,128)S(1)} collective-permute-done((f32[1024,128]{1,0:T(8,128)}, f32[1024,128]{1,0:T(8,128)S(1)}, u32[]{:S(2)}, u32[]{:S(2)}) %collective-permute-start.8) | collective-permute-done | bytes 524320 | tf_op jit(solution)/shard_map/ppermute | solution.py:477
  64.6 0.8 copy-done.9
  65.3 20.5 %all-to-all-done.target_ref = f32[8,64,1024]{2,1,0:T(8,128)S(1)} async-done(((f32[8,64,1024]{2,1,0:T(8,128)}), f32[8,64,1024]{2,1,0:T(8,128)S(1)}, u32[]{:S(2)}, u32[]{:S(2)}) %all-to-all-start) | async-done | bytes 2097184 | tf_op jit(solution)/shard_map/all_to_all | solution.py:510
  85.8 0.1 logit_grad.1.lg_ref.refs_0_
  86.0 0.1 collective-permute-start.10
  86.1 0.4 collective-permute-start.9
  86.5 7.4 %grad_k.1 = (f32[4,128,128]{2,1,0:T(8,128)S(1)}, f32[4,128,128]{2,1,0:T(8,128)S(1)}, f32[16,256]{1,0:T(8,128)S(1)}) custom-call(f32[64,1024]{1,0:T(8,128)S(1)} %logit_grad.1.lg_ref.refs_0_, bf16[64,8192]{1,0:T(8,128)(2,1)S(1)} %copy-done.1, bf16[1024,128]{1,0:T(8,128)(2,1)S(1)} %copy-done.5, f32[64,64]{1,0:T(8,128)S(1)} %copy-done.11), custom_call_target="tpu_custom_call" | custom-call | tf_op jit(solution)/shard_map/grad_k/pallas_call | solution.py:316
  93.9 0.0 collective-permute-done.10.refs_1_
  93.9 0.9 collective-permute-done.9.refs_2_
  94.8 0.0 collective-permute-start.15
  94.8 2.4 %collective-permute-start.11 = (f32[4,128,128]{2,1,0:T(8,128)S(1)}, f32[4,128,128]{2,1,0:T(8,128)S(1)}, u32[]{:S(2)}, u32[]{:S(2)}) collective-permute-start(f32[4,128,128]{2,1,0:T(8,128)S(1)} %get-tuple-element.30), channel_id=1, source_target_pairs={{0,2},{1,3},{2,0},{3,1},{4,6},{5,7},{6,4},{7,5},{8,10},{9,11},{10,... | collective-permute-start | bytes 786440 | tf_op jit(solution)/shard_map/ppermute | solution.py:473
  97.2 0.2 collective-permute-start.14
  97.4 1.1 collective-permute-start.13
  98.5 0.8 collective-permute-start.12
  99.3 8.0 %grad_q.1.gq_ref = f32[8,80,256]{2,1,0:T(8,128)} custom-call(f32[64,1024]{1,0:T(8,128)S(1)} %logit_grad.1.lg_ref.refs_0_, f32[64,1024]{1,0:T(8,128)S(1)} %collective-permute-done.10.refs_1_, f32[64,1024]{1,0:T(8,128)S(1)} %collective-permute-done.9.refs_2_, f32[64,1024]{1,0:T(8,128)S(1)} %collective-permute-done.15.refs_3_, bf16[1024,128]{1,0:T(8,128)(2,1)S(1)} %copy-done.5, ...), custom_call_target="tpu_custom_call" | custom-call | tf_op jit(solution)/shard_map/grad_q/pallas_call | solution.py:316
  107.3 0.0 collective-permute-done.12.gw1
  107.3 0.7 grad_w_rows.1
  108.0 5.2 %all-to-all-start.1 = ((f32[8,80,256]{2,1,0:T(8,128)}), f32[8,80,256]{2,1,0:T(8,128)S(1)}, u32[]{:S(2)}, u32[]{:S(2)}) async-start(f32[8,80,256]{2,1,0:T(8,128)} %grad_w_rows.1), calls=%async_computation.1 | async-start | bytes 1310720 | tf_op jit(solution)/shard_map/all_to_all | solution.py:527
  113.2 0.1 collective-permute-start.16
  113.3 5.1 %collective-permute-done.16 = f32[2,128,128]{2,1,0:T(8,128)S(1)} collective-permute-done((f32[2,128,128]{2,1,0:T(8,128)S(1)}, f32[2,128,128]{2,1,0:T(8,128)S(1)}, u32[]{:S(2)}, u32[]{:S(2)}) %collective-permute-start.16) | collective-permute-done | bytes 131104 | tf_op jit(solution)/shard_map/ppermute | solution.py:473
  118.4 0.6 collective-permute-start.17
  119.0 5.2 %collective-permute-done.17.got_ref = f32[128,128]{1,0:T(8,128)S(1)} collective-permute-done((f32[128,128]{1,0:T(8,128)S(1)}, f32[128,128]{1,0:T(8,128)S(1)}, u32[]{:S(2)}, u32[]{:S(2)}) %collective-permute-start.17) | collective-permute-done | bytes 65568 | tf_op jit(solution)/shard_map/ppermute | solution.py:473
  124.3 9.3 %all-to-all-done.1.parts_ref = f32[8,80,256]{2,1,0:T(8,128)S(1)} async-done(((f32[8,80,256]{2,1,0:T(8,128)}), f32[8,80,256]{2,1,0:T(8,128)S(1)}, u32[]{:S(2)}, u32[]{:S(2)}) %all-to-all-start.1) | async-done | bytes 655392 | tf_op jit(solution)/shard_map/all_to_all | solution.py:527
  133.6 0.8 finish.1
  (35 shorter events, 0.2 us)
Async XLA Ops:
  1.3 28.3 %copy-start.5 = (bf16[1024,128]{1,0:T(8,128)(2,1)S(1)}, bf16[1024,128]{1,0:T(8,128)(2,1)}, u32[]{:S(2)}) copy-start(bf16[1024,128]{1,0:T(8,128)(2,1)} %refs_4_.1) | copy-start | bytes 786436
  1.3 42.3 %copy-start = (bf16[1024,2048]{1,0:T(8,128)(2,1)S(1)}, bf16[1024,2048]{1,0:T(8,128)(2,1)}, u32[]{:S(2)}) copy-start(bf16[1024,2048]{1,0:T(8,128)(2,1)} %kn_ref.3) | copy-start | bytes 12582916
  1.3 42.3 %copy-start.2 = (bf16[512,2048]{1,0:T(8,128)(2,1)S(1)}, bf16[512,2048]{1,0:T(8,128)(2,1)}, u32[]{:S(2)}) copy-start(bf16[512,2048]{1,0:T(8,128)(2,1)} %qn_ref.3) | copy-start | bytes 6291460
  1.3 42.3 %copy-start.6 = (bf16[1024,64]{0,1:T(8,128)(2,1)S(1)}, bf16[1024,64]{0,1:T(8,128)(2,1)}, u32[]{:S(2)}) copy-start(bf16[1024,64]{0,1:T(8,128)(2,1)} %param.12) | copy-start | bytes 393220
  1.3 42.3 %copy-start.13 = (s32[512]{0:T(512)S(1)}, s32[512]{0:T(512)}, u32[]{:S(2)}) copy-start(s32[512]{0:T(512)} %param.16) | copy-start | bytes 6148
  17.2 26.5 %copy-start.4 = (bf16[512,1024]{1,0:T(8,128)(2,1)S(1)}, bf16[512,1024]{1,0:T(8,128)(2,1)}, u32[]{:S(2)}) copy-start(bf16[512,1024]{1,0:T(8,128)(2,1)} %qr_ref.3) | copy-start | bytes 3145732
  17.2 1.5 %collective-permute-start = (f32[16,640]{1,0:T(8,128)}, f32[16,640]{1,0:T(8,128)S(1)}, u32[]{:S(2)}, u32[]{:S(2)}) collective-permute-start(f32[16,640]{1,0:T(8,128)} %get-tuple-element.21), channel_id=1, source_target_pairs={{0,8},{8,0},{16,24},{24,16},{32,40},{40,32},{48,56},{56,48},{64,72... | collective-permute-start | bytes 122888 | tf_op jit(solution)/shard_map/ppermute | solution.py:477
  19.5 4.1 %collective-permute-start.1 = (f32[16,640]{1,0:T(8,128)S(1)}, f32[16,640]{1,0:T(8,128)S(1)}, u32[]{:S(2)}, u32[]{:S(2)}) collective-permute-start(f32[16,640]{1,0:T(8,128)S(1)} %multiply_add_fusion.4), channel_id=1, source_target_pairs={{0,128},{8,136},{16,144},{24,152},{32,160},{40,168},{48,176},{56,1... | collective-permute-start | bytes 122888 | tf_op jit(solution)/shard_map/ppermute | solution.py:477
  23.6 7.7 %collective-permute-start.3 = (f32[16,640]{1,0:T(8,128)S(1)}, f32[16,640]{1,0:T(8,128)S(1)}, u32[]{:S(2)}, u32[]{:S(2)}) collective-permute-start(f32[16,640]{1,0:T(8,128)S(1)} %multiply_add_fusion.3), channel_id=1, source_target_pairs={{0,112},{8,120},{16,0},{24,8},{32,16},{40,24},{48,32},{56,40},{64,... | collective-permute-start | bytes 122888 | tf_op jit(solution)/shard_map/ppermute | solution.py:482
  29.5 5.2 %collective-permute-start.2 = (f32[16,640]{1,0:T(8,128)S(1)}, f32[16,640]{1,0:T(8,128)S(1)}, u32[]{:S(2)}, u32[]{:S(2)}) collective-permute-start(f32[16,640]{1,0:T(8,128)S(1)} %multiply_add_fusion.3), channel_id=1, source_target_pairs={{0,16},{8,24},{16,32},{24,40},{32,48},{40,56},{48,64},{56,72},{64,... | collective-permute-start | bytes 122888 | tf_op jit(solution)/shard_map/ppermute | solution.py:482
  29.6 24.7 %collective-permute-start.7 = (f32[1024,128]{1,0:T(8,128)S(1)}, f32[1024,128]{1,0:T(8,128)S(1)}, u32[]{:S(2)}, u32[]{:S(2)}) collective-permute-start(f32[1024,128]{1,0:T(8,128)S(1)} %convert_element_type.3), channel_id=1, source_target_pairs={{0,8},{8,0},{16,24},{24,16},{32,40},{40,32},{48,56},{56,48},{64,72... | collective-permute-start | bytes 1572872 | tf_op jit(solution)/shard_map/ppermute | solution.py:477
  29.7 25.4 %collective-permute-start.6 = (f32[1024,128]{1,0:T(8,128)S(1)}, f32[1024,128]{1,0:T(8,128)}, u32[]{:S(2)}, u32[]{:S(2)}) collective-permute-start(f32[1024,128]{1,0:T(8,128)S(1)} %convert_element_type.3), channel_id=1, source_target_pairs={{0,128},{8,136},{16,144},{24,152},{32,160},{40,168},{48,176},{56,1... | collective-permute-start | bytes 1572872 | tf_op jit(solution)/shard_map/ppermute | solution.py:477
  34.8 6.2 %collective-permute-start.5 = (f32[16,640]{1,0:T(8,128)S(1)}, f32[16,640]{1,0:T(8,128)S(1)}, u32[]{:S(2)}, u32[]{:S(2)}) collective-permute-start(f32[16,640]{1,0:T(8,128)S(1)} %get-tuple-element.42), channel_id=1, source_target_pairs={{0,80},{8,88},{16,96},{24,104},{32,112},{40,120},{48,0},{56,8},{64... | collective-permute-start | bytes 122888 | tf_op jit(solution)/shard_map/ppermute | solution.py:482
  35.6 8.0 %collective-permute-start.4 = (f32[16,640]{1,0:T(8,128)S(1)}, f32[16,640]{1,0:T(8,128)S(1)}, u32[]{:S(2)}, u32[]{:S(2)}) collective-permute-start(f32[16,640]{1,0:T(8,128)S(1)} %get-tuple-element.41), channel_id=1, source_target_pairs={{0,48},{8,56},{16,64},{24,72},{32,80},{40,88},{48,96},{56,104},{64... | collective-permute-start | bytes 122888 | tf_op jit(solution)/shard_map/ppermute | solution.py:482
  43.6 1.0 copy-start.12
  52.9 1.4 %copy-start.3 = (f32[512,1024]{1,0:T(8,128)}, f32[512,1024]{1,0:T(8,128)S(1)}, u32[]{:S(2)}) copy-start(f32[512,1024]{1,0:T(8,128)S(1)} %main_probs.1) | copy-start | bytes 6291460
  54.3 0.8 copy-start.7
  55.1 30.7 %all-to-all-start = ((f32[8,64,1024]{2,1,0:T(8,128)}), f32[8,64,1024]{2,1,0:T(8,128)S(1)}, u32[]{:S(2)}, u32[]{:S(2)}) async-start(f32[8,64,1024]{2,1,0:T(8,128)} %bitcast.7), calls=%async_computation | async-start | bytes 4194304 | tf_op jit(solution)/shard_map/all_to_all | solution.py:510
  62.4 24.0 %copy-start.1 = (bf16[64,8192]{1,0:T(8,128)(2,1)S(1)}, bf16[64,8192]{1,0:T(8,128)(2,1)}, u32[]{:S(2)}) copy-start(bf16[64,8192]{1,0:T(8,128)(2,1)} %refs_8_.1) | copy-start | bytes 3145732
  62.4 24.0 %copy-start.11 = (f32[64,64]{1,0:T(8,128)S(1)}, f32[64,64]{1,0:T(8,128)}, u32[]{:S(2)}) copy-start(f32[64,64]{1,0:T(8,128)} %refs_9_.1) | copy-start | bytes 49156
  62.4 2.1 %collective-permute-start.8 = (f32[1024,128]{1,0:T(8,128)}, f32[1024,128]{1,0:T(8,128)S(1)}, u32[]{:S(2)}, u32[]{:S(2)}) collective-permute-start(f32[1024,128]{1,0:T(8,128)} %collective-permute-done.6.refs_6_), channel_id=1, source_target_pairs={{0,8},{8,0},{16,24},{24,16},{32,40},{40,32},{48,56},{56,48},{64,72... | collective-permute-start | bytes 1572872 | tf_op jit(solution)/shard_map/ppermute | solution.py:477
  64.6 0.8 copy-start.9
  85.8 13.5 %copy-start.8 = (f32[1024,128]{1,0:T(8,128)S(1)}, f32[1024,128]{1,0:T(8,128)}, u32[]{:S(2)}) copy-start(f32[1024,128]{1,0:T(8,128)} %copy-done.7) | copy-start | bytes 1572868
  85.8 13.5 %copy-start.10 = (f32[1024,128]{1,0:T(8,128)S(1)}, f32[1024,128]{1,0:T(8,128)}, u32[]{:S(2)}) copy-start(f32[1024,128]{1,0:T(8,128)} %copy-done.9) | copy-start | bytes 1572868
  86.0 7.9 %collective-permute-start.10 = (f32[64,1024]{1,0:T(8,128)S(1)}, f32[64,1024]{1,0:T(8,128)S(1)}, u32[]{:S(2)}, u32[]{:S(2)}) collective-permute-start(f32[64,1024]{1,0:T(8,128)S(1)} %logit_grad.1.lg_ref.refs_0_), channel_id=1, source_target_pairs={{0,8},{8,0},{16,24},{24,16},{32,40},{40,32},{48,56},{56,48},{64,72... | collective-permute-start | bytes 786440 | tf_op jit(solution)/shard_map/ppermute | solution.py:477
  86.1 8.7 %collective-permute-start.9 = (f32[64,1024]{1,0:T(8,128)S(1)}, f32[64,1024]{1,0:T(8,128)S(1)}, u32[]{:S(2)}, u32[]{:S(2)}) collective-permute-start(f32[64,1024]{1,0:T(8,128)S(1)} %logit_grad.1.lg_ref.refs_0_), channel_id=1, source_target_pairs={{0,128},{8,136},{16,144},{24,152},{32,160},{40,168},{48,176},{56,1... | collective-permute-start | bytes 786440 | tf_op jit(solution)/shard_map/ppermute | solution.py:477
  94.8 4.5 %collective-permute-start.15 = (f32[64,1024]{1,0:T(8,128)S(1)}, f32[64,1024]{1,0:T(8,128)S(1)}, u32[]{:S(2)}, u32[]{:S(2)}) collective-permute-start(f32[64,1024]{1,0:T(8,128)S(1)} %collective-permute-done.9.refs_2_), channel_id=1, source_target_pairs={{0,8},{8,0},{16,24},{24,16},{32,40},{40,32},{48,56},{56,48},{64,72... | collective-permute-start | bytes 786440 | tf_op jit(solution)/shard_map/ppermute | solution.py:477
  94.8 13.2 %collective-permute-start.11 = (f32[4,128,128]{2,1,0:T(8,128)S(1)}, f32[4,128,128]{2,1,0:T(8,128)S(1)}, u32[]{:S(2)}, u32[]{:S(2)}) collective-permute-start(f32[4,128,128]{2,1,0:T(8,128)S(1)} %get-tuple-element.30), channel_id=1, source_target_pairs={{0,2},{1,3},{2,0},{3,1},{4,6},{5,7},{6,4},{7,5},{8,10},{9,11},{10,... | collective-permute-start | bytes 786440 | tf_op jit(solution)/shard_map/ppermute | solution.py:473
  97.2 10.1 %collective-permute-start.14 = (f32[16,256]{1,0:T(8,128)S(1)}, f32[16,256]{1,0:T(8,128)S(1)}, u32[]{:S(2)}, u32[]{:S(2)}) collective-permute-start(f32[16,256]{1,0:T(8,128)S(1)} %get-tuple-element.31.gw0), channel_id=1, source_target_pairs={{0,8},{8,0},{16,24},{24,16},{32,40},{40,32},{48,56},{56,48},{64,72... | collective-permute-start | bytes 49160 | tf_op jit(solution)/shard_map/ppermute | solution.py:477
  97.4 9.9 %collective-permute-start.13 = (f32[16,256]{1,0:T(8,128)S(1)}, f32[16,256]{1,0:T(8,128)S(1)}, u32[]{:S(2)}, u32[]{:S(2)}) collective-permute-start(f32[16,256]{1,0:T(8,128)S(1)} %get-tuple-element.31.gw0), channel_id=1, source_target_pairs={{0,136},{8,128},{16,152},{24,144},{32,168},{40,160},{48,184},{56,1... | collective-permute-start | bytes 49160 | tf_op jit(solution)/shard_map/ppermute | solution.py:477
  98.5 8.8 %collective-permute-start.12 = (f32[16,256]{1,0:T(8,128)S(1)}, f32[16,256]{1,0:T(8,128)S(1)}, u32[]{:S(2)}, u32[]{:S(2)}) collective-permute-start(f32[16,256]{1,0:T(8,128)S(1)} %get-tuple-element.31.gw0), channel_id=1, source_target_pairs={{0,128},{8,136},{16,144},{24,152},{32,160},{40,168},{48,176},{56,1... | collective-permute-start | bytes 49160 | tf_op jit(solution)/shard_map/ppermute | solution.py:477
  108.0 25.6 %all-to-all-start.1 = ((f32[8,80,256]{2,1,0:T(8,128)}), f32[8,80,256]{2,1,0:T(8,128)S(1)}, u32[]{:S(2)}, u32[]{:S(2)}) async-start(f32[8,80,256]{2,1,0:T(8,128)} %grad_w_rows.1), calls=%async_computation.1 | async-start | bytes 1310720 | tf_op jit(solution)/shard_map/all_to_all | solution.py:527
  113.2 5.2 %collective-permute-start.16 = (f32[2,128,128]{2,1,0:T(8,128)S(1)}, f32[2,128,128]{2,1,0:T(8,128)S(1)}, u32[]{:S(2)}, u32[]{:S(2)}) collective-permute-start(f32[2,128,128]{2,1,0:T(8,128)S(1)} %slice_add_fusion), channel_id=1, source_target_pairs={{0,6},{1,7},{2,4},{3,5},{4,2},{5,3},{6,0},{7,1},{8,14},{9,15},{10,... | collective-permute-start | bytes 393224 | tf_op jit(solution)/shard_map/ppermute | solution.py:473
  118.4 5.9 %collective-permute-start.17 = (f32[128,128]{1,0:T(8,128)S(1)}, f32[128,128]{1,0:T(8,128)S(1)}, u32[]{:S(2)}, u32[]{:S(2)}) collective-permute-start(f32[128,128]{1,0:T(8,128)S(1)} %get-tuple-element.39), channel_id=1, source_target_pairs={{0,1},{1,0},{2,3},{3,2},{4,5},{5,4},{6,7},{7,6},{8,9},{9,8},{10,11... | collective-permute-start | bytes 196616 | tf_op jit(solution)/shard_map/ppermute | solution.py:473

commit v7 on v6

--- a/solution.py
+++ b/solution.py
@@ -502,14 +502,15 @@
     lse, logits = run_front(key_blocks, qpos, krt, ik, w, iq, qn, qr, kn)
     lse = merged(lse, ctx_xor(lse, 1))
     lse = merged(lse, ctx_xor(lse, 16))
-    lse, ik_later = lax.optimization_barrier((lse, ik))
+    lse, ik_later, logits = lax.optimization_barrier((lse, ik, logits))
     ikf = ik_later.astype(F32)
-    ikf_y, ikf_c = ctx_xor(ikf, 16), ctx_xor(ikf, 1)
+    ikf_y = ctx_xor(ikf, 16)
+    logits = jnp.maximum(logits, NEG)
     probs = run_probs(key_blocks, qpos, over_z(lse), logits, qn, qr, kn, krt)
-    probs, ikf_y, ikf_c = lax.optimization_barrier((probs, ikf_y, ikf_c))
+    probs, ikf, ikf_y = lax.optimization_barrier((probs, ikf, ikf_y))
     target = lax.all_to_all(probs.reshape(N_HEAD, -1, probs.shape[1]), "head", 0, 0)
-    ikf_yc = ctx_xor(ikf_y, 1)
-    target, ikf_yc = lax.optimization_barrier((target, ikf_yc))
+    ikf_c, ikf_yc = ctx_xor(ikf, 1), ctx_xor(ikf_y, 1)
+    target, ikf_c, ikf_yc = lax.optimization_barrier((target, ikf_c, ikf_yc))
 
     lg = run_lg(target)
     lg_y, lg_c = ctx_xor(lg, 16), ctx_xor(lg, 1)

time: 136 us -> 132 us (0.971)
  waiting for transfers between devices: 55.2 us -> 50.4 us
  starting transfers between devices: 31.6 us -> 33 us
    all_to_all x1, waiting for transfers between devices: 20.5 us -> 19.1 us  [per_device(): lax.all_to_all(probs.reshape(N_HEAD, -1, probs.shape[1]), 'head', 0, 0)]
  transfers between devices with their start and end apart: 20 -> 20, of which waited for: 11 -> 11; matrix products, arithmetic and copies ran while one was open for 0% -> 1% of each run, Pallas kernels for 18% -> 19%
where the time goes in v7:
time: 132 us; the launch traced here: 131 us
  waiting for transfers between devices  50.4 us (38%)
  Pallas kernels  41.2 us (31%)
  starting transfers between devices  33 us (25%)
  local copies, waits for them, and re-layouts  2.98 us (2%)
  other arithmetic  2 us (2%)
  between operations  1.5 us (1%)
    pallas_call x4, Pallas kernels, call(): pl.pallas_call(kernel, grid=grid, in_specs=in_specs, out_specs=out_specs,...  39.6 us
    all_to_all x1, waiting for transfers between devices, per_device(): lax.all_to_all(probs.reshape(N_HEAD, -1, probs.shape[1]), 'head', 0, 0)  19.1 us
    ppermute x4, starting transfers between devices, z_shift(): return lax.ppermute(value, 'ctx', list(enumerate(to)))  9.83 us
    all_to_all x1, waiting for transfers between devices, per_device(): parts = lax.all_to_all(parts, 'ctx', 0, 0, axis_index_groups=groups)  9.34 us
    ppermute x3, waiting for transfers between devices, head_xor(): return lax.ppermute(value, 'head', [(i, i ^ bits) for i in range(N_HEAD)])  9.11 us
    all_to_all x1, starting transfers between devices, per_device(): lax.all_to_all(probs.reshape(N_HEAD, -1, probs.shape[1]), 'head', 0, 0)  7.46 us
    ppermute x11, starting transfers between devices, ctx_xor(): return lax.ppermute(value, 'ctx', [(i, i ^ bits) for i in range(N_CTX)])  7.07 us
    ppermute x4, waiting for transfers between devices, z_shift(): return lax.ppermute(value, 'ctx', list(enumerate(to)))  7.06 us
  transfers between devices with their start and end apart: 20, of which 11 were waited for; matrix products, arithmetic and copies ran while one was open for 1% of the time, Pallas kernels for 19%

profile of v7, /device:TPU:2, one launch (start us, length us, event | category | flops | bytes accessed | tf_op | source)
XLA Modules:
  0.0 131.1 jit_solution(17341427140174717896)
XLA Ops:
  1.3 15.8 %front.1 = (f32[16,640]{1,0:T(8,128)}, f32[64,1024]{1,0:T(8,128)}) custom-call(s32[1]{0:T(128)S(6)} %copy.14.base_ref, s32[1,512]{1,0:T(1,128)} %bitcast.10, bf16[64,1024]{1,0:T(8,128)(2,1)} %bitcast.8, bf16[1024,128]{1,0:T(8,128)(2,1)} %refs_4_.1, f32[64,64]{1,0:T(8,128)} %refs_9_.1, bf16[64,8192]{1,0:T(8,128)(2,1)} %refs_8_.1, bf16[512,2048]{1,0:T(8,128)(2,1)} %qn_ref.3, ...), custom_call_target="tpu_custom_call" | custom-call | tf_op jit(solution)/shard_map/front/pallas_call | solution.py:316
  17.2 0.1 collective-permute-start
  17.2 1.4 %collective-permute-done = f32[16,640]{1,0:T(8,128)S(1)} collective-permute-done((f32[16,640]{1,0:T(8,128)}, f32[16,640]{1,0:T(8,128)S(1)}, u32[]{:S(2)}, u32[]{:S(2)}) %collective-permute-start) | collective-permute-done | bytes 40992 | tf_op jit(solution)/shard_map/ppermute | solution.py:477
  18.7 0.8 multiply_add_fusion.4
  19.5 1.7 %collective-permute-start.1 = (f32[16,640]{1,0:T(8,128)S(1)}, f32[16,640]{1,0:T(8,128)S(1)}, u32[]{:S(2)}, u32[]{:S(2)}) collective-permute-start(f32[16,640]{1,0:T(8,128)S(1)} %multiply_add_fusion.4), channel_id=1, source_target_pairs={{0,128},{8,136},{16,144},{24,152},{32,160},{40,168},{48,176},{56,1... | collective-permute-start | bytes 122888 | tf_op jit(solution)/shard_map/ppermute | solution.py:477
  21.1 2.4 %collective-permute-done.1 = f32[16,640]{1,0:T(8,128)S(1)} collective-permute-done((f32[16,640]{1,0:T(8,128)S(1)}, f32[16,640]{1,0:T(8,128)S(1)}, u32[]{:S(2)}, u32[]{:S(2)}) %collective-permute-start.1) | collective-permute-done | bytes 40992 | tf_op jit(solution)/shard_map/ppermute | solution.py:477
  23.6 5.9 %collective-permute-start.3 = (f32[16,640]{1,0:T(8,128)S(1)}, f32[16,640]{1,0:T(8,128)S(1)}, u32[]{:S(2)}, u32[]{:S(2)}) collective-permute-start(f32[16,640]{1,0:T(8,128)S(1)} %multiply_add_fusion.3), channel_id=1, source_target_pairs={{0,112},{8,120},{16,0},{24,8},{32,16},{40,24},{48,32},{56,40},{64,... | collective-permute-start | bytes 122888 | tf_op jit(solution)/shard_map/ppermute | solution.py:482
  29.5 0.0 collective-permute-start.2
  29.6 1.7 %collective-permute-start.6 = (f32[1024,128]{1,0:T(8,128)S(1)}, f32[1024,128]{1,0:T(8,128)}, u32[]{:S(2)}, u32[]{:S(2)}) collective-permute-start(f32[1024,128]{1,0:T(8,128)S(1)} %convert_element_type.3), channel_id=1, source_target_pairs={{0,128},{8,136},{16,144},{24,152},{32,160},{40,168},{48,176},{56,1... | collective-permute-start | bytes 1572872 | tf_op jit(solution)/shard_map/ppermute | solution.py:477
  31.2 3.5 %collective-permute-done.2 = f32[16,640]{1,0:T(8,128)S(1)} collective-permute-done((f32[16,640]{1,0:T(8,128)S(1)}, f32[16,640]{1,0:T(8,128)S(1)}, u32[]{:S(2)}, u32[]{:S(2)}) %collective-permute-start.2) | collective-permute-done | bytes 40992 | tf_op jit(solution)/shard_map/ppermute | solution.py:482
  34.7 0.1 multiply_add_fusion.2
  34.8 0.8 collective-permute-start.5
  35.6 3.1 %collective-permute-start.4 = (f32[16,640]{1,0:T(8,128)S(1)}, f32[16,640]{1,0:T(8,128)S(1)}, u32[]{:S(2)}, u32[]{:S(2)}) collective-permute-start(f32[16,640]{1,0:T(8,128)S(1)} %get-tuple-element.45), channel_id=1, source_target_pairs={{0,48},{8,56},{16,64},{24,72},{32,80},{40,88},{48,96},{56,104},{64... | collective-permute-start | bytes 122888 | tf_op jit(solution)/shard_map/ppermute | solution.py:482
  38.7 1.0 broadcast_maximum_fusion.logits_ref
  39.7 1.3 collective-permute-done.5
  41.0 2.3 %collective-permute-done.4 = f32[16,640]{1,0:T(8,128)S(1)} collective-permute-done((f32[16,640]{1,0:T(8,128)S(1)}, f32[16,640]{1,0:T(8,128)S(1)}, u32[]{:S(2)}, u32[]{:S(2)}) %collective-permute-start.4) | collective-permute-done | bytes 40992 | tf_op jit(solution)/shard_map/ppermute | solution.py:482
  43.3 8.4 %main_probs.1 = f32[512,1024]{1,0:T(8,128)S(1)} custom-call(s32[1]{0:T(128)S(6)} %copy.14.base_ref, s32[1,512]{1,0:T(1,128)S(1)} %bitcast.11, f32[16,640]{1,0:T(8,128)S(1)} %multiply_add_fusion.lse_ref, f32[64,1024]{1,0:T(8,128)S(1)} %broadcast_maximum_fusion.logits_ref, bf16[64,1024]{1,0:T(8,128)(2,1)S(1)} %bitcast.9, bf16[512,2048]{1,0:T(8,128)(2,1)S(1)} %copy-done.2, ...), custom_call_target="tpu_custom_call" | custom-call | tf_op jit(solution)/shard_map/main_probs/pallas_call | solution.py:316
  51.7 1.4 %copy-done.3 = f32[512,1024]{1,0:T(8,128)} copy-done((f32[512,1024]{1,0:T(8,128)}, f32[512,1024]{1,0:T(8,128)S(1)}, u32[]{:S(2)}) %copy-start.3) | copy-done | bytes 2097176
  53.1 0.0 collective-permute-done.6.refs_6_
  53.1 7.5 %all-to-all-start = ((f32[8,64,1024]{2,1,0:T(8,128)}), f32[8,64,1024]{2,1,0:T(8,128)S(1)}, u32[]{:S(2)}, u32[]{:S(2)}) async-start(f32[8,64,1024]{2,1,0:T(8,128)} %bitcast.7), calls=%async_computation | async-start | bytes 4194304 | tf_op jit(solution)/shard_map/all_to_all | solution.py:511
  60.6 0.0 collective-permute-start.7
  60.6 0.5 collective-permute-start.8
  61.1 1.6 %collective-permute-done.7.refs_5_ = f32[1024,128]{1,0:T(8,128)S(1)} collective-permute-done((f32[1024,128]{1,0:T(8,128)}, f32[1024,128]{1,0:T(8,128)S(1)}, u32[]{:S(2)}, u32[]{:S(2)}) %collective-permute-start.7) | collective-permute-done | bytes 524320 | tf_op jit(solution)/shard_map/ppermute | solution.py:477
  62.7 0.8 copy-done.7
  63.5 0.0 collective-permute-done.8.refs_7_
  63.5 0.8 copy-done.9
  64.3 19.1 %all-to-all-done.target_ref = f32[8,64,1024]{2,1,0:T(8,128)S(1)} async-done(((f32[8,64,1024]{2,1,0:T(8,128)}), f32[8,64,1024]{2,1,0:T(8,128)S(1)}, u32[]{:S(2)}, u32[]{:S(2)}) %all-to-all-start) | async-done | bytes 2097184 | tf_op jit(solution)/shard_map/all_to_all | solution.py:511
  83.3 0.1 logit_grad.1.lg_ref.refs_0_
  83.5 0.1 collective-permute-start.10
  83.6 0.9 collective-permute-start.9
  84.5 7.4 %grad_k.1 = (f32[4,128,128]{2,1,0:T(8,128)S(1)}, f32[4,128,128]{2,1,0:T(8,128)S(1)}, f32[16,256]{1,0:T(8,128)S(1)}) custom-call(f32[64,1024]{1,0:T(8,128)S(1)} %logit_grad.1.lg_ref.refs_0_, bf16[64,8192]{1,0:T(8,128)(2,1)S(1)} %copy-done.1, bf16[1024,128]{1,0:T(8,128)(2,1)S(1)} %copy-done.5, f32[64,64]{1,0:T(8,128)S(1)} %copy-done.11), custom_call_target="tpu_custom_call" | custom-call | tf_op jit(solution)/shard_map/grad_k/pallas_call | solution.py:316
  92.0 0.3 collective-permute-done.9.refs_2_
  92.3 2.1 %collective-permute-start.11 = (f32[4,128,128]{2,1,0:T(8,128)S(1)}, f32[4,128,128]{2,1,0:T(8,128)S(1)}, u32[]{:S(2)}, u32[]{:S(2)}) collective-permute-start(f32[4,128,128]{2,1,0:T(8,128)S(1)} %get-tuple-element.34), channel_id=1, source_target_pairs={{0,2},{1,3},{2,0},{3,1},{4,6},{5,7},{6,4},{7,5},{8,10},{9,11},{10,... | collective-permute-start | bytes 786440 | tf_op jit(solution)/shard_map/ppermute | solution.py:473
  94.4 0.2 collective-permute-start.14
  94.7 1.1 collective-permute-start.13
  95.8 0.8 collective-permute-start.12
  96.6 0.0 collective-permute-done.15.refs_3_
  96.6 8.0 %grad_q.1.gq_ref = f32[8,80,256]{2,1,0:T(8,128)} custom-call(f32[64,1024]{1,0:T(8,128)S(1)} %logit_grad.1.lg_ref.refs_0_, f32[64,1024]{1,0:T(8,128)S(1)} %collective-permute-done.10.refs_1_, f32[64,1024]{1,0:T(8,128)S(1)} %collective-permute-done.9.refs_2_, f32[64,1024]{1,0:T(8,128)S(1)} %collective-permute-done.15.refs_3_, bf16[1024,128]{1,0:T(8,128)(2,1)S(1)} %copy-done.5, ...), custom_call_target="tpu_custom_call" | custom-call | tf_op jit(solution)/shard_map/grad_q/pallas_call | solution.py:316
  104.5 0.0 collective-permute-done.14.gw3
  104.5 0.0 collective-permute-done.13.gw2
  104.6 0.7 grad_w_rows.1
  105.2 4.6 %all-to-all-start.1 = ((f32[8,80,256]{2,1,0:T(8,128)}), f32[8,80,256]{2,1,0:T(8,128)S(1)}, u32[]{:S(2)}, u32[]{:S(2)}) async-start(f32[8,80,256]{2,1,0:T(8,128)} %grad_w_rows.1), calls=%async_computation.1 | async-start | bytes 1310720 | tf_op jit(solution)/shard_map/all_to_all | solution.py:528
  109.9 0.1 collective-permute-start.16
  110.0 5.1 %collective-permute-done.16 = f32[2,128,128]{2,1,0:T(8,128)S(1)} collective-permute-done((f32[2,128,128]{2,1,0:T(8,128)S(1)}, f32[2,128,128]{2,1,0:T(8,128)S(1)}, u32[]{:S(2)}, u32[]{:S(2)}) %collective-permute-start.16) | collective-permute-done | bytes 131104 | tf_op jit(solution)/shard_map/ppermute | solution.py:473
  115.1 1.8 %collective-permute-start.17 = (f32[128,128]{1,0:T(8,128)S(1)}, f32[128,128]{1,0:T(8,128)S(1)}, u32[]{:S(2)}, u32[]{:S(2)}) collective-permute-start(f32[128,128]{1,0:T(8,128)S(1)} %get-tuple-element.43), channel_id=1, source_target_pairs={{0,1},{1,0},{2,3},{3,2},{4,5},{5,4},{6,7},{7,6},{8,9},{9,8},{10,11... | collective-permute-start | bytes 196616 | tf_op jit(solution)/shard_map/ppermute | solution.py:473
  116.9 4.1 %collective-permute-done.17.got_ref = f32[128,128]{1,0:T(8,128)S(1)} collective-permute-done((f32[128,128]{1,0:T(8,128)S(1)}, f32[128,128]{1,0:T(8,128)S(1)}, u32[]{:S(2)}, u32[]{:S(2)}) %collective-permute-start.17) | collective-permute-done | bytes 65568 | tf_op jit(solution)/shard_map/ppermute | solution.py:473
  121.0 9.3 %all-to-all-done.1.parts_ref = f32[8,80,256]{2,1,0:T(8,128)S(1)} async-done(((f32[8,80,256]{2,1,0:T(8,128)}), f32[8,80,256]{2,1,0:T(8,128)S(1)}, u32[]{:S(2)}, u32[]{:S(2)}) %all-to-all-start.1) | async-done | bytes 655392 | tf_op jit(solution)/shard_map/all_to_all | solution.py:528
  130.3 0.8 finish.1
  (36 shorter events, 0.2 us)
Async XLA Ops:
  1.3 28.3 %copy-start.5 = (bf16[1024,128]{1,0:T(8,128)(2,1)S(1)}, bf16[1024,128]{1,0:T(8,128)(2,1)}, u32[]{:S(2)}) copy-start(bf16[1024,128]{1,0:T(8,128)(2,1)} %refs_4_.1) | copy-start | bytes 786436
  1.3 42.0 %copy-start = (bf16[1024,2048]{1,0:T(8,128)(2,1)S(1)}, bf16[1024,2048]{1,0:T(8,128)(2,1)}, u32[]{:S(2)}) copy-start(bf16[1024,2048]{1,0:T(8,128)(2,1)} %kn_ref.3) | copy-start | bytes 12582916
  1.3 42.0 %copy-start.2 = (bf16[512,2048]{1,0:T(8,128)(2,1)S(1)}, bf16[512,2048]{1,0:T(8,128)(2,1)}, u32[]{:S(2)}) copy-start(bf16[512,2048]{1,0:T(8,128)(2,1)} %qn_ref.3) | copy-start | bytes 6291460
  1.3 42.0 %copy-start.6 = (bf16[1024,64]{0,1:T(8,128)(2,1)S(1)}, bf16[1024,64]{0,1:T(8,128)(2,1)}, u32[]{:S(2)}) copy-start(bf16[1024,64]{0,1:T(8,128)(2,1)} %param.12) | copy-start | bytes 393220
  1.3 42.0 %copy-start.12 = (s32[512]{0:T(512)S(1)}, s32[512]{0:T(512)}, u32[]{:S(2)}) copy-start(s32[512]{0:T(512)} %param.16) | copy-start | bytes 6148
  17.2 26.2 %copy-start.4 = (bf16[512,1024]{1,0:T(8,128)(2,1)S(1)}, bf16[512,1024]{1,0:T(8,128)(2,1)}, u32[]{:S(2)}) copy-start(bf16[512,1024]{1,0:T(8,128)(2,1)} %qr_ref.3) | copy-start | bytes 3145732
  17.2 1.5 %collective-permute-start = (f32[16,640]{1,0:T(8,128)}, f32[16,640]{1,0:T(8,128)S(1)}, u32[]{:S(2)}, u32[]{:S(2)}) collective-permute-start(f32[16,640]{1,0:T(8,128)} %get-tuple-element.23), channel_id=1, source_target_pairs={{0,8},{8,0},{16,24},{24,16},{32,40},{40,32},{48,56},{56,48},{64,72... | collective-permute-start | bytes 122888 | tf_op jit(solution)/shard_map/ppermute | solution.py:477
  19.5 4.1 %collective-permute-start.1 = (f32[16,640]{1,0:T(8,128)S(1)}, f32[16,640]{1,0:T(8,128)S(1)}, u32[]{:S(2)}, u32[]{:S(2)}) collective-permute-start(f32[16,640]{1,0:T(8,128)S(1)} %multiply_add_fusion.4), channel_id=1, source_target_pairs={{0,128},{8,136},{16,144},{24,152},{32,160},{40,168},{48,176},{56,1... | collective-permute-start | bytes 122888 | tf_op jit(solution)/shard_map/ppermute | solution.py:477
  23.6 7.7 %collective-permute-start.3 = (f32[16,640]{1,0:T(8,128)S(1)}, f32[16,640]{1,0:T(8,128)S(1)}, u32[]{:S(2)}, u32[]{:S(2)}) collective-permute-start(f32[16,640]{1,0:T(8,128)S(1)} %multiply_add_fusion.3), channel_id=1, source_target_pairs={{0,112},{8,120},{16,0},{24,8},{32,16},{40,24},{48,32},{56,40},{64,... | collective-permute-start | bytes 122888 | tf_op jit(solution)/shard_map/ppermute | solution.py:482
  29.5 5.2 %collective-permute-start.2 = (f32[16,640]{1,0:T(8,128)S(1)}, f32[16,640]{1,0:T(8,128)S(1)}, u32[]{:S(2)}, u32[]{:S(2)}) collective-permute-start(f32[16,640]{1,0:T(8,128)S(1)} %multiply_add_fusion.3), channel_id=1, source_target_pairs={{0,16},{8,24},{16,32},{24,40},{32,48},{40,56},{48,64},{56,72},{64,... | collective-permute-start | bytes 122888 | tf_op jit(solution)/shard_map/ppermute | solution.py:482
  29.6 22.2 %copy-start.13 = (f32[1024,128]{1,0:T(8,128)}, f32[1024,128]{1,0:T(8,128)S(1)}, u32[]{:S(2)}) copy-start(f32[1024,128]{1,0:T(8,128)S(1)} %convert_element_type.3) | copy-start | bytes 1572868
  29.6 23.5 %collective-permute-start.6 = (f32[1024,128]{1,0:T(8,128)S(1)}, f32[1024,128]{1,0:T(8,128)}, u32[]{:S(2)}, u32[]{:S(2)}) collective-permute-start(f32[1024,128]{1,0:T(8,128)S(1)} %convert_element_type.3), channel_id=1, source_target_pairs={{0,128},{8,136},{16,144},{24,152},{32,160},{40,168},{48,176},{56,1... | collective-permute-start | bytes 1572872 | tf_op jit(solution)/shard_map/ppermute | solution.py:477
  34.8 6.2 %collective-permute-start.5 = (f32[16,640]{1,0:T(8,128)S(1)}, f32[16,640]{1,0:T(8,128)S(1)}, u32[]{:S(2)}, u32[]{:S(2)}) collective-permute-start(f32[16,640]{1,0:T(8,128)S(1)} %get-tuple-element.46), channel_id=1, source_target_pairs={{0,80},{8,88},{16,96},{24,104},{32,112},{40,120},{48,0},{56,8},{64... | collective-permute-start | bytes 122888 | tf_op jit(solution)/shard_map/ppermute | solution.py:482
  35.6 7.7 %collective-permute-start.4 = (f32[16,640]{1,0:T(8,128)S(1)}, f32[16,640]{1,0:T(8,128)S(1)}, u32[]{:S(2)}, u32[]{:S(2)}) collective-permute-start(f32[16,640]{1,0:T(8,128)S(1)} %get-tuple-element.45), channel_id=1, source_target_pairs={{0,48},{8,56},{16,64},{24,72},{32,80},{40,88},{48,96},{56,104},{64... | collective-permute-start | bytes 122888 | tf_op jit(solution)/shard_map/ppermute | solution.py:482
  51.7 1.4 %copy-start.3 = (f32[512,1024]{1,0:T(8,128)}, f32[512,1024]{1,0:T(8,128)S(1)}, u32[]{:S(2)}) copy-start(f32[512,1024]{1,0:T(8,128)S(1)} %main_probs.1) | copy-start | bytes 6291460
  53.1 30.2 %all-to-all-start = ((f32[8,64,1024]{2,1,0:T(8,128)}), f32[8,64,1024]{2,1,0:T(8,128)S(1)}, u32[]{:S(2)}, u32[]{:S(2)}) async-start(f32[8,64,1024]{2,1,0:T(8,128)} %bitcast.7), calls=%async_computation | async-start | bytes 4194304 | tf_op jit(solution)/shard_map/all_to_all | solution.py:511
  60.6 24.0 %copy-start.1 = (bf16[64,8192]{1,0:T(8,128)(2,1)S(1)}, bf16[64,8192]{1,0:T(8,128)(2,1)}, u32[]{:S(2)}) copy-start(bf16[64,8192]{1,0:T(8,128)(2,1)} %refs_8_.1) | copy-start | bytes 3145732
  60.6 24.0 %copy-start.11 = (f32[64,64]{1,0:T(8,128)S(1)}, f32[64,64]{1,0:T(8,128)}, u32[]{:S(2)}) copy-start(f32[64,64]{1,0:T(8,128)} %refs_9_.1) | copy-start | bytes 49156
  60.6 2.1 %collective-permute-start.7 = (f32[1024,128]{1,0:T(8,128)}, f32[1024,128]{1,0:T(8,128)S(1)}, u32[]{:S(2)}, u32[]{:S(2)}) collective-permute-start(f32[1024,128]{1,0:T(8,128)} %copy-done.13), channel_id=1, source_target_pairs={{0,8},{8,0},{16,24},{24,16},{32,40},{40,32},{48,56},{56,48},{64,72... | collective-permute-start | bytes 1572872 | tf_op jit(solution)/shard_map/ppermute | solution.py:477
  60.6 2.9 %collective-permute-start.8 = (f32[1024,128]{1,0:T(8,128)}, f32[1024,128]{1,0:T(8,128)S(1)}, u32[]{:S(2)}, u32[]{:S(2)}) collective-permute-start(f32[1024,128]{1,0:T(8,128)} %collective-permute-done.6.refs_6_), channel_id=1, source_target_pairs={{0,8},{8,0},{16,24},{24,16},{32,40},{40,32},{48,56},{56,48},{64,72... | collective-permute-start | bytes 1572872 | tf_op jit(solution)/shard_map/ppermute | solution.py:477
  62.7 0.8 copy-start.7
  63.5 0.8 copy-start.9
  83.3 13.3 %copy-start.8 = (f32[1024,128]{1,0:T(8,128)S(1)}, f32[1024,128]{1,0:T(8,128)}, u32[]{:S(2)}) copy-start(f32[1024,128]{1,0:T(8,128)} %copy-done.7) | copy-start | bytes 1572868
  83.3 13.3 %copy-start.10 = (f32[1024,128]{1,0:T(8,128)S(1)}, f32[1024,128]{1,0:T(8,128)}, u32[]{:S(2)}) copy-start(f32[1024,128]{1,0:T(8,128)} %copy-done.9) | copy-start | bytes 1572868
  83.5 8.5 %collective-permute-start.10 = (f32[64,1024]{1,0:T(8,128)S(1)}, f32[64,1024]{1,0:T(8,128)S(1)}, u32[]{:S(2)}, u32[]{:S(2)}) collective-permute-start(f32[64,1024]{1,0:T(8,128)S(1)} %logit_grad.1.lg_ref.refs_0_), channel_id=1, source_target_pairs={{0,8},{8,0},{16,24},{24,16},{32,40},{40,32},{48,56},{56,48},{64,72... | collective-permute-start | bytes 786440 | tf_op jit(solution)/shard_map/ppermute | solution.py:477
  83.6 8.7 %collective-permute-start.9 = (f32[64,1024]{1,0:T(8,128)S(1)}, f32[64,1024]{1,0:T(8,128)S(1)}, u32[]{:S(2)}, u32[]{:S(2)}) collective-permute-start(f32[64,1024]{1,0:T(8,128)S(1)} %logit_grad.1.lg_ref.refs_0_), channel_id=1, source_target_pairs={{0,128},{8,136},{16,144},{24,152},{32,160},{40,168},{48,176},{56,1... | collective-permute-start | bytes 786440 | tf_op jit(solution)/shard_map/ppermute | solution.py:477
  92.3 4.3 %collective-permute-start.15 = (f32[64,1024]{1,0:T(8,128)S(1)}, f32[64,1024]{1,0:T(8,128)S(1)}, u32[]{:S(2)}, u32[]{:S(2)}) collective-permute-start(f32[64,1024]{1,0:T(8,128)S(1)} %collective-permute-done.9.refs_2_), channel_id=1, source_target_pairs={{0,8},{8,0},{16,24},{24,16},{32,40},{40,32},{48,56},{56,48},{64,72... | collective-permute-start | bytes 786440 | tf_op jit(solution)/shard_map/ppermute | solution.py:477
  92.3 12.9 %collective-permute-start.11 = (f32[4,128,128]{2,1,0:T(8,128)S(1)}, f32[4,128,128]{2,1,0:T(8,128)S(1)}, u32[]{:S(2)}, u32[]{:S(2)}) collective-permute-start(f32[4,128,128]{2,1,0:T(8,128)S(1)} %get-tuple-element.34), channel_id=1, source_target_pairs={{0,2},{1,3},{2,0},{3,1},{4,6},{5,7},{6,4},{7,5},{8,10},{9,11},{10,... | collective-permute-start | bytes 786440 | tf_op jit(solution)/shard_map/ppermute | solution.py:473
  94.4 10.1 %collective-permute-start.14 = (f32[16,256]{1,0:T(8,128)S(1)}, f32[16,256]{1,0:T(8,128)S(1)}, u32[]{:S(2)}, u32[]{:S(2)}) collective-permute-start(f32[16,256]{1,0:T(8,128)S(1)} %get-tuple-element.35.gw0), channel_id=1, source_target_pairs={{0,8},{8,0},{16,24},{24,16},{32,40},{40,32},{48,56},{56,48},{64,72... | collective-permute-start | bytes 49160 | tf_op jit(solution)/shard_map/ppermute | solution.py:477
  94.7 9.9 %collective-permute-start.13 = (f32[16,256]{1,0:T(8,128)S(1)}, f32[16,256]{1,0:T(8,128)S(1)}, u32[]{:S(2)}, u32[]{:S(2)}) collective-permute-start(f32[16,256]{1,0:T(8,128)S(1)} %get-tuple-element.35.gw0), channel_id=1, source_target_pairs={{0,136},{8,128},{16,152},{24,144},{32,168},{40,160},{48,184},{56,1... | collective-permute-start | bytes 49160 | tf_op jit(solution)/shard_map/ppermute | solution.py:477
  95.8 8.8 %collective-permute-start.12 = (f32[16,256]{1,0:T(8,128)S(1)}, f32[16,256]{1,0:T(8,128)S(1)}, u32[]{:S(2)}, u32[]{:S(2)}) collective-permute-start(f32[16,256]{1,0:T(8,128)S(1)} %get-tuple-element.35.gw0), channel_id=1, source_target_pairs={{0,128},{8,136},{16,144},{24,152},{32,160},{40,168},{48,176},{56,1... | collective-permute-start | bytes 49160 | tf_op jit(solution)/shard_map/ppermute | solution.py:477
  105.2 25.0 %all-to-all-start.1 = ((f32[8,80,256]{2,1,0:T(8,128)}), f32[8,80,256]{2,1,0:T(8,128)S(1)}, u32[]{:S(2)}, u32[]{:S(2)}) async-start(f32[8,80,256]{2,1,0:T(8,128)} %grad_w_rows.1), calls=%async_computation.1 | async-start | bytes 1310720 | tf_op jit(solution)/shard_map/all_to_all | solution.py:528
  109.9 5.2 %collective-permute-start.16 = (f32[2,128,128]{2,1,0:T(8,128)S(1)}, f32[2,128,128]{2,1,0:T(8,128)S(1)}, u32[]{:S(2)}, u32[]{:S(2)}) collective-permute-start(f32[2,128,128]{2,1,0:T(8,128)S(1)} %slice_add_fusion), channel_id=1, source_target_pairs={{0,6},{1,7},{2,4},{3,5},{4,2},{5,3},{6,0},{7,1},{8,14},{9,15},{10,... | collective-permute-start | bytes 393224 | tf_op jit(solution)/shard_map/ppermute | solution.py:473
  115.1 5.9 %collective-permute-start.17 = (f32[128,128]{1,0:T(8,128)S(1)}, f32[128,128]{1,0:T(8,128)S(1)}, u32[]{:S(2)}, u32[]{:S(2)}) collective-permute-start(f32[128,128]{1,0:T(8,128)S(1)} %get-tuple-element.43), channel_id=1, source_target_pairs={{0,1},{1,0},{2,3},{3,2},{4,5},{5,4},{6,7},{7,6},{8,9},{9,8},{10,11... | collective-permute-start | bytes 196616 | tf_op jit(solution)/shard_map/ppermute | solution.py:473

commit v8 on v7

--- a/solution.py
+++ b/solution.py
@@ -101,6 +101,7 @@
             pair = [wt[2 * i : 2 * i + 1], wt[2 * i + 1 : 2 * i + 2]]
             wp[i : i + 1, :] = jnp.concatenate(pair, axis=1)
         acc[...] = jnp.zeros_like(acc)
+        si_ref[...] = jnp.zeros_like(si_ref)
         qcol[...] = column(qpos_ref[...])
 
     def scores(p):
@@ -112,21 +113,26 @@
             cols = slice(qc * 256, (qc + 1) * 256)
             out_ref[pl.ds(2 * step + p, 1), cols] = online_lse(s_ref.at[p], bias, cols)
 
+    def add_logits(group):
+        weights = [wp[pl.ds(group * GROUP // 2 + i, 1), :] for i in range(GROUP // 2)]
+        for r in range(keys // 64):
+            at = slice(r * 64, (r + 1) * 64)
+            total = acc[at, :]
+            for i, weight in enumerate(weights):
+                active = jnp.maximum(si_ref[at, i * 128 : (i + 1) * 128], 0.0)
+                total = total + active * weight
+            acc[at, :] = total
+
     scores(0)
+    add_logits(jnp.maximum(step - 1, 0))
+    scores(1)
+    statistics(0)
     si_ref[...] = dot(ik_ref[...], stacked(iq_ref[...]), NT)
-    statistics(0)
-    scores(1)
-    weights = [wp[pl.ds(step * GROUP // 2 + i, 1), :] for i in range(GROUP // 2)]
-    for r in range(keys // 64):
-        at = slice(r * 64, (r + 1) * 64)
-        total = acc[at, :]
-        for i, weight in enumerate(weights):
-            total = total + jnp.maximum(si_ref[at, i * 128 : (i + 1) * 128], 0.0) * weight
-        acc[at, :] = total
     statistics(1)
 
     @pl.when(step == pl.num_programs(0) - 1)
     def _():
+        add_logits(step)
         turned = acc[...].T
         key = lax.broadcasted_iota(jnp.int32, (rows, keys), 1) + base_ref[0] * keys
         start = pl.multiple_of(lax.axis_index("head") * rows, rows)

time: 132 us -> 134 us (1.015)
  Pallas kernels: 41.2 us -> 42.7 us
    pallas_call x4, Pallas kernels: 39.6 us -> 41.1 us  [call(): pl.pallas_call(kernel, grid=grid, in_specs=in_specs, out_specs=out_specs,...]
  transfers between devices with their start and end apart: 20 -> 20, of which waited for: 11 -> 11; matrix products, arithmetic and copies ran while one was open for 1% -> 1% of each run, Pallas kernels for 19% -> 18%
where the time goes in v8:
time: 134 us; the launch traced here: 133 us
  waiting for transfers between devices  50.4 us (38%)
  Pallas kernels  42.7 us (32%)
  starting transfers between devices  33 us (25%)
  local copies, waits for them, and re-layouts  2.98 us (2%)
  other arithmetic  2 us (1%)
  between operations  1.5 us (1%)
    pallas_call x4, Pallas kernels, call(): pl.pallas_call(kernel, grid=grid, in_specs=in_specs, out_specs=out_specs,...  41.1 us
    all_to_all x1, waiting for transfers between devices, per_device(): lax.all_to_all(probs.reshape(N_HEAD, -1, probs.shape[1]), 'head', 0, 0)  19.1 us
    ppermute x4, starting transfers between devices, z_shift(): return lax.ppermute(value, 'ctx', list(enumerate(to)))  9.83 us
    all_to_all x1, waiting for transfers between devices, per_device(): parts = lax.all_to_all(parts, 'ctx', 0, 0, axis_index_groups=groups)  9.34 us
    ppermute x3, waiting for transfers between devices, head_xor(): return lax.ppermute(value, 'head', [(i, i ^ bits) for i in range(N_HEAD)])  9.11 us
    all_to_all x1, starting transfers between devices, per_device(): lax.all_to_all(probs.reshape(N_HEAD, -1, probs.shape[1]), 'head', 0, 0)  7.46 us
    ppermute x11, starting transfers between devices, ctx_xor(): return lax.ppermute(value, 'ctx', [(i, i ^ bits) for i in range(N_CTX)])  7.08 us
    ppermute x4, waiting for transfers between devices, z_shift(): return lax.ppermute(value, 'ctx', list(enumerate(to)))  7.06 us
  transfers between devices with their start and end apart: 20, of which 11 were waited for; matrix products, arithmetic and copies ran while one was open for 1% of the time, Pallas kernels for 18%

profile of v8, /device:TPU:2, one launch (start us, length us, event | category | flops | bytes accessed | tf_op | source)
XLA Modules:
  0.0 132.6 jit_solution(4552853968343697882)
XLA Ops:
  1.3 17.4 %front.1 = (f32[16,640]{1,0:T(8,128)}, f32[64,1024]{1,0:T(8,128)}) custom-call(s32[1]{0:T(128)S(6)} %copy.14.base_ref, s32[1,512]{1,0:T(1,128)} %bitcast.10, bf16[64,1024]{1,0:T(8,128)(2,1)} %bitcast.8, bf16[1024,128]{1,0:T(8,128)(2,1)} %refs_4_.1, f32[64,64]{1,0:T(8,128)} %refs_9_.1, bf16[64,8192]{1,0:T(8,128)(2,1)} %refs_8_.1, bf16[512,2048]{1,0:T(8,128)(2,1)} %qn_ref.3, ...), custom_call_target="tpu_custom_call" | custom-call | tf_op jit(solution)/shard_map/front/pallas_call | solution.py:322
  18.7 0.1 collective-permute-start
  18.8 1.4 %collective-permute-done = f32[16,640]{1,0:T(8,128)S(1)} collective-permute-done((f32[16,640]{1,0:T(8,128)}, f32[16,640]{1,0:T(8,128)S(1)}, u32[]{:S(2)}, u32[]{:S(2)}) %collective-permute-start) | collective-permute-done | bytes 40992 | tf_op jit(solution)/shard_map/ppermute | solution.py:483
  20.2 0.8 multiply_add_fusion.4
  21.0 1.7 %collective-permute-start.1 = (f32[16,640]{1,0:T(8,128)S(1)}, f32[16,640]{1,0:T(8,128)S(1)}, u32[]{:S(2)}, u32[]{:S(2)}) collective-permute-start(f32[16,640]{1,0:T(8,128)S(1)} %multiply_add_fusion.4), channel_id=1, source_target_pairs={{0,128},{8,136},{16,144},{24,152},{32,160},{40,168},{48,176},{56,1... | collective-permute-start | bytes 122888 | tf_op jit(solution)/shard_map/ppermute | solution.py:483
  22.7 2.4 %collective-permute-done.1 = f32[16,640]{1,0:T(8,128)S(1)} collective-permute-done((f32[16,640]{1,0:T(8,128)S(1)}, f32[16,640]{1,0:T(8,128)S(1)}, u32[]{:S(2)}, u32[]{:S(2)}) %collective-permute-start.1) | collective-permute-done | bytes 40992 | tf_op jit(solution)/shard_map/ppermute | solution.py:483
  25.1 5.9 %collective-permute-start.3 = (f32[16,640]{1,0:T(8,128)S(1)}, f32[16,640]{1,0:T(8,128)S(1)}, u32[]{:S(2)}, u32[]{:S(2)}) collective-permute-start(f32[16,640]{1,0:T(8,128)S(1)} %multiply_add_fusion.3), channel_id=1, source_target_pairs={{0,112},{8,120},{16,0},{24,8},{32,16},{40,24},{48,32},{56,40},{64,... | collective-permute-start | bytes 122888 | tf_op jit(solution)/shard_map/ppermute | solution.py:488
  31.1 0.0 collective-permute-start.2
  31.1 1.7 %collective-permute-start.6 = (f32[1024,128]{1,0:T(8,128)S(1)}, f32[1024,128]{1,0:T(8,128)}, u32[]{:S(2)}, u32[]{:S(2)}) collective-permute-start(f32[1024,128]{1,0:T(8,128)S(1)} %convert_element_type.3), channel_id=1, source_target_pairs={{0,128},{8,136},{16,144},{24,152},{32,160},{40,168},{48,176},{56,1... | collective-permute-start | bytes 1572872 | tf_op jit(solution)/shard_map/ppermute | solution.py:483
  32.8 0.0 collective-permute-done.3
  32.8 3.5 %collective-permute-done.2 = f32[16,640]{1,0:T(8,128)S(1)} collective-permute-done((f32[16,640]{1,0:T(8,128)S(1)}, f32[16,640]{1,0:T(8,128)S(1)}, u32[]{:S(2)}, u32[]{:S(2)}) %collective-permute-start.2) | collective-permute-done | bytes 40992 | tf_op jit(solution)/shard_map/ppermute | solution.py:488
  36.3 0.1 multiply_add_fusion.2
  36.3 0.8 collective-permute-start.5
  37.1 3.1 %collective-permute-start.4 = (f32[16,640]{1,0:T(8,128)S(1)}, f32[16,640]{1,0:T(8,128)S(1)}, u32[]{:S(2)}, u32[]{:S(2)}) collective-permute-start(f32[16,640]{1,0:T(8,128)S(1)} %get-tuple-element.45), channel_id=1, source_target_pairs={{0,48},{8,56},{16,64},{24,72},{32,80},{40,88},{48,96},{56,104},{64... | collective-permute-start | bytes 122888 | tf_op jit(solution)/shard_map/ppermute | solution.py:488
  40.2 1.0 broadcast_maximum_fusion.logits_ref
  41.2 1.3 collective-permute-done.5
  42.5 2.3 %collective-permute-done.4 = f32[16,640]{1,0:T(8,128)S(1)} collective-permute-done((f32[16,640]{1,0:T(8,128)S(1)}, f32[16,640]{1,0:T(8,128)S(1)}, u32[]{:S(2)}, u32[]{:S(2)}) %collective-permute-start.4) | collective-permute-done | bytes 40992 | tf_op jit(solution)/shard_map/ppermute | solution.py:488
  44.9 8.4 %main_probs.1 = f32[512,1024]{1,0:T(8,128)S(1)} custom-call(s32[1]{0:T(128)S(6)} %copy.14.base_ref, s32[1,512]{1,0:T(1,128)S(1)} %bitcast.11, f32[16,640]{1,0:T(8,128)S(1)} %multiply_add_fusion.lse_ref, f32[64,1024]{1,0:T(8,128)S(1)} %broadcast_maximum_fusion.logits_ref, bf16[64,1024]{1,0:T(8,128)(2,1)S(1)} %bitcast.9, bf16[512,2048]{1,0:T(8,128)(2,1)S(1)} %copy-done.2, ...), custom_call_target="tpu_custom_call" | custom-call | tf_op jit(solution)/shard_map/main_probs/pallas_call | solution.py:322
  53.3 1.4 %copy-done.3 = f32[512,1024]{1,0:T(8,128)} copy-done((f32[512,1024]{1,0:T(8,128)}, f32[512,1024]{1,0:T(8,128)S(1)}, u32[]{:S(2)}) %copy-start.3) | copy-done | bytes 2097176
  54.6 0.0 collective-permute-done.6.refs_6_
  54.6 7.5 %all-to-all-start = ((f32[8,64,1024]{2,1,0:T(8,128)}), f32[8,64,1024]{2,1,0:T(8,128)S(1)}, u32[]{:S(2)}, u32[]{:S(2)}) async-start(f32[8,64,1024]{2,1,0:T(8,128)} %bitcast.7), calls=%async_computation | async-start | bytes 4194304 | tf_op jit(solution)/shard_map/all_to_all | solution.py:517
  62.1 0.5 collective-permute-start.8
  62.6 1.6 %collective-permute-done.7.refs_5_ = f32[1024,128]{1,0:T(8,128)S(1)} collective-permute-done((f32[1024,128]{1,0:T(8,128)}, f32[1024,128]{1,0:T(8,128)S(1)}, u32[]{:S(2)}, u32[]{:S(2)}) %collective-permute-start.7) | collective-permute-done | bytes 524320 | tf_op jit(solution)/shard_map/ppermute | solution.py:483
  64.2 0.8 copy-done.7
  65.0 0.8 copy-done.9
  65.8 19.1 %all-to-all-done.target_ref = f32[8,64,1024]{2,1,0:T(8,128)S(1)} async-done(((f32[8,64,1024]{2,1,0:T(8,128)}), f32[8,64,1024]{2,1,0:T(8,128)S(1)}, u32[]{:S(2)}, u32[]{:S(2)}) %all-to-all-start) | async-done | bytes 2097184 | tf_op jit(solution)/shard_map/all_to_all | solution.py:517
  84.9 0.1 logit_grad.1.lg_ref.refs_0_
  85.0 0.1 collective-permute-start.10
  85.1 0.9 collective-permute-start.9
  86.1 7.4 %grad_k.1 = (f32[4,128,128]{2,1,0:T(8,128)S(1)}, f32[4,128,128]{2,1,0:T(8,128)S(1)}, f32[16,256]{1,0:T(8,128)S(1)}) custom-call(f32[64,1024]{1,0:T(8,128)S(1)} %logit_grad.1.lg_ref.refs_0_, bf16[64,8192]{1,0:T(8,128)(2,1)S(1)} %copy-done.1, bf16[1024,128]{1,0:T(8,128)(2,1)S(1)} %copy-done.5, f32[64,64]{1,0:T(8,128)S(1)} %copy-done.11), custom_call_target="tpu_custom_call" | custom-call | tf_op jit(solution)/shard_map/grad_k/pallas_call | solution.py:322
  93.5 0.0 collective-permute-done.10.refs_1_
  93.5 0.3 collective-permute-done.9.refs_2_
  93.8 0.0 collective-permute-start.15
  93.8 2.1 %collective-permute-start.11 = (f32[4,128,128]{2,1,0:T(8,128)S(1)}, f32[4,128,128]{2,1,0:T(8,128)S(1)}, u32[]{:S(2)}, u32[]{:S(2)}) collective-permute-start(f32[4,128,128]{2,1,0:T(8,128)S(1)} %get-tuple-element.34), channel_id=1, source_target_pairs={{0,2},{1,3},{2,0},{3,1},{4,6},{5,7},{6,4},{7,5},{8,10},{9,11},{10,... | collective-permute-start | bytes 786440 | tf_op jit(solution)/shard_map/ppermute | solution.py:479
  96.0 0.2 collective-permute-start.14
  96.2 1.1 collective-permute-start.13
  97.3 0.8 collective-permute-start.12
  98.1 8.0 %grad_q.1.gq_ref = f32[8,80,256]{2,1,0:T(8,128)} custom-call(f32[64,1024]{1,0:T(8,128)S(1)} %logit_grad.1.lg_ref.refs_0_, f32[64,1024]{1,0:T(8,128)S(1)} %collective-permute-done.10.refs_1_, f32[64,1024]{1,0:T(8,128)S(1)} %collective-permute-done.9.refs_2_, f32[64,1024]{1,0:T(8,128)S(1)} %collective-permute-done.15.refs_3_, bf16[1024,128]{1,0:T(8,128)(2,1)S(1)} %copy-done.5, ...), custom_call_target="tpu_custom_call" | custom-call | tf_op jit(solution)/shard_map/grad_q/pallas_call | solution.py:322
  106.1 0.0 collective-permute-done.14.gw3
  106.1 0.7 grad_w_rows.1
  106.8 0.0 collective-permute-done.11
  106.8 4.6 %all-to-all-start.1 = ((f32[8,80,256]{2,1,0:T(8,128)}), f32[8,80,256]{2,1,0:T(8,128)S(1)}, u32[]{:S(2)}, u32[]{:S(2)}) async-start(f32[8,80,256]{2,1,0:T(8,128)} %grad_w_rows.1), calls=%async_computation.1 | async-start | bytes 1310720 | tf_op jit(solution)/shard_map/all_to_all | solution.py:534
  111.4 0.1 collective-permute-start.16
  111.5 5.1 %collective-permute-done.16 = f32[2,128,128]{2,1,0:T(8,128)S(1)} collective-permute-done((f32[2,128,128]{2,1,0:T(8,128)S(1)}, f32[2,128,128]{2,1,0:T(8,128)S(1)}, u32[]{:S(2)}, u32[]{:S(2)}) %collective-permute-start.16) | collective-permute-done | bytes 131104 | tf_op jit(solution)/shard_map/ppermute | solution.py:479
  116.6 1.8 %collective-permute-start.17 = (f32[128,128]{1,0:T(8,128)S(1)}, f32[128,128]{1,0:T(8,128)S(1)}, u32[]{:S(2)}, u32[]{:S(2)}) collective-permute-start(f32[128,128]{1,0:T(8,128)S(1)} %get-tuple-element.43), channel_id=1, source_target_pairs={{0,1},{1,0},{2,3},{3,2},{4,5},{5,4},{6,7},{7,6},{8,9},{9,8},{10,11... | collective-permute-start | bytes 196616 | tf_op jit(solution)/shard_map/ppermute | solution.py:479
  118.4 4.1 %collective-permute-done.17.got_ref = f32[128,128]{1,0:T(8,128)S(1)} collective-permute-done((f32[128,128]{1,0:T(8,128)S(1)}, f32[128,128]{1,0:T(8,128)S(1)}, u32[]{:S(2)}, u32[]{:S(2)}) %collective-permute-start.17) | collective-permute-done | bytes 65568 | tf_op jit(solution)/shard_map/ppermute | solution.py:479
  122.5 9.3 %all-to-all-done.1.parts_ref = f32[8,80,256]{2,1,0:T(8,128)S(1)} async-done(((f32[8,80,256]{2,1,0:T(8,128)}), f32[8,80,256]{2,1,0:T(8,128)S(1)}, u32[]{:S(2)}, u32[]{:S(2)}) %all-to-all-start.1) | async-done | bytes 655392 | tf_op jit(solution)/shard_map/all_to_all | solution.py:534
  131.8 0.8 finish.1
  (36 shorter events, 0.2 us)
Async XLA Ops:
  1.3 29.8 %copy-start.5 = (bf16[1024,128]{1,0:T(8,128)(2,1)S(1)}, bf16[1024,128]{1,0:T(8,128)(2,1)}, u32[]{:S(2)}) copy-start(bf16[1024,128]{1,0:T(8,128)(2,1)} %refs_4_.1) | copy-start | bytes 786436
  1.3 43.5 %copy-start = (bf16[1024,2048]{1,0:T(8,128)(2,1)S(1)}, bf16[1024,2048]{1,0:T(8,128)(2,1)}, u32[]{:S(2)}) copy-start(bf16[1024,2048]{1,0:T(8,128)(2,1)} %kn_ref.3) | copy-start | bytes 12582916
  1.3 43.5 %copy-start.2 = (bf16[512,2048]{1,0:T(8,128)(2,1)S(1)}, bf16[512,2048]{1,0:T(8,128)(2,1)}, u32[]{:S(2)}) copy-start(bf16[512,2048]{1,0:T(8,128)(2,1)} %qn_ref.3) | copy-start | bytes 6291460
  1.3 43.5 %copy-start.6 = (bf16[1024,64]{0,1:T(8,128)(2,1)S(1)}, bf16[1024,64]{0,1:T(8,128)(2,1)}, u32[]{:S(2)}) copy-start(bf16[1024,64]{0,1:T(8,128)(2,1)} %param.12) | copy-start | bytes 393220
  1.3 43.5 %copy-start.12 = (s32[512]{0:T(512)S(1)}, s32[512]{0:T(512)}, u32[]{:S(2)}) copy-start(s32[512]{0:T(512)} %param.16) | copy-start | bytes 6148
  18.7 26.2 %copy-start.4 = (bf16[512,1024]{1,0:T(8,128)(2,1)S(1)}, bf16[512,1024]{1,0:T(8,128)(2,1)}, u32[]{:S(2)}) copy-start(bf16[512,1024]{1,0:T(8,128)(2,1)} %qr_ref.3) | copy-start | bytes 3145732
  18.7 1.5 %collective-permute-start = (f32[16,640]{1,0:T(8,128)}, f32[16,640]{1,0:T(8,128)S(1)}, u32[]{:S(2)}, u32[]{:S(2)}) collective-permute-start(f32[16,640]{1,0:T(8,128)} %get-tuple-element.23), channel_id=1, source_target_pairs={{0,8},{8,0},{16,24},{24,16},{32,40},{40,32},{48,56},{56,48},{64,72... | collective-permute-start | bytes 122888 | tf_op jit(solution)/shard_map/ppermute | solution.py:483
  21.0 4.1 %collective-permute-start.1 = (f32[16,640]{1,0:T(8,128)S(1)}, f32[16,640]{1,0:T(8,128)S(1)}, u32[]{:S(2)}, u32[]{:S(2)}) collective-permute-start(f32[16,640]{1,0:T(8,128)S(1)} %multiply_add_fusion.4), channel_id=1, source_target_pairs={{0,128},{8,136},{16,144},{24,152},{32,160},{40,168},{48,176},{56,1... | collective-permute-start | bytes 122888 | tf_op jit(solution)/shard_map/ppermute | solution.py:483
  25.1 7.7 %collective-permute-start.3 = (f32[16,640]{1,0:T(8,128)S(1)}, f32[16,640]{1,0:T(8,128)S(1)}, u32[]{:S(2)}, u32[]{:S(2)}) collective-permute-start(f32[16,640]{1,0:T(8,128)S(1)} %multiply_add_fusion.3), channel_id=1, source_target_pairs={{0,112},{8,120},{16,0},{24,8},{32,16},{40,24},{48,32},{56,40},{64,... | collective-permute-start | bytes 122888 | tf_op jit(solution)/shard_map/ppermute | solution.py:488
  31.1 5.2 %collective-permute-start.2 = (f32[16,640]{1,0:T(8,128)S(1)}, f32[16,640]{1,0:T(8,128)S(1)}, u32[]{:S(2)}, u32[]{:S(2)}) collective-permute-start(f32[16,640]{1,0:T(8,128)S(1)} %multiply_add_fusion.3), channel_id=1, source_target_pairs={{0,16},{8,24},{16,32},{24,40},{32,48},{40,56},{48,64},{56,72},{64,... | collective-permute-start | bytes 122888 | tf_op jit(solution)/shard_map/ppermute | solution.py:488
  31.1 22.2 %copy-start.13 = (f32[1024,128]{1,0:T(8,128)}, f32[1024,128]{1,0:T(8,128)S(1)}, u32[]{:S(2)}) copy-start(f32[1024,128]{1,0:T(8,128)S(1)} %convert_element_type.3) | copy-start | bytes 1572868
  31.1 23.5 %collective-permute-start.6 = (f32[1024,128]{1,0:T(8,128)S(1)}, f32[1024,128]{1,0:T(8,128)}, u32[]{:S(2)}, u32[]{:S(2)}) collective-permute-start(f32[1024,128]{1,0:T(8,128)S(1)} %convert_element_type.3), channel_id=1, source_target_pairs={{0,128},{8,136},{16,144},{24,152},{32,160},{40,168},{48,176},{56,1... | collective-permute-start | bytes 1572872 | tf_op jit(solution)/shard_map/ppermute | solution.py:483
  36.3 6.2 %collective-permute-start.5 = (f32[16,640]{1,0:T(8,128)S(1)}, f32[16,640]{1,0:T(8,128)S(1)}, u32[]{:S(2)}, u32[]{:S(2)}) collective-permute-start(f32[16,640]{1,0:T(8,128)S(1)} %get-tuple-element.46), channel_id=1, source_target_pairs={{0,80},{8,88},{16,96},{24,104},{32,112},{40,120},{48,0},{56,8},{64... | collective-permute-start | bytes 122888 | tf_op jit(solution)/shard_map/ppermute | solution.py:488
  37.1 7.7 %collective-permute-start.4 = (f32[16,640]{1,0:T(8,128)S(1)}, f32[16,640]{1,0:T(8,128)S(1)}, u32[]{:S(2)}, u32[]{:S(2)}) collective-permute-start(f32[16,640]{1,0:T(8,128)S(1)} %get-tuple-element.45), channel_id=1, source_target_pairs={{0,48},{8,56},{16,64},{24,72},{32,80},{40,88},{48,96},{56,104},{64... | collective-permute-start | bytes 122888 | tf_op jit(solution)/shard_map/ppermute | solution.py:488
  53.3 1.4 %copy-start.3 = (f32[512,1024]{1,0:T(8,128)}, f32[512,1024]{1,0:T(8,128)S(1)}, u32[]{:S(2)}) copy-start(f32[512,1024]{1,0:T(8,128)S(1)} %main_probs.1) | copy-start | bytes 6291460
  54.6 30.2 %all-to-all-start = ((f32[8,64,1024]{2,1,0:T(8,128)}), f32[8,64,1024]{2,1,0:T(8,128)S(1)}, u32[]{:S(2)}, u32[]{:S(2)}) async-start(f32[8,64,1024]{2,1,0:T(8,128)} %bitcast.7), calls=%async_computation | async-start | bytes 4194304 | tf_op jit(solution)/shard_map/all_to_all | solution.py:517
  62.1 24.0 %copy-start.1 = (bf16[64,8192]{1,0:T(8,128)(2,1)S(1)}, bf16[64,8192]{1,0:T(8,128)(2,1)}, u32[]{:S(2)}) copy-start(bf16[64,8192]{1,0:T(8,128)(2,1)} %refs_8_.1) | copy-start | bytes 3145732
  62.1 24.0 %copy-start.11 = (f32[64,64]{1,0:T(8,128)S(1)}, f32[64,64]{1,0:T(8,128)}, u32[]{:S(2)}) copy-start(f32[64,64]{1,0:T(8,128)} %refs_9_.1) | copy-start | bytes 49156
  62.1 2.1 %collective-permute-start.7 = (f32[1024,128]{1,0:T(8,128)}, f32[1024,128]{1,0:T(8,128)S(1)}, u32[]{:S(2)}, u32[]{:S(2)}) collective-permute-start(f32[1024,128]{1,0:T(8,128)} %copy-done.13), channel_id=1, source_target_pairs={{0,8},{8,0},{16,24},{24,16},{32,40},{40,32},{48,56},{56,48},{64,72... | collective-permute-start | bytes 1572872 | tf_op jit(solution)/shard_map/ppermute | solution.py:483
  62.1 2.9 %collective-permute-start.8 = (f32[1024,128]{1,0:T(8,128)}, f32[1024,128]{1,0:T(8,128)S(1)}, u32[]{:S(2)}, u32[]{:S(2)}) collective-permute-start(f32[1024,128]{1,0:T(8,128)} %collective-permute-done.6.refs_6_), channel_id=1, source_target_pairs={{0,8},{8,0},{16,24},{24,16},{32,40},{40,32},{48,56},{56,48},{64,72... | collective-permute-start | bytes 1572872 | tf_op jit(solution)/shard_map/ppermute | solution.py:483
  64.2 0.8 copy-start.7
  65.0 0.8 copy-start.9
  84.9 13.3 %copy-start.8 = (f32[1024,128]{1,0:T(8,128)S(1)}, f32[1024,128]{1,0:T(8,128)}, u32[]{:S(2)}) copy-start(f32[1024,128]{1,0:T(8,128)} %copy-done.7) | copy-start | bytes 1572868
  84.9 13.3 %copy-start.10 = (f32[1024,128]{1,0:T(8,128)S(1)}, f32[1024,128]{1,0:T(8,128)}, u32[]{:S(2)}) copy-start(f32[1024,128]{1,0:T(8,128)} %copy-done.9) | copy-start | bytes 1572868
  85.0 8.5 %collective-permute-start.10 = (f32[64,1024]{1,0:T(8,128)S(1)}, f32[64,1024]{1,0:T(8,128)S(1)}, u32[]{:S(2)}, u32[]{:S(2)}) collective-permute-start(f32[64,1024]{1,0:T(8,128)S(1)} %logit_grad.1.lg_ref.refs_0_), channel_id=1, source_target_pairs={{0,8},{8,0},{16,24},{24,16},{32,40},{40,32},{48,56},{56,48},{64,72... | collective-permute-start | bytes 786440 | tf_op jit(solution)/shard_map/ppermute | solution.py:483
  85.1 8.7 %collective-permute-start.9 = (f32[64,1024]{1,0:T(8,128)S(1)}, f32[64,1024]{1,0:T(8,128)S(1)}, u32[]{:S(2)}, u32[]{:S(2)}) collective-permute-start(f32[64,1024]{1,0:T(8,128)S(1)} %logit_grad.1.lg_ref.refs_0_), channel_id=1, source_target_pairs={{0,128},{8,136},{16,144},{24,152},{32,160},{40,168},{48,176},{56,1... | collective-permute-start | bytes 786440 | tf_op jit(solution)/shard_map/ppermute | solution.py:483
  93.8 4.3 %collective-permute-start.15 = (f32[64,1024]{1,0:T(8,128)S(1)}, f32[64,1024]{1,0:T(8,128)S(1)}, u32[]{:S(2)}, u32[]{:S(2)}) collective-permute-start(f32[64,1024]{1,0:T(8,128)S(1)} %collective-permute-done.9.refs_2_), channel_id=1, source_target_pairs={{0,8},{8,0},{16,24},{24,16},{32,40},{40,32},{48,56},{56,48},{64,72... | collective-permute-start | bytes 786440 | tf_op jit(solution)/shard_map/ppermute | solution.py:483
  93.8 12.9 %collective-permute-start.11 = (f32[4,128,128]{2,1,0:T(8,128)S(1)}, f32[4,128,128]{2,1,0:T(8,128)S(1)}, u32[]{:S(2)}, u32[]{:S(2)}) collective-permute-start(f32[4,128,128]{2,1,0:T(8,128)S(1)} %get-tuple-element.34), channel_id=1, source_target_pairs={{0,2},{1,3},{2,0},{3,1},{4,6},{5,7},{6,4},{7,5},{8,10},{9,11},{10,... | collective-permute-start | bytes 786440 | tf_op jit(solution)/shard_map/ppermute | solution.py:479
  96.0 10.1 %collective-permute-start.14 = (f32[16,256]{1,0:T(8,128)S(1)}, f32[16,256]{1,0:T(8,128)S(1)}, u32[]{:S(2)}, u32[]{:S(2)}) collective-permute-start(f32[16,256]{1,0:T(8,128)S(1)} %get-tuple-element.35.gw0), channel_id=1, source_target_pairs={{0,8},{8,0},{16,24},{24,16},{32,40},{40,32},{48,56},{56,48},{64,72... | collective-permute-start | bytes 49160 | tf_op jit(solution)/shard_map/ppermute | solution.py:483
  96.2 9.9 %collective-permute-start.13 = (f32[16,256]{1,0:T(8,128)S(1)}, f32[16,256]{1,0:T(8,128)S(1)}, u32[]{:S(2)}, u32[]{:S(2)}) collective-permute-start(f32[16,256]{1,0:T(8,128)S(1)} %get-tuple-element.35.gw0), channel_id=1, source_target_pairs={{0,136},{8,128},{16,152},{24,144},{32,168},{40,160},{48,184},{56,1... | collective-permute-start | bytes 49160 | tf_op jit(solution)/shard_map/ppermute | solution.py:483
  97.3 8.8 %collective-permute-start.12 = (f32[16,256]{1,0:T(8,128)S(1)}, f32[16,256]{1,0:T(8,128)S(1)}, u32[]{:S(2)}, u32[]{:S(2)}) collective-permute-start(f32[16,256]{1,0:T(8,128)S(1)} %get-tuple-element.35.gw0), channel_id=1, source_target_pairs={{0,128},{8,136},{16,144},{24,152},{32,160},{40,168},{48,176},{56,1... | collective-permute-start | bytes 49160 | tf_op jit(solution)/shard_map/ppermute | solution.py:483
  106.8 25.0 %all-to-all-start.1 = ((f32[8,80,256]{2,1,0:T(8,128)}), f32[8,80,256]{2,1,0:T(8,128)S(1)}, u32[]{:S(2)}, u32[]{:S(2)}) async-start(f32[8,80,256]{2,1,0:T(8,128)} %grad_w_rows.1), calls=%async_computation.1 | async-start | bytes 1310720 | tf_op jit(solution)/shard_map/all_to_all | solution.py:534
  111.4 5.2 %collective-permute-start.16 = (f32[2,128,128]{2,1,0:T(8,128)S(1)}, f32[2,128,128]{2,1,0:T(8,128)S(1)}, u32[]{:S(2)}, u32[]{:S(2)}) collective-permute-start(f32[2,128,128]{2,1,0:T(8,128)S(1)} %slice_add_fusion), channel_id=1, source_target_pairs={{0,6},{1,7},{2,4},{3,5},{4,2},{5,3},{6,0},{7,1},{8,14},{9,15},{10,... | collective-permute-start | bytes 393224 | tf_op jit(solution)/shard_map/ppermute | solution.py:479
  116.6 5.9 %collective-permute-start.17 = (f32[128,128]{1,0:T(8,128)S(1)}, f32[128,128]{1,0:T(8,128)S(1)}, u32[]{:S(2)}, u32[]{:S(2)}) collective-permute-start(f32[128,128]{1,0:T(8,128)S(1)} %get-tuple-element.43), channel_id=1, source_target_pairs={{0,1},{1,0},{2,3},{3,2},{4,5},{5,4},{6,7},{7,6},{8,9},{9,8},{10,11... | collective-permute-start | bytes 196616 | tf_op jit(solution)/shard_map/ppermute | solution.py:479

commit v9 on v7

--- a/solution.py
+++ b/solution.py
@@ -67,7 +67,7 @@
     return q, jnp.concatenate([kn_ref[:, part], krp[p]], axis=1)
 
 
-def online_lse(s_ref, bias, cols, chunk=64):
+def online_lse(s_ref, bias, cols, chunk=128):
     keys = bias.shape[0]
     top = jnp.full((8, 256), 2.0 * NEG, F32)
     total = jnp.zeros((8, 256), F32)
@@ -113,9 +113,10 @@
             out_ref[pl.ds(2 * step + p, 1), cols] = online_lse(s_ref.at[p], bias, cols)
 
     scores(0)
+    scores(1)
+    statistics(0)
     si_ref[...] = dot(ik_ref[...], stacked(iq_ref[...]), NT)
-    statistics(0)
-    scores(1)
+    statistics(1)
     weights = [wp[pl.ds(step * GROUP // 2 + i, 1), :] for i in range(GROUP // 2)]
     for r in range(keys // 64):
         at = slice(r * 64, (r + 1) * 64)
@@ -123,7 +124,6 @@
         for i, weight in enumerate(weights):
             total = total + jnp.maximum(si_ref[at, i * 128 : (i + 1) * 128], 0.0) * weight
         acc[at, :] = total
-    statistics(1)
 
     @pl.when(step == pl.num_programs(0) - 1)
     def _():

time: 132 us -> 133 us (level)
  no operation moved by 1% of the time
where the time goes in v9:
time: 133 us; the launch traced here: 132 us
  waiting for transfers between devices  50.4 us (38%)
  Pallas kernels  42 us (32%)
  starting transfers between devices  33 us (25%)
  local copies, waits for them, and re-layouts  2.98 us (2%)
  other arithmetic  2 us (2%)
  between operations  1.5 us (1%)
    pallas_call x4, Pallas kernels, call(): pl.pallas_call(kernel, grid=grid, in_specs=in_specs, out_specs=out_specs,...  40.4 us
    all_to_all x1, waiting for transfers between devices, per_device(): lax.all_to_all(probs.reshape(N_HEAD, -1, probs.shape[1]), 'head', 0, 0)  19.1 us
    ppermute x4, starting transfers between devices, z_shift(): return lax.ppermute(value, 'ctx', list(enumerate(to)))  9.83 us
    all_to_all x1, waiting for transfers between devices, per_device(): parts = lax.all_to_all(parts, 'ctx', 0, 0, axis_index_groups=groups)  9.34 us
    ppermute x3, waiting for transfers between devices, head_xor(): return lax.ppermute(value, 'head', [(i, i ^ bits) for i in range(N_HEAD)])  9.13 us
    all_to_all x1, starting transfers between devices, per_device(): lax.all_to_all(probs.reshape(N_HEAD, -1, probs.shape[1]), 'head', 0, 0)  7.45 us
    ppermute x11, starting transfers between devices, ctx_xor(): return lax.ppermute(value, 'ctx', [(i, i ^ bits) for i in range(N_CTX)])  7.08 us
    ppermute x4, waiting for transfers between devices, z_shift(): return lax.ppermute(value, 'ctx', list(enumerate(to)))  7.07 us
  transfers between devices with their start and end apart: 20, of which 11 were waited for; matrix products, arithmetic and copies ran while one was open for 1% of the time, Pallas kernels for 19%

profile of v9, /device:TPU:2, one launch (start us, length us, event | category | flops | bytes accessed | tf_op | source)
XLA Modules:
  0.0 131.9 jit_solution(328803058818360035)
XLA Ops:
  1.3 16.7 %front.1 = (f32[16,640]{1,0:T(8,128)}, f32[64,1024]{1,0:T(8,128)}) custom-call(s32[1]{0:T(128)S(6)} %copy.14.base_ref, s32[1,512]{1,0:T(1,128)} %bitcast.10, bf16[64,1024]{1,0:T(8,128)(2,1)} %bitcast.8, bf16[1024,128]{1,0:T(8,128)(2,1)} %refs_4_.1, f32[64,64]{1,0:T(8,128)} %refs_9_.1, bf16[64,8192]{1,0:T(8,128)(2,1)} %refs_8_.1, bf16[512,2048]{1,0:T(8,128)(2,1)} %qn_ref.3, ...), custom_call_target="tpu_custom_call" | custom-call | tf_op jit(solution)/shard_map/front/pallas_call | solution.py:316
  18.0 0.1 collective-permute-start
  18.1 1.4 %collective-permute-done = f32[16,640]{1,0:T(8,128)S(1)} collective-permute-done((f32[16,640]{1,0:T(8,128)}, f32[16,640]{1,0:T(8,128)S(1)}, u32[]{:S(2)}, u32[]{:S(2)}) %collective-permute-start) | collective-permute-done | bytes 40992 | tf_op jit(solution)/shard_map/ppermute | solution.py:477
  19.5 0.8 multiply_add_fusion.4
  20.3 1.7 %collective-permute-start.1 = (f32[16,640]{1,0:T(8,128)S(1)}, f32[16,640]{1,0:T(8,128)S(1)}, u32[]{:S(2)}, u32[]{:S(2)}) collective-permute-start(f32[16,640]{1,0:T(8,128)S(1)} %multiply_add_fusion.4), channel_id=1, source_target_pairs={{0,128},{8,136},{16,144},{24,152},{32,160},{40,168},{48,176},{56,1... | collective-permute-start | bytes 122888 | tf_op jit(solution)/shard_map/ppermute | solution.py:477
  22.0 2.4 %collective-permute-done.1 = f32[16,640]{1,0:T(8,128)S(1)} collective-permute-done((f32[16,640]{1,0:T(8,128)S(1)}, f32[16,640]{1,0:T(8,128)S(1)}, u32[]{:S(2)}, u32[]{:S(2)}) %collective-permute-start.1) | collective-permute-done | bytes 40992 | tf_op jit(solution)/shard_map/ppermute | solution.py:477
  24.4 5.9 %collective-permute-start.3 = (f32[16,640]{1,0:T(8,128)S(1)}, f32[16,640]{1,0:T(8,128)S(1)}, u32[]{:S(2)}, u32[]{:S(2)}) collective-permute-start(f32[16,640]{1,0:T(8,128)S(1)} %multiply_add_fusion.3), channel_id=1, source_target_pairs={{0,112},{8,120},{16,0},{24,8},{32,16},{40,24},{48,32},{56,40},{64,... | collective-permute-start | bytes 122888 | tf_op jit(solution)/shard_map/ppermute | solution.py:482
  30.4 0.0 collective-permute-start.2
  30.4 1.7 %collective-permute-start.6 = (f32[1024,128]{1,0:T(8,128)S(1)}, f32[1024,128]{1,0:T(8,128)}, u32[]{:S(2)}, u32[]{:S(2)}) collective-permute-start(f32[1024,128]{1,0:T(8,128)S(1)} %convert_element_type.3), channel_id=1, source_target_pairs={{0,128},{8,136},{16,144},{24,152},{32,160},{40,168},{48,176},{56,1... | collective-permute-start | bytes 1572872 | tf_op jit(solution)/shard_map/ppermute | solution.py:477
  32.1 0.0 collective-permute-done.3
  32.1 3.5 %collective-permute-done.2 = f32[16,640]{1,0:T(8,128)S(1)} collective-permute-done((f32[16,640]{1,0:T(8,128)S(1)}, f32[16,640]{1,0:T(8,128)S(1)}, u32[]{:S(2)}, u32[]{:S(2)}) %collective-permute-start.2) | collective-permute-done | bytes 40992 | tf_op jit(solution)/shard_map/ppermute | solution.py:482
  35.6 0.1 multiply_add_fusion.2
  35.6 0.8 collective-permute-start.5
  36.4 3.1 %collective-permute-start.4 = (f32[16,640]{1,0:T(8,128)S(1)}, f32[16,640]{1,0:T(8,128)S(1)}, u32[]{:S(2)}, u32[]{:S(2)}) collective-permute-start(f32[16,640]{1,0:T(8,128)S(1)} %get-tuple-element.45), channel_id=1, source_target_pairs={{0,48},{8,56},{16,64},{24,72},{32,80},{40,88},{48,96},{56,104},{64... | collective-permute-start | bytes 122888 | tf_op jit(solution)/shard_map/ppermute | solution.py:482
  39.5 1.0 broadcast_maximum_fusion.logits_ref
  40.5 1.3 collective-permute-done.5
  41.8 2.3 %collective-permute-done.4 = f32[16,640]{1,0:T(8,128)S(1)} collective-permute-done((f32[16,640]{1,0:T(8,128)S(1)}, f32[16,640]{1,0:T(8,128)S(1)}, u32[]{:S(2)}, u32[]{:S(2)}) %collective-permute-start.4) | collective-permute-done | bytes 40992 | tf_op jit(solution)/shard_map/ppermute | solution.py:482
  44.2 8.4 %main_probs.1 = f32[512,1024]{1,0:T(8,128)S(1)} custom-call(s32[1]{0:T(128)S(6)} %copy.14.base_ref, s32[1,512]{1,0:T(1,128)S(1)} %bitcast.11, f32[16,640]{1,0:T(8,128)S(1)} %multiply_add_fusion.lse_ref, f32[64,1024]{1,0:T(8,128)S(1)} %broadcast_maximum_fusion.logits_ref, bf16[64,1024]{1,0:T(8,128)(2,1)S(1)} %bitcast.9, bf16[512,2048]{1,0:T(8,128)(2,1)S(1)} %copy-done.2, ...), custom_call_target="tpu_custom_call" | custom-call | tf_op jit(solution)/shard_map/main_probs/pallas_call | solution.py:316
  52.6 1.4 %copy-done.3 = f32[512,1024]{1,0:T(8,128)} copy-done((f32[512,1024]{1,0:T(8,128)}, f32[512,1024]{1,0:T(8,128)S(1)}, u32[]{:S(2)}) %copy-start.3) | copy-done | bytes 2097176
  54.0 0.0 collective-permute-done.6.refs_6_
  54.0 7.4 %all-to-all-start = ((f32[8,64,1024]{2,1,0:T(8,128)}), f32[8,64,1024]{2,1,0:T(8,128)S(1)}, u32[]{:S(2)}, u32[]{:S(2)}) async-start(f32[8,64,1024]{2,1,0:T(8,128)} %bitcast.7), calls=%async_computation | async-start | bytes 4194304 | tf_op jit(solution)/shard_map/all_to_all | solution.py:511
  61.4 0.5 collective-permute-start.8
  61.9 1.6 %collective-permute-done.7.refs_5_ = f32[1024,128]{1,0:T(8,128)S(1)} collective-permute-done((f32[1024,128]{1,0:T(8,128)}, f32[1024,128]{1,0:T(8,128)S(1)}, u32[]{:S(2)}, u32[]{:S(2)}) %collective-permute-start.7) | collective-permute-done | bytes 524320 | tf_op jit(solution)/shard_map/ppermute | solution.py:477
  63.5 0.8 copy-done.7
  64.3 0.0 collective-permute-done.8.refs_7_
  64.3 0.8 copy-done.9
  65.1 19.1 %all-to-all-done.target_ref = f32[8,64,1024]{2,1,0:T(8,128)S(1)} async-done(((f32[8,64,1024]{2,1,0:T(8,128)}), f32[8,64,1024]{2,1,0:T(8,128)S(1)}, u32[]{:S(2)}, u32[]{:S(2)}) %all-to-all-start) | async-done | bytes 2097184 | tf_op jit(solution)/shard_map/all_to_all | solution.py:511
  84.2 0.1 logit_grad.1.lg_ref.refs_0_
  84.3 0.1 collective-permute-start.10
  84.4 0.9 collective-permute-start.9
  85.4 7.4 %grad_k.1 = (f32[4,128,128]{2,1,0:T(8,128)S(1)}, f32[4,128,128]{2,1,0:T(8,128)S(1)}, f32[16,256]{1,0:T(8,128)S(1)}) custom-call(f32[64,1024]{1,0:T(8,128)S(1)} %logit_grad.1.lg_ref.refs_0_, bf16[64,8192]{1,0:T(8,128)(2,1)S(1)} %copy-done.1, bf16[1024,128]{1,0:T(8,128)(2,1)S(1)} %copy-done.5, f32[64,64]{1,0:T(8,128)S(1)} %copy-done.11), custom_call_target="tpu_custom_call" | custom-call | tf_op jit(solution)/shard_map/grad_k/pallas_call | solution.py:316
  92.8 0.0 collective-permute-done.10.refs_1_
  92.8 0.3 collective-permute-done.9.refs_2_
  93.2 0.0 collective-permute-start.15
  93.2 2.1 %collective-permute-start.11 = (f32[4,128,128]{2,1,0:T(8,128)S(1)}, f32[4,128,128]{2,1,0:T(8,128)S(1)}, u32[]{:S(2)}, u32[]{:S(2)}) collective-permute-start(f32[4,128,128]{2,1,0:T(8,128)S(1)} %get-tuple-element.34), channel_id=1, source_target_pairs={{0,2},{1,3},{2,0},{3,1},{4,6},{5,7},{6,4},{7,5},{8,10},{9,11},{10,... | collective-permute-start | bytes 786440 | tf_op jit(solution)/shard_map/ppermute | solution.py:473
  95.3 0.2 collective-permute-start.14
  95.5 1.1 collective-permute-start.13
  96.6 0.8 collective-permute-start.12
  97.4 0.0 collective-permute-done.15.refs_3_
  97.4 8.0 %grad_q.1.gq_ref = f32[8,80,256]{2,1,0:T(8,128)} custom-call(f32[64,1024]{1,0:T(8,128)S(1)} %logit_grad.1.lg_ref.refs_0_, f32[64,1024]{1,0:T(8,128)S(1)} %collective-permute-done.10.refs_1_, f32[64,1024]{1,0:T(8,128)S(1)} %collective-permute-done.9.refs_2_, f32[64,1024]{1,0:T(8,128)S(1)} %collective-permute-done.15.refs_3_, bf16[1024,128]{1,0:T(8,128)(2,1)S(1)} %copy-done.5, ...), custom_call_target="tpu_custom_call" | custom-call | tf_op jit(solution)/shard_map/grad_q/pallas_call | solution.py:316
  105.4 0.7 grad_w_rows.1
  106.1 4.6 %all-to-all-start.1 = ((f32[8,80,256]{2,1,0:T(8,128)}), f32[8,80,256]{2,1,0:T(8,128)S(1)}, u32[]{:S(2)}, u32[]{:S(2)}) async-start(f32[8,80,256]{2,1,0:T(8,128)} %grad_w_rows.1), calls=%async_computation.1 | async-start | bytes 1310720 | tf_op jit(solution)/shard_map/all_to_all | solution.py:528
  110.7 0.1 collective-permute-start.16
  110.8 5.1 %collective-permute-done.16 = f32[2,128,128]{2,1,0:T(8,128)S(1)} collective-permute-done((f32[2,128,128]{2,1,0:T(8,128)S(1)}, f32[2,128,128]{2,1,0:T(8,128)S(1)}, u32[]{:S(2)}, u32[]{:S(2)}) %collective-permute-start.16) | collective-permute-done | bytes 131104 | tf_op jit(solution)/shard_map/ppermute | solution.py:473
  115.9 1.8 %collective-permute-start.17 = (f32[128,128]{1,0:T(8,128)S(1)}, f32[128,128]{1,0:T(8,128)S(1)}, u32[]{:S(2)}, u32[]{:S(2)}) collective-permute-start(f32[128,128]{1,0:T(8,128)S(1)} %get-tuple-element.43), channel_id=1, source_target_pairs={{0,1},{1,0},{2,3},{3,2},{4,5},{5,4},{6,7},{7,6},{8,9},{9,8},{10,11... | collective-permute-start | bytes 196616 | tf_op jit(solution)/shard_map/ppermute | solution.py:473
  117.7 4.1 %collective-permute-done.17.got_ref = f32[128,128]{1,0:T(8,128)S(1)} collective-permute-done((f32[128,128]{1,0:T(8,128)S(1)}, f32[128,128]{1,0:T(8,128)S(1)}, u32[]{:S(2)}, u32[]{:S(2)}) %collective-permute-start.17) | collective-permute-done | bytes 65568 | tf_op jit(solution)/shard_map/ppermute | solution.py:473
  121.8 9.3 %all-to-all-done.1.parts_ref = f32[8,80,256]{2,1,0:T(8,128)S(1)} async-done(((f32[8,80,256]{2,1,0:T(8,128)}), f32[8,80,256]{2,1,0:T(8,128)S(1)}, u32[]{:S(2)}, u32[]{:S(2)}) %all-to-all-start.1) | async-done | bytes 655392 | tf_op jit(solution)/shard_map/all_to_all | solution.py:528
  131.1 0.8 finish.1
  (36 shorter events, 0.2 us)
Async XLA Ops:
  1.3 29.1 %copy-start.5 = (bf16[1024,128]{1,0:T(8,128)(2,1)S(1)}, bf16[1024,128]{1,0:T(8,128)(2,1)}, u32[]{:S(2)}) copy-start(bf16[1024,128]{1,0:T(8,128)(2,1)} %refs_4_.1) | copy-start | bytes 786436
  1.3 42.9 %copy-start = (bf16[1024,2048]{1,0:T(8,128)(2,1)S(1)}, bf16[1024,2048]{1,0:T(8,128)(2,1)}, u32[]{:S(2)}) copy-start(bf16[1024,2048]{1,0:T(8,128)(2,1)} %kn_ref.3) | copy-start | bytes 12582916
  1.3 42.9 %copy-start.2 = (bf16[512,2048]{1,0:T(8,128)(2,1)S(1)}, bf16[512,2048]{1,0:T(8,128)(2,1)}, u32[]{:S(2)}) copy-start(bf16[512,2048]{1,0:T(8,128)(2,1)} %qn_ref.3) | copy-start | bytes 6291460
  1.3 42.9 %copy-start.6 = (bf16[1024,64]{0,1:T(8,128)(2,1)S(1)}, bf16[1024,64]{0,1:T(8,128)(2,1)}, u32[]{:S(2)}) copy-start(bf16[1024,64]{0,1:T(8,128)(2,1)} %param.12) | copy-start | bytes 393220
  1.3 42.9 %copy-start.12 = (s32[512]{0:T(512)S(1)}, s32[512]{0:T(512)}, u32[]{:S(2)}) copy-start(s32[512]{0:T(512)} %param.16) | copy-start | bytes 6148
  18.0 26.2 %copy-start.4 = (bf16[512,1024]{1,0:T(8,128)(2,1)S(1)}, bf16[512,1024]{1,0:T(8,128)(2,1)}, u32[]{:S(2)}) copy-start(bf16[512,1024]{1,0:T(8,128)(2,1)} %qr_ref.3) | copy-start | bytes 3145732
  18.0 1.5 %collective-permute-start = (f32[16,640]{1,0:T(8,128)}, f32[16,640]{1,0:T(8,128)S(1)}, u32[]{:S(2)}, u32[]{:S(2)}) collective-permute-start(f32[16,640]{1,0:T(8,128)} %get-tuple-element.23), channel_id=1, source_target_pairs={{0,8},{8,0},{16,24},{24,16},{32,40},{40,32},{48,56},{56,48},{64,72... | collective-permute-start | bytes 122888 | tf_op jit(solution)/shard_map/ppermute | solution.py:477
  20.3 4.1 %collective-permute-start.1 = (f32[16,640]{1,0:T(8,128)S(1)}, f32[16,640]{1,0:T(8,128)S(1)}, u32[]{:S(2)}, u32[]{:S(2)}) collective-permute-start(f32[16,640]{1,0:T(8,128)S(1)} %multiply_add_fusion.4), channel_id=1, source_target_pairs={{0,128},{8,136},{16,144},{24,152},{32,160},{40,168},{48,176},{56,1... | collective-permute-start | bytes 122888 | tf_op jit(solution)/shard_map/ppermute | solution.py:477
  24.4 7.7 %collective-permute-start.3 = (f32[16,640]{1,0:T(8,128)S(1)}, f32[16,640]{1,0:T(8,128)S(1)}, u32[]{:S(2)}, u32[]{:S(2)}) collective-permute-start(f32[16,640]{1,0:T(8,128)S(1)} %multiply_add_fusion.3), channel_id=1, source_target_pairs={{0,112},{8,120},{16,0},{24,8},{32,16},{40,24},{48,32},{56,40},{64,... | collective-permute-start | bytes 122888 | tf_op jit(solution)/shard_map/ppermute | solution.py:482
  30.4 5.2 %collective-permute-start.2 = (f32[16,640]{1,0:T(8,128)S(1)}, f32[16,640]{1,0:T(8,128)S(1)}, u32[]{:S(2)}, u32[]{:S(2)}) collective-permute-start(f32[16,640]{1,0:T(8,128)S(1)} %multiply_add_fusion.3), channel_id=1, source_target_pairs={{0,16},{8,24},{16,32},{24,40},{32,48},{40,56},{48,64},{56,72},{64,... | collective-permute-start | bytes 122888 | tf_op jit(solution)/shard_map/ppermute | solution.py:482
  30.4 22.2 %copy-start.13 = (f32[1024,128]{1,0:T(8,128)}, f32[1024,128]{1,0:T(8,128)S(1)}, u32[]{:S(2)}) copy-start(f32[1024,128]{1,0:T(8,128)S(1)} %convert_element_type.3) | copy-start | bytes 1572868
  30.4 23.5 %collective-permute-start.6 = (f32[1024,128]{1,0:T(8,128)S(1)}, f32[1024,128]{1,0:T(8,128)}, u32[]{:S(2)}, u32[]{:S(2)}) collective-permute-start(f32[1024,128]{1,0:T(8,128)S(1)} %convert_element_type.3), channel_id=1, source_target_pairs={{0,128},{8,136},{16,144},{24,152},{32,160},{40,168},{48,176},{56,1... | collective-permute-start | bytes 1572872 | tf_op jit(solution)/shard_map/ppermute | solution.py:477
  35.6 6.2 %collective-permute-start.5 = (f32[16,640]{1,0:T(8,128)S(1)}, f32[16,640]{1,0:T(8,128)S(1)}, u32[]{:S(2)}, u32[]{:S(2)}) collective-permute-start(f32[16,640]{1,0:T(8,128)S(1)} %get-tuple-element.46), channel_id=1, source_target_pairs={{0,80},{8,88},{16,96},{24,104},{32,112},{40,120},{48,0},{56,8},{64... | collective-permute-start | bytes 122888 | tf_op jit(solution)/shard_map/ppermute | solution.py:482
  36.4 7.7 %collective-permute-start.4 = (f32[16,640]{1,0:T(8,128)S(1)}, f32[16,640]{1,0:T(8,128)S(1)}, u32[]{:S(2)}, u32[]{:S(2)}) collective-permute-start(f32[16,640]{1,0:T(8,128)S(1)} %get-tuple-element.45), channel_id=1, source_target_pairs={{0,48},{8,56},{16,64},{24,72},{32,80},{40,88},{48,96},{56,104},{64... | collective-permute-start | bytes 122888 | tf_op jit(solution)/shard_map/ppermute | solution.py:482
  52.6 1.4 %copy-start.3 = (f32[512,1024]{1,0:T(8,128)}, f32[512,1024]{1,0:T(8,128)S(1)}, u32[]{:S(2)}) copy-start(f32[512,1024]{1,0:T(8,128)S(1)} %main_probs.1) | copy-start | bytes 6291460
  54.0 30.2 %all-to-all-start = ((f32[8,64,1024]{2,1,0:T(8,128)}), f32[8,64,1024]{2,1,0:T(8,128)S(1)}, u32[]{:S(2)}, u32[]{:S(2)}) async-start(f32[8,64,1024]{2,1,0:T(8,128)} %bitcast.7), calls=%async_computation | async-start | bytes 4194304 | tf_op jit(solution)/shard_map/all_to_all | solution.py:511
  61.4 24.0 %copy-start.1 = (bf16[64,8192]{1,0:T(8,128)(2,1)S(1)}, bf16[64,8192]{1,0:T(8,128)(2,1)}, u32[]{:S(2)}) copy-start(bf16[64,8192]{1,0:T(8,128)(2,1)} %refs_8_.1) | copy-start | bytes 3145732
  61.4 24.0 %copy-start.11 = (f32[64,64]{1,0:T(8,128)S(1)}, f32[64,64]{1,0:T(8,128)}, u32[]{:S(2)}) copy-start(f32[64,64]{1,0:T(8,128)} %refs_9_.1) | copy-start | bytes 49156
  61.4 2.1 %collective-permute-start.7 = (f32[1024,128]{1,0:T(8,128)}, f32[1024,128]{1,0:T(8,128)S(1)}, u32[]{:S(2)}, u32[]{:S(2)}) collective-permute-start(f32[1024,128]{1,0:T(8,128)} %copy-done.13), channel_id=1, source_target_pairs={{0,8},{8,0},{16,24},{24,16},{32,40},{40,32},{48,56},{56,48},{64,72... | collective-permute-start | bytes 1572872 | tf_op jit(solution)/shard_map/ppermute | solution.py:477
  61.4 2.9 %collective-permute-start.8 = (f32[1024,128]{1,0:T(8,128)}, f32[1024,128]{1,0:T(8,128)S(1)}, u32[]{:S(2)}, u32[]{:S(2)}) collective-permute-start(f32[1024,128]{1,0:T(8,128)} %collective-permute-done.6.refs_6_), channel_id=1, source_target_pairs={{0,8},{8,0},{16,24},{24,16},{32,40},{40,32},{48,56},{56,48},{64,72... | collective-permute-start | bytes 1572872 | tf_op jit(solution)/shard_map/ppermute | solution.py:477
  63.5 0.8 copy-start.7
  64.3 0.8 copy-start.9
  84.2 13.3 %copy-start.8 = (f32[1024,128]{1,0:T(8,128)S(1)}, f32[1024,128]{1,0:T(8,128)}, u32[]{:S(2)}) copy-start(f32[1024,128]{1,0:T(8,128)} %copy-done.7) | copy-start | bytes 1572868
  84.2 13.3 %copy-start.10 = (f32[1024,128]{1,0:T(8,128)S(1)}, f32[1024,128]{1,0:T(8,128)}, u32[]{:S(2)}) copy-start(f32[1024,128]{1,0:T(8,128)} %copy-done.9) | copy-start | bytes 1572868
  84.3 8.5 %collective-permute-start.10 = (f32[64,1024]{1,0:T(8,128)S(1)}, f32[64,1024]{1,0:T(8,128)S(1)}, u32[]{:S(2)}, u32[]{:S(2)}) collective-permute-start(f32[64,1024]{1,0:T(8,128)S(1)} %logit_grad.1.lg_ref.refs_0_), channel_id=1, source_target_pairs={{0,8},{8,0},{16,24},{24,16},{32,40},{40,32},{48,56},{56,48},{64,72... | collective-permute-start | bytes 786440 | tf_op jit(solution)/shard_map/ppermute | solution.py:477
  84.4 8.7 %collective-permute-start.9 = (f32[64,1024]{1,0:T(8,128)S(1)}, f32[64,1024]{1,0:T(8,128)S(1)}, u32[]{:S(2)}, u32[]{:S(2)}) collective-permute-start(f32[64,1024]{1,0:T(8,128)S(1)} %logit_grad.1.lg_ref.refs_0_), channel_id=1, source_target_pairs={{0,128},{8,136},{16,144},{24,152},{32,160},{40,168},{48,176},{56,1... | collective-permute-start | bytes 786440 | tf_op jit(solution)/shard_map/ppermute | solution.py:477
  93.2 4.3 %collective-permute-start.15 = (f32[64,1024]{1,0:T(8,128)S(1)}, f32[64,1024]{1,0:T(8,128)S(1)}, u32[]{:S(2)}, u32[]{:S(2)}) collective-permute-start(f32[64,1024]{1,0:T(8,128)S(1)} %collective-permute-done.9.refs_2_), channel_id=1, source_target_pairs={{0,8},{8,0},{16,24},{24,16},{32,40},{40,32},{48,56},{56,48},{64,72... | collective-permute-start | bytes 786440 | tf_op jit(solution)/shard_map/ppermute | solution.py:477
  93.2 12.9 %collective-permute-start.11 = (f32[4,128,128]{2,1,0:T(8,128)S(1)}, f32[4,128,128]{2,1,0:T(8,128)S(1)}, u32[]{:S(2)}, u32[]{:S(2)}) collective-permute-start(f32[4,128,128]{2,1,0:T(8,128)S(1)} %get-tuple-element.34), channel_id=1, source_target_pairs={{0,2},{1,3},{2,0},{3,1},{4,6},{5,7},{6,4},{7,5},{8,10},{9,11},{10,... | collective-permute-start | bytes 786440 | tf_op jit(solution)/shard_map/ppermute | solution.py:473
  95.3 10.1 %collective-permute-start.14 = (f32[16,256]{1,0:T(8,128)S(1)}, f32[16,256]{1,0:T(8,128)S(1)}, u32[]{:S(2)}, u32[]{:S(2)}) collective-permute-start(f32[16,256]{1,0:T(8,128)S(1)} %get-tuple-element.35.gw0), channel_id=1, source_target_pairs={{0,8},{8,0},{16,24},{24,16},{32,40},{40,32},{48,56},{56,48},{64,72... | collective-permute-start | bytes 49160 | tf_op jit(solution)/shard_map/ppermute | solution.py:477
  95.5 9.9 %collective-permute-start.13 = (f32[16,256]{1,0:T(8,128)S(1)}, f32[16,256]{1,0:T(8,128)S(1)}, u32[]{:S(2)}, u32[]{:S(2)}) collective-permute-start(f32[16,256]{1,0:T(8,128)S(1)} %get-tuple-element.35.gw0), channel_id=1, source_target_pairs={{0,136},{8,128},{16,152},{24,144},{32,168},{40,160},{48,184},{56,1... | collective-permute-start | bytes 49160 | tf_op jit(solution)/shard_map/ppermute | solution.py:477
  96.6 8.8 %collective-permute-start.12 = (f32[16,256]{1,0:T(8,128)S(1)}, f32[16,256]{1,0:T(8,128)S(1)}, u32[]{:S(2)}, u32[]{:S(2)}) collective-permute-start(f32[16,256]{1,0:T(8,128)S(1)} %get-tuple-element.35.gw0), channel_id=1, source_target_pairs={{0,128},{8,136},{16,144},{24,152},{32,160},{40,168},{48,176},{56,1... | collective-permute-start | bytes 49160 | tf_op jit(solution)/shard_map/ppermute | solution.py:477
  106.1 25.0 %all-to-all-start.1 = ((f32[8,80,256]{2,1,0:T(8,128)}), f32[8,80,256]{2,1,0:T(8,128)S(1)}, u32[]{:S(2)}, u32[]{:S(2)}) async-start(f32[8,80,256]{2,1,0:T(8,128)} %grad_w_rows.1), calls=%async_computation.1 | async-start | bytes 1310720 | tf_op jit(solution)/shard_map/all_to_all | solution.py:528
  110.7 5.2 %collective-permute-start.16 = (f32[2,128,128]{2,1,0:T(8,128)S(1)}, f32[2,128,128]{2,1,0:T(8,128)S(1)}, u32[]{:S(2)}, u32[]{:S(2)}) collective-permute-start(f32[2,128,128]{2,1,0:T(8,128)S(1)} %slice_add_fusion), channel_id=1, source_target_pairs={{0,6},{1,7},{2,4},{3,5},{4,2},{5,3},{6,0},{7,1},{8,14},{9,15},{10,... | collective-permute-start | bytes 393224 | tf_op jit(solution)/shard_map/ppermute | solution.py:473
  115.9 5.9 %collective-permute-start.17 = (f32[128,128]{1,0:T(8,128)S(1)}, f32[128,128]{1,0:T(8,128)S(1)}, u32[]{:S(2)}, u32[]{:S(2)}) collective-permute-start(f32[128,128]{1,0:T(8,128)S(1)} %get-tuple-element.43), channel_id=1, source_target_pairs={{0,1},{1,0},{2,3},{3,2},{4,5},{5,4},{6,7},{7,6},{8,9},{9,8},{10,11... | collective-permute-start | bytes 196616 | tf_op jit(solution)/shard_map/ppermute | solution.py:473
